TPU v7x, 512 devices: a whole 4x8x8 slice. The times are simulated.
512 devices in a mesh: pipe: 16 (over y, core), expert: 32 (over x, z).
Axes of the slice: x: 4, y: 8, z: 8, core: 2. Of those that a mesh axis runs over, the one named last changes fastest.
Arguments:
- x_forward: bfloat16 [16, 2048, 3584], P('pipe', 'expert'), may hold values from -6 to 6
- x_backward: bfloat16 [16, 2048, 3584], P('pipe', 'expert'), may hold values from -6 to 6
- norm_gain: float32 [16, 3584], P('pipe'), may hold values from 0.1 to 1.9
- w_gate: bfloat16 [16, 3584, 4096], P('pipe', None, 'expert'), may hold values from -0.09375 to 0.09375
- w_up: bfloat16 [16, 3584, 4096], P('pipe', None, 'expert'), may hold values from -0.09375 to 0.09375
- w_down: bfloat16 [16, 4096, 3584], P('pipe', 'expert'), may hold values from -0.1875 to 0.1875
- routes_forward: int32 [16, 2048, 1], P('pipe', 'expert'), may hold values from 0 to 3; in each aligned block of 64 rows (0 to 63, 64 to 127, ..., all dimensions but the last counted through in order) at most 16 rows name the same one
- routes_backward: int32 [16, 2048, 1], P('pipe', 'expert'), may hold values from 0 to 3; in each aligned block of 64 rows (0 to 63, 64 to 127, ..., all dimensions but the last counted through in order) at most 16 rows name the same one
- gates_forward: float32 [16, 2048, 1], P('pipe', 'expert'), may hold values from 0.2 to 2
- gates_backward: float32 [16, 2048, 1], P('pipe', 'expert'), may hold values from 0.2 to 2
Outputs:
- out_forward: bfloat16 [16, 2048, 3584], P('pipe', 'expert')
- out_backward: bfloat16 [16, 2048, 3584], P('pipe', 'expert')
Inputs may be any that keep to these rules, and one draw needn't show every extreme that they name: `routes_forward`: each row names one expert; in each aligned block of 64 rows (the rows of one device) every expert is named by exactly 16 rows. `routes_backward`: as for routes_forward.
All inputs are finite; a program needn't handle non-finite values.
Results may differ from a plain program's by a relative error of at most 0.0085.
Values may be sent and summed in bfloat16 or wider, within the bound.
No kernel may reach another device: no remote copies, remote signals or barrier semaphores. Data moves between devices by JAX's collectives and lax.ppermute only.
A program may use at most 64 MiB of HBM per device.

v0:
```python
import jax
import jax.numpy as jnp
from jax import lax
from jax.sharding import PartitionSpec as P

EXPERTS = 4


def shifted(array, axis, by):
    peers = lax.axis_size(axis)
    return lax.ppermute(array, axis, [(i, (i + by) % peers) for i in range(peers)])


def rms_norm(values, norm_scale):
    widened = values.astype(jnp.float32)
    mean_square = jnp.mean(widened * widened, axis=-1, keepdims=True)
    return (widened * lax.rsqrt(mean_square + 1e-06) * norm_scale).astype(jnp.bfloat16)


def prepare(states, routes, norm_scale, experts_here, slot_count):
    normed = rms_norm(states, norm_scale)
    tok_rows, top_count = routes.shape
    row_width = states.shape[1]
    onehot = (routes[..., None] == jnp.arange(experts_here, dtype=jnp.int32)).astype(jnp.int32)
    onehot = onehot.reshape(tok_rows * top_count, experts_here)
    earlier = jnp.cumsum(onehot, axis=0) - onehot
    slot_ids = jnp.sum(earlier * onehot, axis=1).reshape(tok_rows, top_count)
    targets = routes * slot_count + slot_ids
    placing = jnp.any(
        targets[None, :, :]
        == jnp.arange(experts_here * slot_count, dtype=jnp.int32)[:, None, None],
        axis=2,
    )
    buffer = jnp.dot(
        placing.astype(jnp.bfloat16), normed, preferred_element_type=jnp.float32
    ).astype(jnp.bfloat16)
    return (buffer.reshape(experts_here, slot_count, row_width), targets)


def expert_partial(received, gate_cols, up_cols, down_rows):
    sources, item_count, row_width = received.shape
    flat_rows = received.reshape(sources * item_count, row_width)
    gate_part = jnp.dot(flat_rows, gate_cols, preferred_element_type=jnp.float32)
    up_part = jnp.dot(flat_rows, up_cols, preferred_element_type=jnp.float32)
    hidden = (jax.nn.silu(gate_part) * up_part).astype(jnp.bfloat16)
    partial_value = jnp.dot(hidden, down_rows, preferred_element_type=jnp.float32).astype(
        jnp.bfloat16
    )
    return partial_value.reshape(sources, item_count, row_width)


def combine(states, targets, gate_vals, returned, experts_here):
    group_count, slot_count, row_width = returned.shape
    shards = group_count // experts_here
    summed = jnp.sum(
        returned.astype(jnp.float32).reshape(experts_here, shards, slot_count, row_width), axis=1
    )
    picked = summed.reshape(experts_here * slot_count, row_width)[targets]
    mixed_rows = jnp.sum(gate_vals[..., None] * picked, axis=1)
    return (states.astype(jnp.float32) + mixed_rows).astype(jnp.bfloat16)


def body(
    x_forward,
    x_backward,
    norm_gain,
    w_gate,
    w_up,
    w_down,
    routes_forward,
    routes_backward,
    gates_forward,
    gates_backward,
):
    norm_scale = norm_gain[0]
    gate_cols = w_gate[0]
    up_cols = w_up[0]
    down_rows = w_down[0]
    shards = lax.axis_size("expert") // EXPERTS
    states_fwd = x_forward[0]
    states_bwd = x_backward[0]
    slot_count = states_fwd.shape[0] * routes_forward.shape[2] // EXPERTS
    buffer_fwd, targets_fwd = prepare(
        states_fwd, routes_forward[0], norm_scale, EXPERTS, slot_count
    )
    buffer_bwd, targets_bwd = prepare(
        states_bwd, routes_backward[0], norm_scale, EXPERTS, slot_count
    )
    outgoing_fwd = jnp.repeat(buffer_fwd, shards, axis=0)
    outgoing_bwd = jnp.repeat(buffer_bwd, shards, axis=0)

    def apply_one(received):
        partial_value = expert_partial(received, gate_cols, up_cols, down_rows)
        return lax.all_to_all(partial_value, "expert", split_axis=0, concat_axis=0, tiled=True)

    def dispatch_one(outgoing):
        return apply_one(
            lax.all_to_all(outgoing, "expert", split_axis=0, concat_axis=0, tiled=True)
        )

    returned_fwd = dispatch_one(outgoing_fwd)
    returned_bwd = dispatch_one(outgoing_bwd)
    done_fwd = combine(states_fwd, targets_fwd, gates_forward[0], returned_fwd, EXPERTS)
    done_bwd = combine(states_bwd, targets_bwd, gates_backward[0], returned_bwd, EXPERTS)
    moved_fwd = shifted(done_fwd[None], "pipe", 1)
    moved_bwd = shifted(done_bwd[None], "pipe", -1)
    return (moved_fwd, moved_bwd)


def solution(mesh):
    placed = (
        P("pipe", "expert", None),
        P("pipe", "expert", None),
        P("pipe", None),
        P("pipe", None, "expert"),
        P("pipe", None, "expert"),
        P("pipe", "expert", None),
        P("pipe", "expert", None),
        P("pipe", "expert", None),
        P("pipe", "expert", None),
        P("pipe", "expert", None),
    )
    return jax.shard_map(
        body,
        mesh=mesh,
        in_specs=placed,
        out_specs=(P("pipe", "expert", None), P("pipe", "expert", None)),
        check_vma=False,
    )
```

profile of v0, /device:TPU:32, one launch (start us, length us, event | category | flops | bytes accessed | tf_op | source)
XLA Modules:
  0.0 398.9 jit_solution(7459877319373628396)
XLA Ops:
  1.5 0.8 select_reduce_fusion
  3.1 1.2 fusion.6
  5.0 1.4 convolution_convert_fusion.2
  6.4 2.3 broadcast_in_dim.5
  8.7 13.4 %all-to-all-start.2 = ((bf16[32,16,3584]{2,1,0:T(8,128)(2,1)}), bf16[32,16,3584]{2,1,0:T(8,128)(2,1)}, u32[]{:S(2)}, u32[]{:S(2)}) async-start(bf16[32,16,3584]{2,1,0:T(8,128)(2,1)} %bitcast.93), calls=%async_computation.2 | async-start | bytes 7340032 | tf_op jit(solution)/shard_map/all_to_all | solution.py:98
  23.0 84.9 %all-to-all-done.2 = bf16[32,16,3584]{2,1,0:T(8,128)(2,1)} async-done(((bf16[32,16,3584]{2,1,0:T(8,128)(2,1)}), bf16[32,16,3584]{2,1,0:T(8,128)(2,1)}, u32[]{:S(2)}, u32[]{:S(2)}) %all-to-all-start.2) | async-done | bytes 3670048 | tf_op jit(solution)/shard_map/all_to_all | solution.py:98
  107.9 2.3 broadcast_in_dim.4
  110.3 5.0 %all-to-all-start = ((bf16[32,16,3584]{2,1,0:T(8,128)(2,1)}), bf16[32,16,3584]{2,1,0:T(8,128)(2,1)}, u32[]{:S(2)}, u32[]{:S(2)}) async-start(bf16[32,16,3584]{2,1,0:T(8,128)(2,1)} %bitcast.94), calls=%async_computation | async-start | bytes 7340032 | tf_op jit(solution)/shard_map/all_to_all | solution.py:98
  115.3 3.5 fusion.16
  118.8 7.9 %convolution_convert_fusion = bf16[512,3584]{1,0:T(8,128)(2,1)} fusion(bf16[512,3584]{1,0:T(8,128)(2,1)} %bitcast.27, bf16[1,128,3584]{2,1,0:T(8,128)(2,1)S(1)} %copy-done, bf16[1,3584,128]{2,1,0:T(8,128)(2,1)S(1)} %copy-done.3, f32[512,128]{1,0:T(8,128)S(1)} %fusion.16), kind=kOutput, calls=%fused_computation.4 | convolution fusion | flops 941752320 | bytes 9437184 | tf_op jit(solution)/shard_map/dot_general | solution.py:46
  126.7 74.3 %all-to-all-done = bf16[32,16,3584]{2,1,0:T(8,128)(2,1)} async-done(((bf16[32,16,3584]{2,1,0:T(8,128)(2,1)}), bf16[32,16,3584]{2,1,0:T(8,128)(2,1)}, u32[]{:S(2)}, u32[]{:S(2)}) %all-to-all-start) | async-done | bytes 3670048 | tf_op jit(solution)/shard_map/all_to_all | solution.py:98
  201.0 5.1 %all-to-all-start.3 = ((bf16[32,16,3584]{2,1,0:T(8,128)(2,1)}), bf16[32,16,3584]{2,1,0:T(8,128)(2,1)}, u32[]{:S(2)}, u32[]{:S(2)}) async-start(bf16[32,16,3584]{2,1,0:T(8,128)(2,1)} %bitcast.92), calls=%async_computation.3 | async-start | bytes 7340032 | tf_op jit(solution)/shard_map/all_to_all | solution.py:94
  206.2 3.4 fusion.18
  209.6 7.8 %convolution_convert_fusion.1 = bf16[512,3584]{1,0:T(8,128)(2,1)} fusion(bf16[512,3584]{1,0:T(8,128)(2,1)} %bitcast.8, bf16[1,128,3584]{2,1,0:T(8,128)(2,1)S(1)} %copy-done, bf16[1,3584,128]{2,1,0:T(8,128)(2,1)S(1)} %copy-done.3, f32[512,128]{1,0:T(8,128)S(1)} %fusion.18), kind=kOutput, calls=%fused_computation.5 | convolution fusion | flops 941752320 | bytes 9437184 | tf_op jit(solution)/shard_map/dot_general | solution.py:46
  217.3 74.4 %all-to-all-done.3 = bf16[32,16,3584]{2,1,0:T(8,128)(2,1)} async-done(((bf16[32,16,3584]{2,1,0:T(8,128)(2,1)}), bf16[32,16,3584]{2,1,0:T(8,128)(2,1)}, u32[]{:S(2)}, u32[]{:S(2)}) %all-to-all-start.3) | async-done | bytes 3670048 | tf_op jit(solution)/shard_map/all_to_all | solution.py:94
  291.7 5.3 %all-to-all-start.1 = ((bf16[32,16,3584]{2,1,0:T(8,128)(2,1)}), bf16[32,16,3584]{2,1,0:T(8,128)(2,1)}, u32[]{:S(2)}, u32[]{:S(2)}) async-start(bf16[32,16,3584]{2,1,0:T(8,128)(2,1)} %bitcast.91), calls=%async_computation.1 | async-start | bytes 7340032 | tf_op jit(solution)/shard_map/all_to_all | solution.py:94
  297.1 2.7 convert_reduce_fusion
  299.8 1.8 gather_fusion.1
  301.6 1.4 fusion.9
  303.0 79.4 %all-to-all-done.1 = bf16[32,16,3584]{2,1,0:T(8,128)(2,1)} async-done(((bf16[32,16,3584]{2,1,0:T(8,128)(2,1)}), bf16[32,16,3584]{2,1,0:T(8,128)(2,1)}, u32[]{:S(2)}, u32[]{:S(2)}) %all-to-all-start.1) | async-done | bytes 3670048 | tf_op jit(solution)/shard_map/all_to_all | solution.py:94
  382.4 2.6 convert_reduce_fusion.1
  385.1 1.8 gather_fusion
  386.9 1.4 fusion.5
  388.3 9.1 %collective-permute-done = bf16[1,64,3584]{2,1,0:T(8,128)(2,1)S(1)} collective-permute-done((bf16[1,64,3584]{2,1,0:T(8,128)(2,1)S(1)}, bf16[1,64,3584]{2,1,0:T(8,128)(2,1)S(1)}, u32[]{:S(2)}, u32[]{:S(2)}) %collective-permute-start) | collective-permute-done | bytes 458784 | tf_op jit(solution)/shard_map/ppermute | solution.py:11
  (37 shorter events, 4.9 us)
Async XLA Ops:
  0.6 118.2 %copy-start = (bf16[1,128,3584]{2,1,0:T(8,128)(2,1)S(1)}, bf16[1,128,3584]{2,1,0:T(8,128)(2,1)}, u32[]{:S(2)}) copy-start(bf16[1,128,3584]{2,1,0:T(8,128)(2,1)} %param.15) | copy-start | bytes 2752516
  8.7 13.4 %copy-start.5 = (s32[1,64,1]{1,2,0:T(1,128)S(1)}, s32[1,64,1]{1,2,0:T(1,128)}, u32[]{:S(2)}) copy-start(s32[1,64,1]{1,2,0:T(1,128)} %param.16) | copy-start | bytes 772
  8.7 13.8 %copy-start.2 = (bf16[1,64,3584]{2,1,0:T(8,128)(2,1)S(1)}, bf16[1,64,3584]{2,1,0:T(8,128)(2,1)}, u32[]{:S(2)}) copy-start(bf16[1,64,3584]{2,1,0:T(8,128)(2,1)} %param.10) | copy-start | bytes 1376260
  8.7 99.3 %all-to-all-start.2 = ((bf16[32,16,3584]{2,1,0:T(8,128)(2,1)}), bf16[32,16,3584]{2,1,0:T(8,128)(2,1)}, u32[]{:S(2)}, u32[]{:S(2)}) async-start(bf16[32,16,3584]{2,1,0:T(8,128)(2,1)} %bitcast.93), calls=%async_computation.2 | async-start | bytes 7340032 | tf_op jit(solution)/shard_map/all_to_all | solution.py:98
  110.3 90.8 %all-to-all-start = ((bf16[32,16,3584]{2,1,0:T(8,128)(2,1)}), bf16[32,16,3584]{2,1,0:T(8,128)(2,1)}, u32[]{:S(2)}, u32[]{:S(2)}) async-start(bf16[32,16,3584]{2,1,0:T(8,128)(2,1)} %bitcast.94), calls=%async_computation | async-start | bytes 7340032 | tf_op jit(solution)/shard_map/all_to_all | solution.py:98
  115.3 3.5 copy-start.3
  201.0 90.7 %all-to-all-start.3 = ((bf16[32,16,3584]{2,1,0:T(8,128)(2,1)}), bf16[32,16,3584]{2,1,0:T(8,128)(2,1)}, u32[]{:S(2)}, u32[]{:S(2)}) async-start(bf16[32,16,3584]{2,1,0:T(8,128)(2,1)} %bitcast.92), calls=%async_computation.3 | async-start | bytes 7340032 | tf_op jit(solution)/shard_map/all_to_all | solution.py:94
  291.7 5.3 %copy-start.4 = (s32[1,64,1]{1,2,0:T(1,128)S(1)}, s32[1,64,1]{1,2,0:T(1,128)}, u32[]{:S(2)}) copy-start(s32[1,64,1]{1,2,0:T(1,128)} %param.17) | copy-start | bytes 772
  291.7 90.7 %all-to-all-start.1 = ((bf16[32,16,3584]{2,1,0:T(8,128)(2,1)}), bf16[32,16,3584]{2,1,0:T(8,128)(2,1)}, u32[]{:S(2)}, u32[]{:S(2)}) async-start(bf16[32,16,3584]{2,1,0:T(8,128)(2,1)} %bitcast.91), calls=%async_computation.1 | async-start | bytes 7340032 | tf_op jit(solution)/shard_map/all_to_all | solution.py:94
  299.8 1.8 copy-start.1
  299.8 1.8 copy-start.6
  302.9 85.3 %collective-permute-start.1 = (bf16[1,64,3584]{2,1,0:T(8,128)(2,1)S(1)}, bf16[1,64,3584]{2,1,0:T(8,128)(2,1)S(1)}, u32[]{:S(2)}, u32[]{:S(2)}) collective-permute-start(bf16[1,64,3584]{2,1,0:T(8,128)(2,1)S(1)} %fusion.9), channel_id=1, source_target_pairs={{0,480},{32,0},{64,32},{96,64},{128,96},{160,128},{192,160},{224,1... | collective-permute-start | bytes 1376264 | tf_op jit(solution)/shard_map/ppermute | solution.py:11
  385.1 1.8 copy-start.7
  388.2 9.1 %collective-permute-start = (bf16[1,64,3584]{2,1,0:T(8,128)(2,1)S(1)}, bf16[1,64,3584]{2,1,0:T(8,128)(2,1)S(1)}, u32[]{:S(2)}, u32[]{:S(2)}) collective-permute-start(bf16[1,64,3584]{2,1,0:T(8,128)(2,1)S(1)} %fusion.5), channel_id=1, source_target_pairs={{0,32},{32,64},{64,96},{96,128},{128,160},{160,192},{192,224},{224... | collective-permute-start | bytes 1376264 | tf_op jit(solution)/shard_map/ppermute | solution.py:11
where the time goes:
time: 400 us; the launch traced here: 399 us
  waiting for transfers between devices  322 us (80%)
  starting transfers between devices  28.9 us (7%)
  matrix products  24.2 us (6%)
  other arithmetic  13 us (3%)
  local copies, waits for them, and re-layouts  9.74 us (2%)
    all_to_all x2, waiting for transfers between devices, dispatch_one(): lax.all_to_all(outgoing, 'expert', split_axis=0, concat_axis=0, tiled=True)  159 us
    all_to_all x2, waiting for transfers between devices, apply_one(): lax.all_to_all(partial_value, 'expert', split_axis=0, concat_axis=0, tile...  154 us
    all_to_all x2, starting transfers between devices, dispatch_one(): lax.all_to_all(outgoing, 'expert', split_axis=0, concat_axis=0, tiled=True)  18.4 us
    dot_general x2, matrix products, expert_partial(): jnp.dot(hidden, down_rows, preferred_element_type=jnp.float32)  15.6 us
    all_to_all x2, starting transfers between devices, apply_one(): lax.all_to_all(partial_value, 'expert', split_axis=0, concat_axis=0, tile...  10.5 us
    ppermute x2, waiting for transfers between devices, shifted(): lax.ppermute(array, axis, [(i, (i + by) % peers) for i in range(peers)])  9.09 us
  transfers between devices with their start and end apart: 6, of which 5 were waited for; matrix products, arithmetic and copies ran while one was open for 9% of the time, Pallas kernels for 0%

commit v1 on v0

v1 whole, which is shorter than its diff:
```python
import jax
import jax.numpy as jnp
from jax import lax
from jax.experimental import pallas as pl
from jax.experimental.pallas import tpu as pltpu
from jax.sharding import Mesh, PartitionSpec as P

EXPERTS = 4
EXTRA = 16
VMEM_BYTES = 48 * 1024 * 1024


def vmem_spec():
    return pl.BlockSpec(memory_space=pltpu.VMEM)


def smem_spec():
    return pl.BlockSpec(memory_space=pltpu.SMEM)


def call(kernel, out_shape, arguments, scalars=0, flops=0, moved=0, after=()):
    specs = [smem_spec()] * scalars + [vmem_spec()] * (len(arguments) - scalars)
    specs += [pl.BlockSpec(memory_space=pl.ANY)] * len(after)
    used = len(arguments)

    def ordered(*refs):
        kernel(*refs[:used], *refs[used + len(after) :])

    return pl.pallas_call(
        ordered,
        out_shape=out_shape,
        in_specs=specs,
        out_specs=jax.tree.map(lambda _: vmem_spec(), out_shape),
        compiler_params=pltpu.CompilerParams(vmem_limit_bytes=VMEM_BYTES),
        cost_estimate=pl.CostEstimate(flops=flops, bytes_accessed=moved, transcendentals=0),
    )(*arguments, *after)


def shifted(array, axis, by):
    peers = lax.axis_size(axis)
    return lax.ppermute(array, axis, [(i, (i + by) % peers) for i in range(peers)])


def as_column(row):
    count = row.shape[1]
    place = lax.broadcasted_iota(jnp.int32, (count, count), 0)
    other = lax.broadcasted_iota(jnp.int32, (count, count), 1)
    return jnp.sum(jnp.where(place == other, row, jnp.zeros_like(row)), axis=1, keepdims=True)


def slots(routes, blocks, per_block):
    count = routes.shape[1]
    place = lax.broadcasted_iota(jnp.int32, (count, count), 0)
    other = lax.broadcasted_iota(jnp.int32, (count, count), 1)
    earlier = (as_column(routes) == routes) & (place < other)
    rank = jnp.sum(earlier.astype(jnp.int32), axis=0, keepdims=True)
    return place == blocks * per_block + rank


def prepare_kernel(states, routes, gates, gain, buffer, travelling):
    count = states.shape[0]
    values = states[...].astype(jnp.float32)
    mean_square = jnp.mean(values * values, axis=-1, keepdims=True)
    normed = (values * lax.rsqrt(mean_square + 1e-06) * gain[...]).astype(jnp.bfloat16)
    placing = slots(routes[...], routes[...], count // EXPERTS).astype(jnp.bfloat16)
    buffer[...] = jnp.dot(placing, normed, preferred_element_type=jnp.float32).astype(jnp.bfloat16)
    travelling[:count, :] = states[...]
    extra = travelling.shape[0] - count
    travelling[count:, :] = jnp.zeros((extra, states.shape[1]), jnp.bfloat16)
    gate = gates[...]
    high = gate.astype(jnp.bfloat16).astype(jnp.float32)
    middle = (gate - high).astype(jnp.bfloat16).astype(jnp.float32)
    low = gate - high - middle
    row = lax.broadcasted_iota(jnp.int32, (extra, count), 0)
    table = jnp.zeros((extra, count), jnp.float32)
    for place, term in enumerate((routes[...].astype(jnp.float32), high, middle, low)):
        table = jnp.where(row == place, term, table)
    travelling[count:, :count] = table.astype(jnp.bfloat16)


def prepare(states, routes, gates, gain):
    rows, width = states.shape
    return call(
        prepare_kernel,
        (
            jax.ShapeDtypeStruct((rows, width), jnp.bfloat16),
            jax.ShapeDtypeStruct((rows + EXTRA, width), jnp.bfloat16),
        ),
        (states, routes, gates, gain),
        flops=2 * rows * states.size,
        moved=6 * states.size,
    )


def expert_kernel(blocks, gate_ref, up_ref, down_ref, *outs):
    width = gate_ref.shape[1]
    depth = gate_ref.shape[0]
    step = depth // 7
    rows = [ref[...] for ref in blocks]
    rows = rows[0] if len(rows) == 1 else jnp.concatenate(rows, axis=0)
    total = jnp.zeros((rows.shape[0], 2 * width), jnp.float32)
    for k in range(0, depth, step):
        both = jnp.concatenate([gate_ref[k : k + step, :], up_ref[k : k + step, :]], axis=1)
        total += jnp.dot(rows[:, k : k + step], both, preferred_element_type=jnp.float32)
    gate_part, up_part = total[:, :width], total[:, width:]
    hidden = (gate_part * jax.nn.sigmoid(gate_part) * up_part).astype(jnp.bfloat16)
    for k in range(0, depth, step):
        part = jnp.dot(hidden, down_ref[:, k : k + step], preferred_element_type=jnp.float32)
        part = part.astype(jnp.bfloat16)
        first = 0
        for out in outs:
            count = out.shape[0]
            out[:, k : k + step] = part[first : first + count]
            first += count


def experts(blocks, gate_cols, up_cols, down_rows, after=()):
    number = len(blocks)

    def kernel(*refs):
        expert_kernel(refs[:number], *refs[number:])

    row_count = sum(block.shape[0] for block in blocks)
    return call(
        kernel,
        tuple(jax.ShapeDtypeStruct(block.shape, jnp.bfloat16) for block in blocks),
        (*blocks, gate_cols, up_cols, down_rows),
        flops=6 * row_count * gate_cols.size,
        moved=6 * gate_cols.size + 4 * sum(block.size for block in blocks),
        after=after,
    )


def add(parts, sums, after):
    number = len(parts)

    def kernel(*refs):
        for part, received, out in zip(refs[:number], refs[number:], refs[2 * number :]):
            total = part[...].astype(jnp.float32) + received[...].astype(jnp.float32)
            out[...] = total.astype(jnp.bfloat16)

    return call(
        kernel,
        tuple(jax.ShapeDtypeStruct(part.shape, jnp.bfloat16) for part in parts),
        (*parts, *sums),
        flops=sum(part.size for part in parts),
        moved=6 * sum(part.size for part in parts),
        after=after,
    )


def split_kernel(x_ref, own, from_left, from_right, *outs):
    count = outs[0].shape[0]
    for d, out in enumerate(outs):
        start = pl.multiple_of(lax.rem(x_ref[0] + d, EXPERTS) * count, count)
        rows = pl.ds(start, count)
        total = own[rows, :].astype(jnp.float32) + from_left[rows, :].astype(jnp.float32)
        out[...] = (total + from_right[rows, :].astype(jnp.float32)).astype(jnp.bfloat16)


def split(x_index, own, from_left, from_right):
    rows, width = own.shape
    return call(
        split_kernel,
        tuple(jax.ShapeDtypeStruct((rows // EXPERTS, width), jnp.bfloat16) for _ in range(EXPERTS)),
        (x_index, own, from_left, from_right),
        scalars=1,
        flops=2 * own.size,
        moved=8 * own.size,
    )


def combine_kernel(x_ref, travelled, *refs):
    blocks, out = refs[:-1], refs[-1]
    count = out.shape[0]
    table = travelled[count:, :count].astype(jnp.float32)
    routes = table[0:1].astype(jnp.int32)
    gates = table[1:2] + table[2:3] + table[3:4]
    block_of = lax.rem(x_ref[0] + EXPERTS - routes, EXPERTS)
    placing = slots(block_of, block_of, count // EXPERTS).astype(jnp.bfloat16)
    rows = jnp.concatenate([block[...] for block in blocks], axis=0)
    picked = lax.dot_general(
        placing, rows, (((0,), (0,)), ((), ())), preferred_element_type=jnp.float32
    )
    mixed = travelled[:count, :].astype(jnp.float32) + as_column(gates) * picked
    out[...] = mixed.astype(jnp.bfloat16)


def combine(x_index, travelled, blocks):
    rows = travelled.shape[0] - EXTRA
    return call(
        combine_kernel,
        jax.ShapeDtypeStruct((rows, travelled.shape[1]), jnp.bfloat16),
        (x_index, travelled, *blocks),
        scalars=1,
        flops=2 * rows * travelled.size,
        moved=6 * travelled.size,
    )


def body(
    x_forward,
    x_backward,
    norm_gain,
    w_gate,
    w_up,
    w_down,
    routes_forward,
    routes_backward,
    gates_forward,
    gates_backward,
):
    weights = (w_gate[0], w_up[0], w_down[0])
    ring = lax.axis_size("z")
    far = ring // 2
    x_index = lax.axis_index("x").astype(jnp.int32).reshape(1)
    states = (x_forward[0], x_backward[0])
    routes = (routes_forward.reshape(1, -1), routes_backward.reshape(1, -1))
    gates = (gates_forward.reshape(1, -1), gates_backward.reshape(1, -1))
    travel = (1, -1)

    here, moved = [], []
    for m in range(2):
        buffer, travelling = prepare(states[m], routes[m], gates[m], norm_gain)
        here.append(lax.all_to_all(buffer, "x", split_axis=0, concat_axis=0, tiled=True))
        moved.append(shifted(travelling, "pipe", travel[m]))

    parts = [{}, {}]
    for m, part in enumerate(experts(here, *weights)):
        parts[m][0] = part
    moving = [{way: here[m] for way in (1, -1)} for m in range(2)]
    for step in range(1, far + 1):
        for m in range(2):
            arrived = []
            for way in (travel[m], -travel[m]):
                if step < far or way == travel[m]:
                    moving[m][way] = shifted(moving[m][way], "z", way)
                    arrived.append(way)
            results = experts(
                [moving[m][way] for way in arrived],
                *weights,
                after=(moved[m],) if step == 2 else (),
            )
            for way, part in zip(arrived, results):
                parts[m][-way * step] = part

    sums, last = [{}, {}], ()
    for stage in range(far):
        for m in range(2):
            left = {-travel[m]: far - stage, travel[m]: far - 1 - stage}
            ways = [way for way in left if left[way] > 0]
            totals = [parts[m][way * left[way]] for way in ways]
            if stage > 0:
                totals = add(totals, [sums[m][way] for way in ways], last)
                last = (totals[0],)
            for way, total in zip(ways, totals):
                sums[m][way] = shifted(total, "z", way)

    sections, columns = lax.axis_size("pipe"), lax.axis_size("x")
    done = []
    for m in range(2):
        blocks = split(x_index, parts[m][0], sums[m][1], sums[m][-1])
        returned = []
        for d, block in enumerate(blocks):
            pairs = [
                (s * columns + x, (s + travel[m]) % sections * columns + (x + d) % columns)
                for s in range(sections)
                for x in range(columns)
            ]
            returned.append(lax.ppermute(block, ("pipe", "x"), pairs))
        done.append(combine(x_index, moved[m], returned))
    return (done[0][None], done[1][None])


def solution(mesh):
    sections, members = mesh.devices.shape
    inner = Mesh(
        mesh.devices.reshape(sections, EXPERTS, members // EXPERTS), ("pipe", "x", "z")
    )
    tokens = P("pipe", ("x", "z"), None)
    placed = (
        tokens,
        tokens,
        P("pipe", None),
        P("pipe", None, ("x", "z")),
        P("pipe", None, ("x", "z")),
        tokens,
        tokens,
        tokens,
        tokens,
        tokens,
    )
    return jax.shard_map(
        body, mesh=inner, in_specs=placed, out_specs=(tokens, tokens), check_vma=False
    )
```

time: 400 us -> 232 us (0.58)
  the two profiles are of different devices: /device:TPU:32 before, /device:TPU:7 now
where the time goes in v1:
time: 232 us; the launch traced here: 230 us
  starting transfers between devices  141 us (61%)
  waiting for transfers between devices  56.6 us (24%)
  Pallas kernels  23 us (10%)
  local copies, waits for them, and re-layouts  8.98 us (4%)
    ppermute x30, starting transfers between devices, shifted(): lax.ppermute(array, axis, [(i, (i + by) % peers) for i in range(peers)])  105 us
    ppermute x30, waiting for transfers between devices, shifted(): lax.ppermute(array, axis, [(i, (i + by) % peers) for i in range(peers)])  51.2 us
    ppermute x8, starting transfers between devices, body(): returned.append(lax.ppermute(block, ('pipe', 'x'), pairs))  26.1 us
    pallas_call x21, Pallas kernels, call(): pl.pallas_call(ordered, out_shape=out_shape, in_specs=specs, out_specs=ja...  23 us
    all_to_all x2, starting transfers between devices, body(): lax.all_to_all(buffer, 'x', split_axis=0, concat_axis=0, tiled=True)  9.8 us
    unnamed x36, local copies, waits for them, and re-layouts  8.98 us
    ppermute x8, waiting for transfers between devices, body(): returned.append(lax.ppermute(block, ('pipe', 'x'), pairs))  5.41 us
  transfers between devices with their start and end apart: 40, of which 11 were waited for; matrix products, arithmetic and copies ran while one was open for 0% of the time, Pallas kernels for 9%

profile of v1, /device:TPU:7, one launch (start us, length us, event | category | flops | bytes accessed | tf_op | source)
XLA Modules:
  0.0 230.5 jit_solution(8636265404660334134)
XLA Ops:
  5.1 4.3 %all-to-all-start = ((bf16[4,16,3584]{2,1,0:T(8,128)(2,1)}), bf16[4,16,3584]{2,1,0:T(8,128)(2,1)S(1)}, u32[]{:S(2)}, u32[]{:S(2)}) async-start(bf16[4,16,3584]{2,1,0:T(8,128)(2,1)} %bitcast.4), calls=%async_computation | async-start | bytes 917504 | tf_op jit(solution)/shard_map/all_to_all | solution.py:225
  14.7 5.5 %all-to-all-start.1 = ((bf16[4,16,3584]{2,1,0:T(8,128)(2,1)}), bf16[4,16,3584]{2,1,0:T(8,128)(2,1)}, u32[]{:S(2)}, u32[]{:S(2)}) async-start(bf16[4,16,3584]{2,1,0:T(8,128)(2,1)} %bitcast.46), calls=%async_computation.1 | async-start | bytes 917504 | tf_op jit(solution)/shard_map/all_to_all | solution.py:225
  20.1 5.0 %collective-permute-start.1 = (bf16[64,3584]{1,0:T(8,128)(2,1)S(1)}, bf16[64,3584]{1,0:T(8,128)(2,1)}, u32[]{:S(2)}, u32[]{:S(2)}) collective-permute-start(bf16[64,3584]{1,0:T(8,128)(2,1)S(1)} %bitcast.43), channel_id=1, source_target_pairs={{0,1},{1,2},{2,3},{3,4},{4,5},{5,6},{6,7},{7,0},{8,9},{9,10},{10,1... | collective-permute-start | bytes 1376264 | tf_op jit(solution)/shard_map/ppermute | solution.py:41
  25.1 11.7 %collective-permute-start.12 = (bf16[64,3584]{1,0:T(8,128)(2,1)}, bf16[64,3584]{1,0:T(8,128)(2,1)S(1)}, u32[]{:S(2)}, u32[]{:S(2)}) collective-permute-start(bf16[64,3584]{1,0:T(8,128)(2,1)} %bitcast.10.refs_1_), channel_id=1, source_target_pairs={{0,7},{1,0},{2,1},{3,2},{4,3},{5,4},{6,5},{7,6},{8,15},{9,8},{10,9... | collective-permute-start | bytes 1376264 | tf_op jit(solution)/shard_map/ppermute | solution.py:41
  44.1 4.8 %collective-permute-start.13 = (bf16[64,3584]{1,0:T(8,128)(2,1)S(1)}, bf16[64,3584]{1,0:T(8,128)(2,1)S(1)}, u32[]{:S(2)}, u32[]{:S(2)}) collective-permute-start(bf16[64,3584]{1,0:T(8,128)(2,1)S(1)} %collective-permute-done.12.refs_0_), channel_id=1, source_target_pairs={{0,7},{1,0},{2,1},{3,2},{4,3},{5,4},{6,5},{7,6},{8,15},{9,8},{10,9... | collective-permute-start | bytes 1376264 | tf_op jit(solution)/shard_map/ppermute | solution.py:41
  48.9 4.5 %collective-permute-done.3.refs_1_ = bf16[64,3584]{1,0:T(8,128)(2,1)S(1)} collective-permute-done((bf16[64,3584]{1,0:T(8,128)(2,1)S(1)}, bf16[64,3584]{1,0:T(8,128)(2,1)S(1)}, u32[]{:S(2)}, u32[]{:S(2)}) %collective-permute-start.3) | collective-permute-done | bytes 458784 | tf_op jit(solution)/shard_map/ppermute | solution.py:41
  53.4 5.3 %collective-permute-start.4 = (bf16[64,3584]{1,0:T(8,128)(2,1)S(1)}, bf16[64,3584]{1,0:T(8,128)(2,1)S(1)}, u32[]{:S(2)}, u32[]{:S(2)}) collective-permute-start(bf16[64,3584]{1,0:T(8,128)(2,1)S(1)} %collective-permute-done.3.refs_1_), channel_id=1, source_target_pairs={{0,7},{1,0},{2,1},{3,2},{4,3},{5,4},{6,5},{7,6},{8,15},{9,8},{10,9... | collective-permute-start | bytes 1376264 | tf_op jit(solution)/shard_map/ppermute | solution.py:41
  63.3 5.3 %collective-permute-start.14 = (bf16[64,3584]{1,0:T(8,128)(2,1)S(1)}, bf16[64,3584]{1,0:T(8,128)(2,1)S(1)}, u32[]{:S(2)}, u32[]{:S(2)}) collective-permute-start(bf16[64,3584]{1,0:T(8,128)(2,1)S(1)} %collective-permute-done.13.refs_0_), channel_id=1, source_target_pairs={{0,7},{1,0},{2,1},{3,2},{4,3},{5,4},{6,5},{7,6},{8,15},{9,8},{10,9... | collective-permute-start | bytes 1376264 | tf_op jit(solution)/shard_map/ppermute | solution.py:41
  68.6 4.5 %collective-permute-done.4.refs_1_ = bf16[64,3584]{1,0:T(8,128)(2,1)S(1)} collective-permute-done((bf16[64,3584]{1,0:T(8,128)(2,1)S(1)}, bf16[64,3584]{1,0:T(8,128)(2,1)S(1)}, u32[]{:S(2)}, u32[]{:S(2)}) %collective-permute-start.4) | collective-permute-done | bytes 458784 | tf_op jit(solution)/shard_map/ppermute | solution.py:41
  73.1 5.3 %collective-permute-start.6 = (bf16[64,3584]{1,0:T(8,128)(2,1)S(1)}, bf16[64,3584]{1,0:T(8,128)(2,1)S(1)}, u32[]{:S(2)}, u32[]{:S(2)}) collective-permute-start(bf16[64,3584]{1,0:T(8,128)(2,1)S(1)} %collective-permute-done.4.refs_1_), channel_id=1, source_target_pairs={{0,7},{1,0},{2,1},{3,2},{4,3},{5,4},{6,5},{7,6},{8,15},{9,8},{10,9... | collective-permute-start | bytes 1376264 | tf_op jit(solution)/shard_map/ppermute | solution.py:41
  78.4 9.3 %collective-permute-start = (bf16[80,3584]{1,0:T(8,128)(2,1)}, bf16[80,3584]{1,0:T(8,128)(2,1)S(1)}, u32[]{:S(2)}, u32[]{:S(2)}) collective-permute-start(bf16[80,3584]{1,0:T(8,128)(2,1)} %copy-done.17), channel_id=1, source_target_pairs={{0,32},{32,64},{64,96},{96,128},{128,160},{160,192},{192,224},{224... | collective-permute-start | bytes 1720328 | tf_op jit(solution)/shard_map/ppermute | solution.py:41
  91.6 4.6 %collective-permute-start.19 = (bf16[64,3584]{1,0:T(8,128)(2,1)S(1)}, bf16[64,3584]{1,0:T(8,128)(2,1)S(1)}, u32[]{:S(2)}, u32[]{:S(2)}) collective-permute-start(bf16[64,3584]{1,0:T(8,128)(2,1)S(1)} %collective-permute-done.14.refs_0_), channel_id=1, source_target_pairs={{0,7},{1,0},{2,1},{3,2},{4,3},{5,4},{6,5},{7,6},{8,15},{9,8},{10,9... | collective-permute-start | bytes 1376264 | tf_op jit(solution)/shard_map/ppermute | solution.py:41
  98.1 5.2 %collective-permute-done.17.refs_1_ = bf16[64,3584]{1,0:T(8,128)(2,1)S(1)} collective-permute-done((bf16[64,3584]{1,0:T(8,128)(2,1)S(1)}, bf16[64,3584]{1,0:T(8,128)(2,1)S(1)}, u32[]{:S(2)}, u32[]{:S(2)}) %collective-permute-start.17) | collective-permute-done | bytes 458784 | tf_op jit(solution)/shard_map/ppermute | solution.py:41
  106.4 6.7 %collective-permute-done.7.refs_0_ = bf16[64,3584]{1,0:T(8,128)(2,1)S(1)} collective-permute-done((bf16[64,3584]{1,0:T(8,128)(2,1)S(1)}, bf16[64,3584]{1,0:T(8,128)(2,1)S(1)}, u32[]{:S(2)}, u32[]{:S(2)}) %collective-permute-start.7) | collective-permute-done | bytes 458784 | tf_op jit(solution)/shard_map/ppermute | solution.py:41
  124.6 12.0 %collective-permute-done.8.refs_2_ = bf16[64,3584]{1,0:T(8,128)(2,1)S(1)} collective-permute-done((bf16[64,3584]{1,0:T(8,128)(2,1)S(1)}, bf16[64,3584]{1,0:T(8,128)(2,1)S(1)}, u32[]{:S(2)}, u32[]{:S(2)}) %collective-permute-start.8) | collective-permute-done | bytes 458784 | tf_op jit(solution)/shard_map/ppermute | solution.py:41
  144.4 4.6 %collective-permute-start.25 = (bf16[64,3584]{1,0:T(8,128)(2,1)S(1)}, bf16[64,3584]{1,0:T(8,128)(2,1)S(1)}, u32[]{:S(2)}, u32[]{:S(2)}) collective-permute-start(bf16[64,3584]{1,0:T(8,128)(2,1)S(1)} %get-tuple-element.57), channel_id=1, source_target_pairs={{0,7},{1,0},{2,1},{3,2},{4,3},{5,4},{6,5},{7,6},{8,15},{9,8},{10,9... | collective-permute-start | bytes 1376264 | tf_op jit(solution)/shard_map/ppermute | solution.py:41
  157.5 7.0 %collective-permute-done.24.refs_2_ = bf16[64,3584]{1,0:T(8,128)(2,1)S(1)} collective-permute-done((bf16[64,3584]{1,0:T(8,128)(2,1)S(1)}, bf16[64,3584]{1,0:T(8,128)(2,1)S(1)}, u32[]{:S(2)}, u32[]{:S(2)}) %collective-permute-start.24) | collective-permute-done | bytes 458784 | tf_op jit(solution)/shard_map/ppermute | solution.py:41
  167.4 4.6 %collective-permute-start.33 = (bf16[64,3584]{1,0:T(8,128)(2,1)}, bf16[64,3584]{1,0:T(8,128)(2,1)}, u32[]{:S(2)}, u32[]{:S(2)}) collective-permute-start(bf16[64,3584]{1,0:T(8,128)(2,1)} %get-tuple-element.65), channel_id=1, source_target_pairs={{0,7},{1,0},{2,1},{3,2},{4,3},{5,4},{6,5},{7,6},{8,15},{9,8},{10,9... | collective-permute-start | bytes 1376264 | tf_op jit(solution)/shard_map/ppermute | solution.py:41
  172.8 6.6 %collective-permute-done.31.refs_1_ = bf16[64,3584]{1,0:T(8,128)(2,1)S(1)} collective-permute-done((bf16[64,3584]{1,0:T(8,128)(2,1)S(1)}, bf16[64,3584]{1,0:T(8,128)(2,1)S(1)}, u32[]{:S(2)}, u32[]{:S(2)}) %collective-permute-start.31) | collective-permute-done | bytes 458784 | tf_op jit(solution)/shard_map/ppermute | solution.py:41
  184.4 4.6 %collective-permute-start.26 = (bf16[64,3584]{1,0:T(8,128)(2,1)}, bf16[64,3584]{1,0:T(8,128)(2,1)}, u32[]{:S(2)}, u32[]{:S(2)}) collective-permute-start(bf16[64,3584]{1,0:T(8,128)(2,1)} %shard_map.128.refs_2_), channel_id=1, source_target_pairs={{0,7},{1,0},{2,1},{3,2},{4,3},{5,4},{6,5},{7,6},{8,15},{9,8},{10,9... | collective-permute-start | bytes 1376264 | tf_op jit(solution)/shard_map/ppermute | solution.py:41
  195.1 5.5 %collective-permute-start.34 = (bf16[16,3584]{1,0:T(8,128)(2,1)S(1)}, bf16[16,3584]{1,0:T(8,128)(2,1)S(1)}, u32[]{:S(2)}, u32[]{:S(2)}) collective-permute-start(bf16[16,3584]{1,0:T(8,128)(2,1)S(1)} %get-tuple-element.66), channel_id=1, source_target_pairs={{0,480},{8,488},{16,496},{24,504},{32,0},{40,8},{48,16},{56,24},{6... | collective-permute-start | bytes 344072 | tf_op jit(solution)/shard_map/ppermute | solution.py:270
  211.5 4.2 %collective-permute-start.28 = (bf16[16,3584]{1,0:T(8,128)(2,1)S(1)}, bf16[16,3584]{1,0:T(8,128)(2,1)S(1)}, u32[]{:S(2)}, u32[]{:S(2)}) collective-permute-start(bf16[16,3584]{1,0:T(8,128)(2,1)S(1)} %get-tuple-element.60), channel_id=1, source_target_pairs={{0,40},{8,48},{16,56},{24,32},{32,72},{40,80},{48,88},{56,64},{64,... | collective-permute-start | bytes 344072 | tf_op jit(solution)/shard_map/ppermute | solution.py:270
  215.7 5.0 %collective-permute-start.29 = (bf16[16,3584]{1,0:T(8,128)(2,1)S(1)}, bf16[16,3584]{1,0:T(8,128)(2,1)S(1)}, u32[]{:S(2)}, u32[]{:S(2)}) collective-permute-start(bf16[16,3584]{1,0:T(8,128)(2,1)S(1)} %get-tuple-element.61), channel_id=1, source_target_pairs={{0,48},{8,56},{16,32},{24,40},{32,80},{40,88},{48,64},{56,72},{64,... | collective-permute-start | bytes 344072 | tf_op jit(solution)/shard_map/ppermute | solution.py:270
  223.9 5.4 %collective-permute-done.30.refs_5_ = bf16[16,3584]{1,0:T(8,128)(2,1)S(1)} collective-permute-done((bf16[16,3584]{1,0:T(8,128)(2,1)S(1)}, bf16[16,3584]{1,0:T(8,128)(2,1)S(1)}, u32[]{:S(2)}, u32[]{:S(2)}) %collective-permute-start.30) | collective-permute-done | bytes 114720 | tf_op jit(solution)/shard_map/ppermute | solution.py:270
  (113 shorter events, 87.6 us)
Async XLA Ops:
  20.1 22.0 %collective-permute-start.1 = (bf16[64,3584]{1,0:T(8,128)(2,1)S(1)}, bf16[64,3584]{1,0:T(8,128)(2,1)}, u32[]{:S(2)}, u32[]{:S(2)}) collective-permute-start(bf16[64,3584]{1,0:T(8,128)(2,1)S(1)} %bitcast.43), channel_id=1, source_target_pairs={{0,1},{1,2},{2,3},{3,4},{4,5},{5,6},{6,7},{7,0},{8,9},{9,10},{10,1... | collective-permute-start | bytes 1376264 | tf_op jit(solution)/shard_map/ppermute | solution.py:41
  25.1 18.9 %collective-permute-start.12 = (bf16[64,3584]{1,0:T(8,128)(2,1)}, bf16[64,3584]{1,0:T(8,128)(2,1)S(1)}, u32[]{:S(2)}, u32[]{:S(2)}) collective-permute-start(bf16[64,3584]{1,0:T(8,128)(2,1)} %bitcast.10.refs_1_), channel_id=1, source_target_pairs={{0,7},{1,0},{2,1},{3,2},{4,3},{5,4},{6,5},{7,6},{8,15},{9,8},{10,9... | collective-permute-start | bytes 1376264 | tf_op jit(solution)/shard_map/ppermute | solution.py:41
  36.8 16.6 %collective-permute-start.3 = (bf16[64,3584]{1,0:T(8,128)(2,1)S(1)}, bf16[64,3584]{1,0:T(8,128)(2,1)S(1)}, u32[]{:S(2)}, u32[]{:S(2)}) collective-permute-start(bf16[64,3584]{1,0:T(8,128)(2,1)S(1)} %bitcast.44), channel_id=1, source_target_pairs={{0,7},{1,0},{2,1},{3,2},{4,3},{5,4},{6,5},{7,6},{8,15},{9,8},{10,9... | collective-permute-start | bytes 1376264 | tf_op jit(solution)/shard_map/ppermute | solution.py:41
  39.0 19.8 %collective-permute-start.15 = (bf16[64,3584]{1,0:T(8,128)(2,1)}, bf16[64,3584]{1,0:T(8,128)(2,1)S(1)}, u32[]{:S(2)}, u32[]{:S(2)}) collective-permute-start(bf16[64,3584]{1,0:T(8,128)(2,1)} %bitcast.10.refs_1_), channel_id=1, source_target_pairs={{0,1},{1,2},{2,3},{3,4},{4,5},{5,6},{6,7},{7,0},{8,9},{9,10},{10,1... | collective-permute-start | bytes 1376264 | tf_op jit(solution)/shard_map/ppermute | solution.py:41
  42.1 18.6 %collective-permute-start.2 = (bf16[64,3584]{1,0:T(8,128)(2,1)}, bf16[64,3584]{1,0:T(8,128)(2,1)S(1)}, u32[]{:S(2)}, u32[]{:S(2)}) collective-permute-start(bf16[64,3584]{1,0:T(8,128)(2,1)} %collective-permute-done.1.refs_0_), channel_id=1, source_target_pairs={{0,1},{1,2},{2,3},{3,4},{4,5},{5,6},{6,7},{7,0},{8,9},{9,10},{10,1... | collective-permute-start | bytes 1376264 | tf_op jit(solution)/shard_map/ppermute | solution.py:41
  44.1 19.2 %collective-permute-start.13 = (bf16[64,3584]{1,0:T(8,128)(2,1)S(1)}, bf16[64,3584]{1,0:T(8,128)(2,1)S(1)}, u32[]{:S(2)}, u32[]{:S(2)}) collective-permute-start(bf16[64,3584]{1,0:T(8,128)(2,1)S(1)} %collective-permute-done.12.refs_0_), channel_id=1, source_target_pairs={{0,7},{1,0},{2,1},{3,2},{4,3},{5,4},{6,5},{7,6},{8,15},{9,8},{10,9... | collective-permute-start | bytes 1376264 | tf_op jit(solution)/shard_map/ppermute | solution.py:41
  53.4 19.7 %collective-permute-start.4 = (bf16[64,3584]{1,0:T(8,128)(2,1)S(1)}, bf16[64,3584]{1,0:T(8,128)(2,1)S(1)}, u32[]{:S(2)}, u32[]{:S(2)}) collective-permute-start(bf16[64,3584]{1,0:T(8,128)(2,1)S(1)} %collective-permute-done.3.refs_1_), channel_id=1, source_target_pairs={{0,7},{1,0},{2,1},{3,2},{4,3},{5,4},{6,5},{7,6},{8,15},{9,8},{10,9... | collective-permute-start | bytes 1376264 | tf_op jit(solution)/shard_map/ppermute | solution.py:41
  58.8 29.0 %collective-permute-start.16 = (bf16[64,3584]{1,0:T(8,128)(2,1)S(1)}, bf16[64,3584]{1,0:T(8,128)(2,1)S(1)}, u32[]{:S(2)}, u32[]{:S(2)}) collective-permute-start(bf16[64,3584]{1,0:T(8,128)(2,1)S(1)} %collective-permute-done.15.refs_1_), channel_id=1, source_target_pairs={{0,1},{1,2},{2,3},{3,4},{4,5},{5,6},{6,7},{7,0},{8,9},{9,10},{10,1... | collective-permute-start | bytes 1376264 | tf_op jit(solution)/shard_map/ppermute | solution.py:41
  60.7 29.0 %collective-permute-start.5 = (bf16[64,3584]{1,0:T(8,128)(2,1)S(1)}, bf16[64,3584]{1,0:T(8,128)(2,1)S(1)}, u32[]{:S(2)}, u32[]{:S(2)}) collective-permute-start(bf16[64,3584]{1,0:T(8,128)(2,1)S(1)} %collective-permute-done.2.refs_0_), channel_id=1, source_target_pairs={{0,1},{1,2},{2,3},{3,4},{4,5},{5,6},{6,7},{7,0},{8,9},{9,10},{10,1... | collective-permute-start | bytes 1376264 | tf_op jit(solution)/shard_map/ppermute | solution.py:41
  63.3 28.3 %collective-permute-start.14 = (bf16[64,3584]{1,0:T(8,128)(2,1)S(1)}, bf16[64,3584]{1,0:T(8,128)(2,1)S(1)}, u32[]{:S(2)}, u32[]{:S(2)}) collective-permute-start(bf16[64,3584]{1,0:T(8,128)(2,1)S(1)} %collective-permute-done.13.refs_0_), channel_id=1, source_target_pairs={{0,7},{1,0},{2,1},{3,2},{4,3},{5,4},{6,5},{7,6},{8,15},{9,8},{10,9... | collective-permute-start | bytes 1376264 | tf_op jit(solution)/shard_map/ppermute | solution.py:41
  73.1 23.1 %collective-permute-start.6 = (bf16[64,3584]{1,0:T(8,128)(2,1)S(1)}, bf16[64,3584]{1,0:T(8,128)(2,1)S(1)}, u32[]{:S(2)}, u32[]{:S(2)}) collective-permute-start(bf16[64,3584]{1,0:T(8,128)(2,1)S(1)} %collective-permute-done.4.refs_1_), channel_id=1, source_target_pairs={{0,7},{1,0},{2,1},{3,2},{4,3},{5,4},{6,5},{7,6},{8,15},{9,8},{10,9... | collective-permute-start | bytes 1376264 | tf_op jit(solution)/shard_map/ppermute | solution.py:41
  78.4 40.4 %collective-permute-start = (bf16[80,3584]{1,0:T(8,128)(2,1)}, bf16[80,3584]{1,0:T(8,128)(2,1)S(1)}, u32[]{:S(2)}, u32[]{:S(2)}) collective-permute-start(bf16[80,3584]{1,0:T(8,128)(2,1)} %copy-done.17), channel_id=1, source_target_pairs={{0,32},{32,64},{64,96},{96,128},{128,160},{160,192},{192,224},{224... | collective-permute-start | bytes 1720328 | tf_op jit(solution)/shard_map/ppermute | solution.py:41
  89.7 23.5 %collective-permute-start.7 = (bf16[64,3584]{1,0:T(8,128)(2,1)S(1)}, bf16[64,3584]{1,0:T(8,128)(2,1)S(1)}, u32[]{:S(2)}, u32[]{:S(2)}) collective-permute-start(bf16[64,3584]{1,0:T(8,128)(2,1)S(1)} %collective-permute-done.5.refs_0_), channel_id=1, source_target_pairs={{0,1},{1,2},{2,3},{3,4},{4,5},{5,6},{6,7},{7,0},{8,9},{9,10},{10,1... | collective-permute-start | bytes 1376264 | tf_op jit(solution)/shard_map/ppermute | solution.py:41
  91.6 24.4 %collective-permute-start.19 = (bf16[64,3584]{1,0:T(8,128)(2,1)S(1)}, bf16[64,3584]{1,0:T(8,128)(2,1)S(1)}, u32[]{:S(2)}, u32[]{:S(2)}) collective-permute-start(bf16[64,3584]{1,0:T(8,128)(2,1)S(1)} %collective-permute-done.14.refs_0_), channel_id=1, source_target_pairs={{0,7},{1,0},{2,1},{3,2},{4,3},{5,4},{6,5},{7,6},{8,15},{9,8},{10,9... | collective-permute-start | bytes 1376264 | tf_op jit(solution)/shard_map/ppermute | solution.py:41
  96.2 27.2 %collective-permute-start.18 = (bf16[80,3584]{1,0:T(8,128)(2,1)}, bf16[80,3584]{1,0:T(8,128)(2,1)S(1)}, u32[]{:S(2)}, u32[]{:S(2)}) collective-permute-start(bf16[80,3584]{1,0:T(8,128)(2,1)} %copy-done.16), channel_id=1, source_target_pairs={{0,480},{32,0},{64,32},{96,64},{128,96},{160,128},{192,160},{224,1... | collective-permute-start | bytes 1720328 | tf_op jit(solution)/shard_map/ppermute | solution.py:41
  103.3 21.3 %collective-permute-start.9 = (bf16[64,3584]{1,0:T(8,128)(2,1)S(1)}, bf16[64,3584]{1,0:T(8,128)(2,1)S(1)}, u32[]{:S(2)}, u32[]{:S(2)}) collective-permute-start(bf16[64,3584]{1,0:T(8,128)(2,1)S(1)} %get-tuple-element.44), channel_id=1, source_target_pairs={{0,1},{1,2},{2,3},{3,4},{4,5},{5,6},{6,7},{7,0},{8,9},{9,10},{10,1... | collective-permute-start | bytes 1376264 | tf_op jit(solution)/shard_map/ppermute | solution.py:41
  113.2 29.0 %collective-permute-start.21 = (bf16[64,3584]{1,0:T(8,128)(2,1)S(1)}, bf16[64,3584]{1,0:T(8,128)(2,1)S(1)}, u32[]{:S(2)}, u32[]{:S(2)}) collective-permute-start(bf16[64,3584]{1,0:T(8,128)(2,1)S(1)} %get-tuple-element.50), channel_id=1, source_target_pairs={{0,7},{1,0},{2,1},{3,2},{4,3},{5,4},{6,5},{7,6},{8,15},{9,8},{10,9... | collective-permute-start | bytes 1376264 | tf_op jit(solution)/shard_map/ppermute | solution.py:41
  116.0 20.7 %collective-permute-start.8 = (bf16[64,3584]{1,0:T(8,128)(2,1)S(1)}, bf16[64,3584]{1,0:T(8,128)(2,1)S(1)}, u32[]{:S(2)}, u32[]{:S(2)}) collective-permute-start(bf16[64,3584]{1,0:T(8,128)(2,1)S(1)} %shard_map.119), channel_id=1, source_target_pairs={{0,7},{1,0},{2,1},{3,2},{4,3},{5,4},{6,5},{7,6},{8,15},{9,8},{10,9... | collective-permute-start | bytes 1376264 | tf_op jit(solution)/shard_map/ppermute | solution.py:41
  118.8 23.4 %collective-permute-start.20 = (bf16[64,3584]{1,0:T(8,128)(2,1)S(1)}, bf16[64,3584]{1,0:T(8,128)(2,1)S(1)}, u32[]{:S(2)}, u32[]{:S(2)}) collective-permute-start(bf16[64,3584]{1,0:T(8,128)(2,1)S(1)} %shard_map.123), channel_id=1, source_target_pairs={{0,1},{1,2},{2,3},{3,4},{4,5},{5,6},{6,7},{7,0},{8,9},{9,10},{10,1... | collective-permute-start | bytes 1376264 | tf_op jit(solution)/shard_map/ppermute | solution.py:41
  142.4 22.1 %collective-permute-start.24 = (bf16[64,3584]{1,0:T(8,128)(2,1)S(1)}, bf16[64,3584]{1,0:T(8,128)(2,1)S(1)}, u32[]{:S(2)}, u32[]{:S(2)}) collective-permute-start(bf16[64,3584]{1,0:T(8,128)(2,1)S(1)} %get-tuple-element.51.refs_4_), channel_id=1, source_target_pairs={{0,1},{1,2},{2,3},{3,4},{4,5},{5,6},{6,7},{7,0},{8,9},{9,10},{10,1... | collective-permute-start | bytes 1376264 | tf_op jit(solution)/shard_map/ppermute | solution.py:41
  144.4 20.2 %collective-permute-start.25 = (bf16[64,3584]{1,0:T(8,128)(2,1)S(1)}, bf16[64,3584]{1,0:T(8,128)(2,1)S(1)}, u32[]{:S(2)}, u32[]{:S(2)}) collective-permute-start(bf16[64,3584]{1,0:T(8,128)(2,1)S(1)} %get-tuple-element.57), channel_id=1, source_target_pairs={{0,7},{1,0},{2,1},{3,2},{4,3},{5,4},{6,5},{7,6},{8,15},{9,8},{10,9... | collective-permute-start | bytes 1376264 | tf_op jit(solution)/shard_map/ppermute | solution.py:41
  167.4 24.8 %collective-permute-start.33 = (bf16[64,3584]{1,0:T(8,128)(2,1)}, bf16[64,3584]{1,0:T(8,128)(2,1)}, u32[]{:S(2)}, u32[]{:S(2)}) collective-permute-start(bf16[64,3584]{1,0:T(8,128)(2,1)} %get-tuple-element.65), channel_id=1, source_target_pairs={{0,7},{1,0},{2,1},{3,2},{4,3},{5,4},{6,5},{7,6},{8,15},{9,8},{10,9... | collective-permute-start | bytes 1376264 | tf_op jit(solution)/shard_map/ppermute | solution.py:41
  182.4 23.7 %collective-permute-start.22 = (bf16[64,3584]{1,0:T(8,128)(2,1)}, bf16[64,3584]{1,0:T(8,128)(2,1)}, u32[]{:S(2)}, u32[]{:S(2)}) collective-permute-start(bf16[64,3584]{1,0:T(8,128)(2,1)} %get-tuple-element.52), channel_id=1, source_target_pairs={{0,1},{1,2},{2,3},{3,4},{4,5},{5,6},{6,7},{7,0},{8,9},{9,10},{10,1... | collective-permute-start | bytes 1376264 | tf_op jit(solution)/shard_map/ppermute | solution.py:41
  184.4 23.7 %collective-permute-start.26 = (bf16[64,3584]{1,0:T(8,128)(2,1)}, bf16[64,3584]{1,0:T(8,128)(2,1)}, u32[]{:S(2)}, u32[]{:S(2)}) collective-permute-start(bf16[64,3584]{1,0:T(8,128)(2,1)} %shard_map.128.refs_2_), channel_id=1, source_target_pairs={{0,7},{1,0},{2,1},{3,2},{4,3},{5,4},{6,5},{7,6},{8,15},{9,8},{10,9... | collective-permute-start | bytes 1376264 | tf_op jit(solution)/shard_map/ppermute | solution.py:41
  (34 other events, 538.5 us)

commit v2 on v1

v2 whole, which is shorter than its diff:
```python
import jax
import jax.numpy as jnp
from jax import lax
from jax.experimental import pallas as pl
from jax.experimental.pallas import tpu as pltpu
from jax.sharding import Mesh, PartitionSpec as P

EXPERTS = 4
EXTRA = 16
VMEM_BYTES = 48 * 1024 * 1024


def vmem_spec():
    return pl.BlockSpec(memory_space=pltpu.VMEM)


def call(kernel, out_shape, arguments, flops=0, moved=0, after=(), plain=0):
    specs = [pl.BlockSpec()] * plain + [vmem_spec()] * (len(arguments) - plain)
    specs += [pl.BlockSpec(memory_space=pl.ANY)] * len(after)
    used = len(arguments)

    def ordered(*refs):
        kernel(*refs[:used], *refs[used + len(after) :])

    return pl.pallas_call(
        ordered,
        out_shape=out_shape,
        in_specs=specs,
        out_specs=jax.tree.map(lambda _: vmem_spec(), out_shape),
        compiler_params=pltpu.CompilerParams(vmem_limit_bytes=VMEM_BYTES),
        cost_estimate=pl.CostEstimate(flops=flops, bytes_accessed=moved, transcendentals=0),
    )(*arguments, *after)


def shifted(array, axis, by):
    peers = lax.axis_size(axis)
    return lax.ppermute(array, axis, [(i, (i + by) % peers) for i in range(peers)])


def shifted_twice(array, along, across):
    peers, sections = lax.axis_size("z"), lax.axis_size("pipe")
    pairs = [
        (s * peers + z, (s + across) % sections * peers + (z + along) % peers)
        for s in range(sections)
        for z in range(peers)
    ]
    return lax.ppermute(array, ("pipe", "z"), pairs)


def as_column(row):
    count = row.shape[1]
    place = lax.broadcasted_iota(jnp.int32, (count, count), 0)
    other = lax.broadcasted_iota(jnp.int32, (count, count), 1)
    return jnp.sum(jnp.where(place == other, row, jnp.zeros_like(row)), axis=1, keepdims=True)


def slots(routes, blocks, per_block):
    count = routes.shape[1]
    place = lax.broadcasted_iota(jnp.int32, (count, count), 0)
    other = lax.broadcasted_iota(jnp.int32, (count, count), 1)
    earlier = (as_column(routes) == routes) & (place < other)
    rank = jnp.sum(earlier.astype(jnp.int32), axis=0, keepdims=True)
    return place == blocks * per_block + rank


def prepare_kernel(states, routes, gain, buffer):
    count = states.shape[0]
    values = states[...].astype(jnp.float32)
    mean_square = jnp.mean(values * values, axis=-1, keepdims=True)
    normed = (values * lax.rsqrt(mean_square + 1e-06) * gain[...]).astype(jnp.bfloat16)
    placing = slots(routes[...], routes[...], count // EXPERTS).astype(jnp.bfloat16)
    buffer[...] = jnp.dot(placing, normed, preferred_element_type=jnp.float32).astype(jnp.bfloat16)


def prepare(states, routes, gain, after):
    rows, width = states.shape
    return call(
        prepare_kernel,
        jax.ShapeDtypeStruct((rows, width), jnp.bfloat16),
        (states, routes, gain),
        flops=2 * rows * rows * width,
        moved=4 * rows * width,
        after=after,
        plain=3,
    )


def expert_kernel(blocks, gate_ref, up_ref, down_ref, *outs):
    width = gate_ref.shape[1]
    depth = gate_ref.shape[0]
    step = depth // 7
    rows = [ref[...] for ref in blocks]
    rows = rows[0] if len(rows) == 1 else jnp.concatenate(rows, axis=0)
    total = jnp.zeros((rows.shape[0], 2 * width), jnp.float32)
    for k in range(0, depth, step):
        both = jnp.concatenate([gate_ref[k : k + step, :], up_ref[k : k + step, :]], axis=1)
        total += jnp.dot(rows[:, k : k + step], both, preferred_element_type=jnp.float32)
    gate_part, up_part = total[:, :width], total[:, width:]
    hidden = (gate_part * jax.nn.sigmoid(gate_part) * up_part).astype(jnp.bfloat16)
    for k in range(0, depth, step):
        part = jnp.dot(hidden, down_ref[:, k : k + step], preferred_element_type=jnp.float32)
        part = part.astype(jnp.bfloat16)
        first = 0
        for out in outs:
            count = out.shape[0]
            out[:, k : k + step] = part[first : first + count]
            first += count


def experts(blocks, gate_cols, up_cols, down_rows, passed=0, after=()):
    number = len(blocks)

    def kernel(*refs):
        outs = refs[number + 3 :]
        expert_kernel(refs[:number], *refs[number : number + 3], *outs[:number])
        for block, out in zip(refs, outs[number:]):
            out[...] = block[...]

    row_count = sum(block.shape[0] for block in blocks)
    shapes = [jax.ShapeDtypeStruct(block.shape, jnp.bfloat16) for block in blocks]
    return call(
        kernel,
        tuple(shapes + shapes[:passed]),
        (*blocks, gate_cols, up_cols, down_rows),
        flops=6 * row_count * gate_cols.size,
        moved=6 * gate_cols.size + 4 * sum(block.size for block in blocks),
        after=after,
    )


def own_kernel(states, routes, gates, rows, gate_ref, up_ref, down_ref, out):
    count = states.shape[0]
    expert_kernel([rows], gate_ref, up_ref, down_ref, out.at[pl.ds(0, count)])
    out[count : 2 * count, :] = states[...]
    gate = gates[...]
    high = gate.astype(jnp.bfloat16).astype(jnp.float32)
    middle = (gate - high).astype(jnp.bfloat16).astype(jnp.float32)
    low = gate - high - middle
    row = lax.broadcasted_iota(jnp.int32, (EXTRA, count), 0)
    table = jnp.zeros((EXTRA, count), jnp.float32)
    for place, term in enumerate((routes[...].astype(jnp.float32), high, middle, low)):
        table = jnp.where(row == place, term, table)
    out[2 * count :, :] = jnp.zeros((EXTRA, states.shape[1]), jnp.bfloat16)
    out[2 * count :, :count] = table.astype(jnp.bfloat16)


def own_part(states, routes, gates, rows, gate_cols, up_cols, down_rows, after):
    count, width = states.shape
    return call(
        own_kernel,
        jax.ShapeDtypeStruct((2 * count + EXTRA, width), jnp.bfloat16),
        (states, routes, gates, rows, gate_cols, up_cols, down_rows),
        flops=6 * count * gate_cols.size,
        moved=6 * gate_cols.size + 10 * states.size,
        after=after,
        plain=3,
    )


def add(parts, sums, after):
    number = len(parts)

    def kernel(*refs):
        for part, received, out in zip(refs[:number], refs[number:], refs[2 * number :]):
            total = part[...].astype(jnp.float32) + received[...].astype(jnp.float32)
            out[...] = total.astype(jnp.bfloat16)

    return call(
        kernel,
        tuple(jax.ShapeDtypeStruct(part.shape, jnp.bfloat16) for part in parts),
        (*parts, *sums),
        flops=sum(part.size for part in parts),
        moved=6 * sum(part.size for part in parts),
        after=after,
    )


def finish_kernel(*refs):
    *refs, out = refs
    count = refs[1].shape[0]
    slot_count = count // EXPERTS
    number = len(refs) // 3
    for m in range(number):
        shipped, from_left, from_right = refs[3 * m : 3 * m + 3]
        total = shipped[:count, :].astype(jnp.float32) + from_left[...].astype(jnp.float32)
        total = (total + from_right[...].astype(jnp.float32)).astype(jnp.bfloat16)
        for e in range(EXPERTS):
            start = (e * number + m) * slot_count
            out[start : start + slot_count, :] = total[e * slot_count : (e + 1) * slot_count]


def finish(shipped, sums):
    rows, width = sums[0][1].shape
    arguments = []
    for m in range(2):
        arguments += [shipped[m], sums[m][1], sums[m][-1]]
    return call(
        finish_kernel,
        jax.ShapeDtypeStruct((2 * rows, width), jnp.bfloat16),
        arguments,
        flops=4 * rows * width,
        moved=16 * rows * width,
    )


def combine_kernel(*refs):
    *shipped, rows, out_forward, out_backward = refs
    for m, out in enumerate((out_forward, out_backward)):
        count = out.shape[0]
        slot_count = count // EXPERTS
        table = shipped[m][2 * count :, :count].astype(jnp.float32)
        routes = table[0:1].astype(jnp.int32)
        gates = table[1:2] + table[2:3] + table[3:4]
        placing = slots(routes, routes, slot_count).astype(jnp.bfloat16)
        starts = [(2 * e + m) * slot_count for e in range(EXPERTS)]
        returned = jnp.concatenate([rows[s : s + slot_count, :] for s in starts], axis=0)
        picked = lax.dot_general(
            placing, returned, (((0,), (0,)), ((), ())), preferred_element_type=jnp.float32
        )
        mixed = shipped[m][count : 2 * count, :].astype(jnp.float32) + as_column(gates) * picked
        out[...] = mixed.astype(jnp.bfloat16)


def combine(shipped, rows):
    count, width = rows.shape[0] // 2, rows.shape[1]
    return call(
        combine_kernel,
        (jax.ShapeDtypeStruct((count, width), jnp.bfloat16),) * 2,
        (*shipped, rows),
        flops=4 * count * count * width,
        moved=16 * count * width,
    )


def body(
    x_forward,
    x_backward,
    norm_gain,
    w_gate,
    w_up,
    w_down,
    routes_forward,
    routes_backward,
    gates_forward,
    gates_backward,
):
    weights = (w_gate[0], w_up[0], w_down[0])
    ring = lax.axis_size("z")
    far = ring // 2
    states = (x_forward[0], x_backward[0])
    routes = (routes_forward.reshape(1, -1), routes_backward.reshape(1, -1))
    gates = (gates_forward.reshape(1, -1), gates_backward.reshape(1, -1))
    travel = (1, -1)

    here, last = [], ()
    for m in range(2):
        buffer = prepare(states[m], routes[m], norm_gain, last)
        here.append(lax.all_to_all(buffer, "x", split_axis=0, concat_axis=0, tiled=True))
        last = (here[m],)

    parts = [{}, {}]
    moving = [{way: here[m] for way in (1, -1)} for m in range(2)]
    last, shipped = (), []
    for step in range(1, far + 1):
        for m in range(2):
            ways = [way for way in (travel[m], -travel[m]) if step < far or way == travel[m]]
            for way in ways:
                moving[m][way] = shifted(moving[m][way], "z", way)
        for m in range(2):
            ways = [way for way in (travel[m], -travel[m]) if step < far or way == travel[m]]
            if step == 1:
                own = own_part(states[m], routes[m], gates[m], here[m], *weights, last)
                shipped.append(shifted(own, "pipe", travel[m]))
                last = (own,)
            goes_on = [way for way in ways if step + 1 < far or (step < far and way == travel[m])]
            results = experts(
                [moving[m][way] for way in ways],
                *weights,
                passed=len(goes_on),
                after=last + ((shipped[m],) if step == far - 1 else ()),
            )
            last = (results[0],)
            for way, part in zip(ways, results):
                parts[m][-way * step] = part
            for way, block in zip(goes_on, results[len(ways) :]):
                moving[m][way] = block

    sums = [{}, {}]

    def send(m, stage, last):
        left = {-travel[m]: far - stage, travel[m]: far - 1 - stage}
        ways = [way for way in left if left[way] > 0]
        totals = [parts[m][way * left[way]] for way in ways]
        if stage > 0:
            totals = add(totals, [sums[m][way] for way in ways], last)
            last = (totals[0],)
        for way, total in zip(ways, totals):
            if left[way] == 1:
                sums[m][way] = shifted_twice(total, way, travel[m])
            else:
                sums[m][way] = shifted(total, "z", way)
        return last

    for stage in range(far):
        for m in range(2):
            last = send(m, stage, last)
    total = finish(shipped, sums)
    returned = lax.all_to_all(total, "x", split_axis=0, concat_axis=0, tiled=True)
    done_forward, done_backward = combine(shipped, returned)
    return (done_forward[None], done_backward[None])


def solution(mesh):
    sections, members = mesh.devices.shape
    inner = Mesh(
        mesh.devices.reshape(sections, EXPERTS, members // EXPERTS), ("pipe", "x", "z")
    )
    tokens = P("pipe", ("x", "z"), None)
    placed = (
        tokens,
        tokens,
        P("pipe", None),
        P("pipe", None, ("x", "z")),
        P("pipe", None, ("x", "z")),
        tokens,
        tokens,
        tokens,
        tokens,
        tokens,
    )
    return jax.shard_map(
        body, mesh=inner, in_specs=placed, out_specs=(tokens, tokens), check_vma=False
    )
```

time: 232 us -> 224 us (0.966)
  the two profiles are of different devices: /device:TPU:7 before, /device:TPU:25 now
where the time goes in v2:
time: 224 us; the launch traced here: 221 us
  starting transfers between devices  114 us (51%)
  waiting for transfers between devices  53.3 us (24%)
  blocking collectives  26 us (12%)
  Pallas kernels  20.1 us (9%)
  local copies, waits for them, and re-layouts  6.09 us (3%)
    ppermute x26, starting transfers between devices, shifted(): lax.ppermute(array, axis, [(i, (i + by) % peers) for i in range(peers)])  88.1 us
    ppermute x26, waiting for transfers between devices, shifted(): lax.ppermute(array, axis, [(i, (i + by) % peers) for i in range(peers)])  41.3 us
    ppermute x4, starting transfers between devices, shifted_twice(): return lax.ppermute(array, ('pipe', 'z'), pairs)  22 us
    pallas_call x20, Pallas kernels, call(): pl.pallas_call(ordered, out_shape=out_shape, in_specs=specs, out_specs=ja...  20.1 us
    all_to_all x1, blocking collectives, body(): lax.all_to_all(total, 'x', split_axis=0, concat_axis=0, tiled=True)  14.5 us
    ppermute x4, waiting for transfers between devices, shifted_twice(): return lax.ppermute(array, ('pipe', 'z'), pairs)  12 us
    all_to_all x1, blocking collectives, body(): lax.all_to_all(buffer, 'x', split_axis=0, concat_axis=0, tiled=True)  11.5 us
    unnamed x34, local copies, waits for them, and re-layouts  6.09 us
  transfers between devices with their start and end apart: 31, of which 11 were waited for; matrix products, arithmetic and copies ran while one was open for 0% of the time, Pallas kernels for 7%

profile of v2, /device:TPU:25, one launch (start us, length us, event | category | flops | bytes accessed | tf_op | source)
XLA Modules:
  0.0 221.0 jit_solution(3747896023966571309)
XLA Ops:
  3.5 11.5 %all_to_all.33 = bf16[4,16,3584]{2,1,0:T(8,128)(2,1)S(1)} all-to-all(bf16[4,16,3584]{2,1,0:T(8,128)(2,1)S(1)} %bitcast.55), channel_id=1, replica_groups=mesh['pipe'=16,'x'=4,'z'=8] {'x'}, dimensions={0} | all-to-all | bytes 917504 | tf_op jit(solution)/shard_map/all_to_all | solution.py:258
  15.0 4.0 %collective-permute-start.1 = (bf16[64,3584]{1,0:T(8,128)(2,1)S(1)}, bf16[64,3584]{1,0:T(8,128)(2,1)}, u32[]{:S(2)}, u32[]{:S(2)}) collective-permute-start(bf16[64,3584]{1,0:T(8,128)(2,1)S(1)} %bitcast.47), channel_id=1, source_target_pairs={{0,1},{1,2},{2,3},{3,4},{4,5},{5,6},{6,7},{7,0},{8,9},{9,10},{10,1... | collective-permute-start | bytes 1376264 | tf_op jit(solution)/shard_map/ppermute | solution.py:37
  19.0 8.6 %collective-permute-start.2 = (bf16[64,3584]{1,0:T(8,128)(2,1)S(1)}, bf16[64,3584]{1,0:T(8,128)(2,1)}, u32[]{:S(2)}, u32[]{:S(2)}) collective-permute-start(bf16[64,3584]{1,0:T(8,128)(2,1)S(1)} %bitcast.48), channel_id=1, source_target_pairs={{0,7},{1,0},{2,1},{3,2},{4,3},{5,4},{6,5},{7,6},{8,15},{9,8},{10,9... | collective-permute-start | bytes 1376264 | tf_op jit(solution)/shard_map/ppermute | solution.py:37
  29.5 4.1 %all-to-all-start.1 = ((bf16[4,16,3584]{2,1,0:T(8,128)(2,1)}), bf16[4,16,3584]{2,1,0:T(8,128)(2,1)}, u32[]{:S(2)}, u32[]{:S(2)}) async-start(bf16[4,16,3584]{2,1,0:T(8,128)(2,1)} %bitcast.56), calls=%async_computation.1 | async-start | bytes 917504 | tf_op jit(solution)/shard_map/all_to_all | solution.py:258
  37.2 4.8 %collective-permute-start = (bf16[144,3584]{1,0:T(8,128)(2,1)}, bf16[144,3584]{1,0:T(8,128)(2,1)}, u32[]{:S(2)}, u32[]{:S(2)}) collective-permute-start(bf16[144,3584]{1,0:T(8,128)(2,1)} %shard_map.114.refs_5_), channel_id=1, source_target_pairs={{0,32},{32,64},{64,96},{96,128},{128,160},{160,192},{192,224},{224... | collective-permute-start | bytes 3096584 | tf_op jit(solution)/shard_map/ppermute | solution.py:37
  42.0 3.8 %collective-permute-start.6 = (bf16[64,3584]{1,0:T(8,128)(2,1)}, bf16[64,3584]{1,0:T(8,128)(2,1)S(1)}, u32[]{:S(2)}, u32[]{:S(2)}) collective-permute-start(bf16[64,3584]{1,0:T(8,128)(2,1)} %bitcast.12.refs_3_), channel_id=1, source_target_pairs={{0,7},{1,0},{2,1},{3,2},{4,3},{5,4},{6,5},{7,6},{8,15},{9,8},{10,9... | collective-permute-start | bytes 1376264 | tf_op jit(solution)/shard_map/ppermute | solution.py:37
  56.8 4.8 %collective-permute-start.5 = (bf16[64,3584]{1,0:T(8,128)(2,1)S(1)}, bf16[64,3584]{1,0:T(8,128)(2,1)S(1)}, u32[]{:S(2)}, u32[]{:S(2)}) collective-permute-start(bf16[64,3584]{1,0:T(8,128)(2,1)S(1)} %get-tuple-element.36), channel_id=1, source_target_pairs={{0,7},{1,0},{2,1},{3,2},{4,3},{5,4},{6,5},{7,6},{8,15},{9,8},{10,9... | collective-permute-start | bytes 1376264 | tf_op jit(solution)/shard_map/ppermute | solution.py:37
  62.9 3.6 %collective-permute-start.10 = (bf16[64,3584]{1,0:T(8,128)(2,1)S(1)}, bf16[64,3584]{1,0:T(8,128)(2,1)S(1)}, u32[]{:S(2)}, u32[]{:S(2)}) collective-permute-start(bf16[64,3584]{1,0:T(8,128)(2,1)S(1)} %get-tuple-element.42), channel_id=1, source_target_pairs={{0,7},{1,0},{2,1},{3,2},{4,3},{5,4},{6,5},{7,6},{8,15},{9,8},{10,9... | collective-permute-start | bytes 1376264 | tf_op jit(solution)/shard_map/ppermute | solution.py:37
  75.0 6.1 %collective-permute-done.10.refs_0_ = bf16[64,3584]{1,0:T(8,128)(2,1)S(1)} collective-permute-done((bf16[64,3584]{1,0:T(8,128)(2,1)S(1)}, bf16[64,3584]{1,0:T(8,128)(2,1)S(1)}, u32[]{:S(2)}, u32[]{:S(2)}) %collective-permute-start.10) | collective-permute-done | bytes 458784 | tf_op jit(solution)/shard_map/ppermute | solution.py:37
  81.1 5.3 %collective-permute-start.9 = (bf16[64,3584]{1,0:T(8,128)(2,1)S(1)}, bf16[64,3584]{1,0:T(8,128)(2,1)S(1)}, u32[]{:S(2)}, u32[]{:S(2)}) collective-permute-start(bf16[64,3584]{1,0:T(8,128)(2,1)S(1)} %get-tuple-element.41), channel_id=1, source_target_pairs={{0,7},{1,0},{2,1},{3,2},{4,3},{5,4},{6,5},{7,6},{8,15},{9,8},{10,9... | collective-permute-start | bytes 1376264 | tf_op jit(solution)/shard_map/ppermute | solution.py:37
  98.8 6.0 %collective-permute-done.13.refs_0_ = bf16[64,3584]{1,0:T(8,128)(2,1)S(1)} collective-permute-done((bf16[64,3584]{1,0:T(8,128)(2,1)S(1)}, bf16[64,3584]{1,0:T(8,128)(2,1)S(1)}, u32[]{:S(2)}, u32[]{:S(2)}) %collective-permute-start.13) | collective-permute-done | bytes 458784 | tf_op jit(solution)/shard_map/ppermute | solution.py:37
  106.0 5.3 %collective-permute-start.17 = (bf16[64,3584]{1,0:T(8,128)(2,1)S(1)}, bf16[64,3584]{1,0:T(8,128)(2,1)S(1)}, u32[]{:S(2)}, u32[]{:S(2)}) collective-permute-start(bf16[64,3584]{1,0:T(8,128)(2,1)S(1)} %get-tuple-element.52), channel_id=1, source_target_pairs={{0,7},{1,0},{2,1},{3,2},{4,3},{5,4},{6,5},{7,6},{8,15},{9,8},{10,9... | collective-permute-start | bytes 1376264 | tf_op jit(solution)/shard_map/ppermute | solution.py:37
  113.3 4.6 %collective-permute-start.21 = (bf16[64,3584]{1,0:T(8,128)(2,1)S(1)}, bf16[64,3584]{1,0:T(8,128)(2,1)S(1)}, u32[]{:S(2)}, u32[]{:S(2)}) collective-permute-start(bf16[64,3584]{1,0:T(8,128)(2,1)S(1)} %get-tuple-element.56), channel_id=1, source_target_pairs={{0,7},{1,0},{2,1},{3,2},{4,3},{5,4},{6,5},{7,6},{8,15},{9,8},{10,9... | collective-permute-start | bytes 1376264 | tf_op jit(solution)/shard_map/ppermute | solution.py:37
  121.6 3.4 %collective-permute-start.20 = (bf16[64,3584]{1,0:T(8,128)(2,1)S(1)}, bf16[64,3584]{1,0:T(8,128)(2,1)S(1)}, u32[]{:S(2)}, u32[]{:S(2)}) collective-permute-start(bf16[64,3584]{1,0:T(8,128)(2,1)S(1)} %shard_map.124.refs_4_), channel_id=1, source_target_pairs={{0,1},{1,2},{2,3},{3,4},{4,5},{5,6},{6,7},{7,0},{8,9},{9,10},{10,1... | collective-permute-start | bytes 1376264 | tf_op jit(solution)/shard_map/ppermute | solution.py:37
  125.0 13.7 %collective-permute-done.15.refs_2_ = bf16[64,3584]{1,0:T(8,128)(2,1)S(1)} collective-permute-done((bf16[64,3584]{1,0:T(8,128)(2,1)S(1)}, bf16[64,3584]{1,0:T(8,128)(2,1)S(1)}, u32[]{:S(2)}, u32[]{:S(2)}) %collective-permute-start.15) | collective-permute-done | bytes 458784 | tf_op jit(solution)/shard_map/ppermute | solution.py:37
  138.9 5.3 %collective-permute-start.18 = (bf16[64,3584]{1,0:T(8,128)(2,1)S(1)}, bf16[64,3584]{1,0:T(8,128)(2,1)S(1)}, u32[]{:S(2)}, u32[]{:S(2)}) collective-permute-start(bf16[64,3584]{1,0:T(8,128)(2,1)S(1)} %get-tuple-element.53.refs_4_), channel_id=1, source_target_pairs={{0,7},{1,0},{2,1},{3,2},{4,3},{5,4},{6,5},{7,6},{8,15},{9,8},{10,9... | collective-permute-start | bytes 1376264 | tf_op jit(solution)/shard_map/ppermute | solution.py:37
  148.5 4.6 %collective-permute-start.25 = (bf16[64,3584]{1,0:T(8,128)(2,1)S(1)}, bf16[64,3584]{1,0:T(8,128)(2,1)S(1)}, u32[]{:S(2)}, u32[]{:S(2)}) collective-permute-start(bf16[64,3584]{1,0:T(8,128)(2,1)S(1)} %get-tuple-element.61), channel_id=1, source_target_pairs={{0,7},{1,0},{2,1},{3,2},{4,3},{5,4},{6,5},{7,6},{8,15},{9,8},{10,9... | collective-permute-start | bytes 1376264 | tf_op jit(solution)/shard_map/ppermute | solution.py:37
  153.1 3.0 %collective-permute-done.19.refs_3_ = bf16[64,3584]{1,0:T(8,128)(2,1)S(1)} collective-permute-done((bf16[64,3584]{1,0:T(8,128)(2,1)S(1)}, bf16[64,3584]{1,0:T(8,128)(2,1)S(1)}, u32[]{:S(2)}, u32[]{:S(2)}) %collective-permute-start.19) | collective-permute-done | bytes 458784 | tf_op jit(solution)/shard_map/ppermute | solution.py:37
  158.2 7.7 %collective-permute-done.24.refs_2_ = bf16[64,3584]{1,0:T(8,128)(2,1)S(1)} collective-permute-done((bf16[64,3584]{1,0:T(8,128)(2,1)S(1)}, bf16[64,3584]{1,0:T(8,128)(2,1)S(1)}, u32[]{:S(2)}, u32[]{:S(2)}) %collective-permute-start.24) | collective-permute-done | bytes 458784 | tf_op jit(solution)/shard_map/ppermute | solution.py:37
  168.1 10.6 %collective-permute-start.22 = (bf16[64,3584]{1,0:T(8,128)(2,1)S(1)}, bf16[64,3584]{1,0:T(8,128)(2,1)S(1)}, u32[]{:S(2)}, u32[]{:S(2)}) collective-permute-start(bf16[64,3584]{1,0:T(8,128)(2,1)S(1)} %get-tuple-element.58), channel_id=1, source_target_pairs={{0,33},{1,34},{2,35},{3,36},{4,37},{5,38},{6,39},{7,32},{32,65},{3... | collective-permute-start | bytes 1376264 | tf_op jit(solution)/shard_map/ppermute | solution.py:47
  180.7 7.6 %collective-permute-start.26 = (bf16[64,3584]{1,0:T(8,128)(2,1)S(1)}, bf16[64,3584]{1,0:T(8,128)(2,1)S(1)}, u32[]{:S(2)}, u32[]{:S(2)}) collective-permute-start(bf16[64,3584]{1,0:T(8,128)(2,1)S(1)} %shard_map.129.refs_2_), channel_id=1, source_target_pairs={{0,39},{1,32},{2,33},{3,34},{4,35},{5,36},{6,37},{7,38},{32,71},{3... | collective-permute-start | bytes 1376264 | tf_op jit(solution)/shard_map/ppermute | solution.py:47
  191.4 4.9 %collective-permute-done.29.refs_5_ = bf16[64,3584]{1,0:T(8,128)(2,1)S(1)} collective-permute-done((bf16[64,3584]{1,0:T(8,128)(2,1)S(1)}, bf16[64,3584]{1,0:T(8,128)(2,1)S(1)}, u32[]{:S(2)}, u32[]{:S(2)}) %collective-permute-start.29) | collective-permute-done | bytes 458784 | tf_op jit(solution)/shard_map/ppermute | solution.py:47
  196.3 6.1 %collective-permute-done.26.refs_2_ = bf16[64,3584]{1,0:T(8,128)(2,1)S(1)} collective-permute-done((bf16[64,3584]{1,0:T(8,128)(2,1)S(1)}, bf16[64,3584]{1,0:T(8,128)(2,1)S(1)}, u32[]{:S(2)}, u32[]{:S(2)}) %collective-permute-start.26) | collective-permute-done | bytes 458784 | tf_op jit(solution)/shard_map/ppermute | solution.py:47
  204.0 14.5 %all_to_all.34 = bf16[4,32,3584]{2,1,0:T(8,128)(2,1)S(1)} all-to-all(bf16[4,32,3584]{2,1,0:T(8,128)(2,1)S(1)} %bitcast.51), channel_id=1, replica_groups=mesh['pipe'=16,'x'=4,'z'=8] {'x'}, dimensions={0} | all-to-all | bytes 1835008 | tf_op jit(solution)/shard_map/all_to_all | solution.py:308
  (94 shorter events, 66.0 us)
Async XLA Ops:
  15.0 32.7 %collective-permute-start.1 = (bf16[64,3584]{1,0:T(8,128)(2,1)S(1)}, bf16[64,3584]{1,0:T(8,128)(2,1)}, u32[]{:S(2)}, u32[]{:S(2)}) collective-permute-start(bf16[64,3584]{1,0:T(8,128)(2,1)S(1)} %bitcast.47), channel_id=1, source_target_pairs={{0,1},{1,2},{2,3},{3,4},{4,5},{5,6},{6,7},{7,0},{8,9},{9,10},{10,1... | collective-permute-start | bytes 1376264 | tf_op jit(solution)/shard_map/ppermute | solution.py:37
  19.0 28.8 %collective-permute-start.2 = (bf16[64,3584]{1,0:T(8,128)(2,1)S(1)}, bf16[64,3584]{1,0:T(8,128)(2,1)}, u32[]{:S(2)}, u32[]{:S(2)}) collective-permute-start(bf16[64,3584]{1,0:T(8,128)(2,1)S(1)} %bitcast.48), channel_id=1, source_target_pairs={{0,7},{1,0},{2,1},{3,2},{4,3},{5,4},{6,5},{7,6},{8,15},{9,8},{10,9... | collective-permute-start | bytes 1376264 | tf_op jit(solution)/shard_map/ppermute | solution.py:37
  37.2 53.2 %collective-permute-start = (bf16[144,3584]{1,0:T(8,128)(2,1)}, bf16[144,3584]{1,0:T(8,128)(2,1)}, u32[]{:S(2)}, u32[]{:S(2)}) collective-permute-start(bf16[144,3584]{1,0:T(8,128)(2,1)} %shard_map.114.refs_5_), channel_id=1, source_target_pairs={{0,32},{32,64},{64,96},{96,128},{128,160},{160,192},{192,224},{224... | collective-permute-start | bytes 3096584 | tf_op jit(solution)/shard_map/ppermute | solution.py:37
  42.0 14.8 %collective-permute-start.6 = (bf16[64,3584]{1,0:T(8,128)(2,1)}, bf16[64,3584]{1,0:T(8,128)(2,1)S(1)}, u32[]{:S(2)}, u32[]{:S(2)}) collective-permute-start(bf16[64,3584]{1,0:T(8,128)(2,1)} %bitcast.12.refs_3_), channel_id=1, source_target_pairs={{0,7},{1,0},{2,1},{3,2},{4,3},{5,4},{6,5},{7,6},{8,15},{9,8},{10,9... | collective-permute-start | bytes 1376264 | tf_op jit(solution)/shard_map/ppermute | solution.py:37
  45.8 15.9 %collective-permute-start.7 = (bf16[64,3584]{1,0:T(8,128)(2,1)}, bf16[64,3584]{1,0:T(8,128)(2,1)S(1)}, u32[]{:S(2)}, u32[]{:S(2)}) collective-permute-start(bf16[64,3584]{1,0:T(8,128)(2,1)} %bitcast.12.refs_3_), channel_id=1, source_target_pairs={{0,1},{1,2},{2,3},{3,4},{4,5},{5,6},{6,7},{7,0},{8,9},{9,10},{10,1... | collective-permute-start | bytes 1376264 | tf_op jit(solution)/shard_map/ppermute | solution.py:37
  50.2 18.7 %collective-permute-start.4 = (bf16[64,3584]{1,0:T(8,128)(2,1)S(1)}, bf16[64,3584]{1,0:T(8,128)(2,1)S(1)}, u32[]{:S(2)}, u32[]{:S(2)}) collective-permute-start(bf16[64,3584]{1,0:T(8,128)(2,1)S(1)} %get-tuple-element.35), channel_id=1, source_target_pairs={{0,1},{1,2},{2,3},{3,4},{4,5},{5,6},{6,7},{7,0},{8,9},{9,10},{10,1... | collective-permute-start | bytes 1376264 | tf_op jit(solution)/shard_map/ppermute | solution.py:37
  54.7 44.1 %collective-permute-start.3 = (bf16[144,3584]{1,0:T(8,128)(2,1)S(1)}, bf16[144,3584]{1,0:T(8,128)(2,1)S(1)}, u32[]{:S(2)}, u32[]{:S(2)}) collective-permute-start(bf16[144,3584]{1,0:T(8,128)(2,1)S(1)} %shard_map.117.refs_5_), channel_id=1, source_target_pairs={{0,480},{32,0},{64,32},{96,64},{128,96},{160,128},{192,160},{224,1... | collective-permute-start | bytes 3096584 | tf_op jit(solution)/shard_map/ppermute | solution.py:37
  62.9 18.2 %collective-permute-start.10 = (bf16[64,3584]{1,0:T(8,128)(2,1)S(1)}, bf16[64,3584]{1,0:T(8,128)(2,1)S(1)}, u32[]{:S(2)}, u32[]{:S(2)}) collective-permute-start(bf16[64,3584]{1,0:T(8,128)(2,1)S(1)} %get-tuple-element.42), channel_id=1, source_target_pairs={{0,7},{1,0},{2,1},{3,2},{4,3},{5,4},{6,5},{7,6},{8,15},{9,8},{10,9... | collective-permute-start | bytes 1376264 | tf_op jit(solution)/shard_map/ppermute | solution.py:37
  68.8 17.5 %collective-permute-start.11 = (bf16[64,3584]{1,0:T(8,128)(2,1)S(1)}, bf16[64,3584]{1,0:T(8,128)(2,1)S(1)}, u32[]{:S(2)}, u32[]{:S(2)}) collective-permute-start(bf16[64,3584]{1,0:T(8,128)(2,1)S(1)} %get-tuple-element.43), channel_id=1, source_target_pairs={{0,1},{1,2},{2,3},{3,4},{4,5},{5,6},{6,7},{7,0},{8,9},{9,10},{10,1... | collective-permute-start | bytes 1376264 | tf_op jit(solution)/shard_map/ppermute | solution.py:37
  72.4 20.5 %collective-permute-start.8 = (bf16[64,3584]{1,0:T(8,128)(2,1)S(1)}, bf16[64,3584]{1,0:T(8,128)(2,1)S(1)}, u32[]{:S(2)}, u32[]{:S(2)}) collective-permute-start(bf16[64,3584]{1,0:T(8,128)(2,1)S(1)} %get-tuple-element.40), channel_id=1, source_target_pairs={{0,1},{1,2},{2,3},{3,4},{4,5},{5,6},{6,7},{7,0},{8,9},{9,10},{10,1... | collective-permute-start | bytes 1376264 | tf_op jit(solution)/shard_map/ppermute | solution.py:37
  87.6 17.2 %collective-permute-start.13 = (bf16[64,3584]{1,0:T(8,128)(2,1)S(1)}, bf16[64,3584]{1,0:T(8,128)(2,1)S(1)}, u32[]{:S(2)}, u32[]{:S(2)}) collective-permute-start(bf16[64,3584]{1,0:T(8,128)(2,1)S(1)} %get-tuple-element.48), channel_id=1, source_target_pairs={{0,7},{1,0},{2,1},{3,2},{4,3},{5,4},{6,5},{7,6},{8,15},{9,8},{10,9... | collective-permute-start | bytes 1376264 | tf_op jit(solution)/shard_map/ppermute | solution.py:37
  90.4 14.4 %collective-permute-start.14 = (bf16[64,3584]{1,0:T(8,128)(2,1)S(1)}, bf16[64,3584]{1,0:T(8,128)(2,1)S(1)}, u32[]{:S(2)}, u32[]{:S(2)}) collective-permute-start(bf16[64,3584]{1,0:T(8,128)(2,1)S(1)} %get-tuple-element.49), channel_id=1, source_target_pairs={{0,1},{1,2},{2,3},{3,4},{4,5},{5,6},{6,7},{7,0},{8,9},{9,10},{10,1... | collective-permute-start | bytes 1376264 | tf_op jit(solution)/shard_map/ppermute | solution.py:37
  96.2 21.7 %collective-permute-start.12 = (bf16[64,3584]{1,0:T(8,128)(2,1)S(1)}, bf16[64,3584]{1,0:T(8,128)(2,1)S(1)}, u32[]{:S(2)}, u32[]{:S(2)}) collective-permute-start(bf16[64,3584]{1,0:T(8,128)(2,1)S(1)} %get-tuple-element.47), channel_id=1, source_target_pairs={{0,1},{1,2},{2,3},{3,4},{4,5},{5,6},{6,7},{7,0},{8,9},{9,10},{10,1... | collective-permute-start | bytes 1376264 | tf_op jit(solution)/shard_map/ppermute | solution.py:37
  106.0 14.7 %collective-permute-start.17 = (bf16[64,3584]{1,0:T(8,128)(2,1)S(1)}, bf16[64,3584]{1,0:T(8,128)(2,1)S(1)}, u32[]{:S(2)}, u32[]{:S(2)}) collective-permute-start(bf16[64,3584]{1,0:T(8,128)(2,1)S(1)} %get-tuple-element.52), channel_id=1, source_target_pairs={{0,7},{1,0},{2,1},{3,2},{4,3},{5,4},{6,5},{7,6},{8,15},{9,8},{10,9... | collective-permute-start | bytes 1376264 | tf_op jit(solution)/shard_map/ppermute | solution.py:37
  113.3 32.9 %collective-permute-start.21 = (bf16[64,3584]{1,0:T(8,128)(2,1)S(1)}, bf16[64,3584]{1,0:T(8,128)(2,1)S(1)}, u32[]{:S(2)}, u32[]{:S(2)}) collective-permute-start(bf16[64,3584]{1,0:T(8,128)(2,1)S(1)} %get-tuple-element.56), channel_id=1, source_target_pairs={{0,7},{1,0},{2,1},{3,2},{4,3},{5,4},{6,5},{7,6},{8,15},{9,8},{10,9... | collective-permute-start | bytes 1376264 | tf_op jit(solution)/shard_map/ppermute | solution.py:37
  118.8 19.9 %collective-permute-start.15 = (bf16[64,3584]{1,0:T(8,128)(2,1)S(1)}, bf16[64,3584]{1,0:T(8,128)(2,1)S(1)}, u32[]{:S(2)}, u32[]{:S(2)}) collective-permute-start(bf16[64,3584]{1,0:T(8,128)(2,1)S(1)} %shard_map.123.refs_4_), channel_id=1, source_target_pairs={{0,7},{1,0},{2,1},{3,2},{4,3},{5,4},{6,5},{7,6},{8,15},{9,8},{10,9... | collective-permute-start | bytes 1376264 | tf_op jit(solution)/shard_map/ppermute | solution.py:37
  121.6 24.6 %collective-permute-start.20 = (bf16[64,3584]{1,0:T(8,128)(2,1)S(1)}, bf16[64,3584]{1,0:T(8,128)(2,1)S(1)}, u32[]{:S(2)}, u32[]{:S(2)}) collective-permute-start(bf16[64,3584]{1,0:T(8,128)(2,1)S(1)} %shard_map.124.refs_4_), channel_id=1, source_target_pairs={{0,1},{1,2},{2,3},{3,4},{4,5},{5,6},{6,7},{7,0},{8,9},{9,10},{10,1... | collective-permute-start | bytes 1376264 | tf_op jit(solution)/shard_map/ppermute | solution.py:37
  146.4 19.5 %collective-permute-start.24 = (bf16[64,3584]{1,0:T(8,128)(2,1)S(1)}, bf16[64,3584]{1,0:T(8,128)(2,1)S(1)}, u32[]{:S(2)}, u32[]{:S(2)}) collective-permute-start(bf16[64,3584]{1,0:T(8,128)(2,1)S(1)} %get-tuple-element.57.refs_4_), channel_id=1, source_target_pairs={{0,1},{1,2},{2,3},{3,4},{4,5},{5,6},{6,7},{7,0},{8,9},{9,10},{10,1... | collective-permute-start | bytes 1376264 | tf_op jit(solution)/shard_map/ppermute | solution.py:37
  148.5 17.4 %collective-permute-start.25 = (bf16[64,3584]{1,0:T(8,128)(2,1)S(1)}, bf16[64,3584]{1,0:T(8,128)(2,1)S(1)}, u32[]{:S(2)}, u32[]{:S(2)}) collective-permute-start(bf16[64,3584]{1,0:T(8,128)(2,1)S(1)} %get-tuple-element.61), channel_id=1, source_target_pairs={{0,7},{1,0},{2,1},{3,2},{4,3},{5,4},{6,5},{7,6},{8,15},{9,8},{10,9... | collective-permute-start | bytes 1376264 | tf_op jit(solution)/shard_map/ppermute | solution.py:37
  156.3 24.3 %collective-permute-start.23 = (bf16[64,3584]{1,0:T(8,128)(2,1)S(1)}, bf16[64,3584]{1,0:T(8,128)(2,1)S(1)}, u32[]{:S(2)}, u32[]{:S(2)}) collective-permute-start(bf16[64,3584]{1,0:T(8,128)(2,1)S(1)} %get-tuple-element.59.refs_4_), channel_id=1, source_target_pairs={{0,7},{1,0},{2,1},{3,2},{4,3},{5,4},{6,5},{7,6},{8,15},{9,8},{10,9... | collective-permute-start | bytes 1376264 | tf_op jit(solution)/shard_map/ppermute | solution.py:37
  166.1 22.2 %collective-permute-start.27 = (bf16[64,3584]{1,0:T(8,128)(2,1)S(1)}, bf16[64,3584]{1,0:T(8,128)(2,1)S(1)}, u32[]{:S(2)}, u32[]{:S(2)}) collective-permute-start(bf16[64,3584]{1,0:T(8,128)(2,1)S(1)} %get-tuple-element.62.refs_2_), channel_id=1, source_target_pairs={{0,1},{1,2},{2,3},{3,4},{4,5},{5,6},{6,7},{7,0},{8,9},{9,10},{10,1... | collective-permute-start | bytes 1376264 | tf_op jit(solution)/shard_map/ppermute | solution.py:37
  168.1 23.4 %collective-permute-start.22 = (bf16[64,3584]{1,0:T(8,128)(2,1)S(1)}, bf16[64,3584]{1,0:T(8,128)(2,1)S(1)}, u32[]{:S(2)}, u32[]{:S(2)}) collective-permute-start(bf16[64,3584]{1,0:T(8,128)(2,1)S(1)} %get-tuple-element.58), channel_id=1, source_target_pairs={{0,33},{1,34},{2,35},{3,36},{4,37},{5,38},{6,39},{7,32},{32,65},{3... | collective-permute-start | bytes 1376264 | tf_op jit(solution)/shard_map/ppermute | solution.py:47
  178.6 17.7 %collective-permute-start.29 = (bf16[64,3584]{1,0:T(8,128)(2,1)S(1)}, bf16[64,3584]{1,0:T(8,128)(2,1)S(1)}, u32[]{:S(2)}, u32[]{:S(2)}) collective-permute-start(bf16[64,3584]{1,0:T(8,128)(2,1)S(1)} %get-tuple-element.63), channel_id=1, source_target_pairs={{0,487},{1,480},{2,481},{3,482},{4,483},{5,484},{6,485},{7,486},{3... | collective-permute-start | bytes 1376264 | tf_op jit(solution)/shard_map/ppermute | solution.py:47
  180.7 21.7 %collective-permute-start.26 = (bf16[64,3584]{1,0:T(8,128)(2,1)S(1)}, bf16[64,3584]{1,0:T(8,128)(2,1)S(1)}, u32[]{:S(2)}, u32[]{:S(2)}) collective-permute-start(bf16[64,3584]{1,0:T(8,128)(2,1)S(1)} %shard_map.129.refs_2_), channel_id=1, source_target_pairs={{0,39},{1,32},{2,33},{3,34},{4,35},{5,36},{6,37},{7,38},{32,71},{3... | collective-permute-start | bytes 1376264 | tf_op jit(solution)/shard_map/ppermute | solution.py:47
  (24 other events, 235.6 us)

commit v3 on v2

v3 whole, which is shorter than its diff:
```python
import functools

import jax
import jax.numpy as jnp
from jax import lax
from jax.experimental import pallas as pl
from jax.experimental.pallas import tpu as pltpu
from jax.sharding import Mesh, PartitionSpec as P

EXPERTS = 4
VMEM_BYTES = 48 * 1024 * 1024


def vmem_spec():
    return pl.BlockSpec(memory_space=pltpu.VMEM)


def call(kernel, out_shape, arguments, flops=0, moved=0, after=(), plain=0):
    specs = [pl.BlockSpec()] * plain + [vmem_spec()] * (len(arguments) - plain)
    specs += [pl.BlockSpec(memory_space=pl.ANY)] * len(after)
    used = len(arguments)

    def ordered(*refs):
        kernel(*refs[:used], *refs[used + len(after) :])

    return pl.pallas_call(
        ordered,
        out_shape=out_shape,
        in_specs=specs,
        out_specs=jax.tree.map(lambda _: vmem_spec(), out_shape),
        compiler_params=pltpu.CompilerParams(vmem_limit_bytes=VMEM_BYTES),
        cost_estimate=pl.CostEstimate(flops=flops, bytes_accessed=moved, transcendentals=0),
    )(*arguments, *after)


def shifted(array, axis, by):
    peers = lax.axis_size(axis)
    return lax.ppermute(array, axis, [(i, (i + by) % peers) for i in range(peers)])


def as_column(row):
    count = row.shape[1]
    place = lax.broadcasted_iota(jnp.int32, (count, count), 0)
    other = lax.broadcasted_iota(jnp.int32, (count, count), 1)
    return jnp.sum(jnp.where(place == other, row, jnp.zeros_like(row)), axis=1, keepdims=True)


def slots(routes, blocks, per_block):
    count = routes.shape[1]
    place = lax.broadcasted_iota(jnp.int32, (count, count), 0)
    other = lax.broadcasted_iota(jnp.int32, (count, count), 1)
    earlier = (as_column(routes) == routes) & (place < other)
    rank = jnp.sum(earlier.astype(jnp.int32), axis=0, keepdims=True)
    return place == blocks * per_block + rank


def prepare_kernel(states, routes, gain, buffer):
    count = states.shape[0]
    values = states[...].astype(jnp.float32)
    mean_square = jnp.mean(values * values, axis=-1, keepdims=True)
    normed = (values * lax.rsqrt(mean_square + 1e-06) * gain[...]).astype(jnp.bfloat16)
    placing = slots(routes[...], routes[...], count // EXPERTS).astype(jnp.bfloat16)
    buffer[...] = jnp.dot(placing, normed, preferred_element_type=jnp.float32).astype(jnp.bfloat16)


def prepare(states, routes, gain, after):
    rows, width = states.shape
    return call(
        prepare_kernel,
        jax.ShapeDtypeStruct((rows, width), jnp.bfloat16),
        (states, routes, gain),
        flops=2 * rows * rows * width,
        moved=4 * rows * width,
        after=after,
    )


def experts(blocks, gate_cols, up_cols, passed=0, after=()):
    number = len(blocks)
    width = gate_cols.shape[1]
    depth = gate_cols.shape[0]
    step = depth // 7

    def kernel(*refs):
        gate_ref, up_ref = refs[number : number + 2]
        outs = refs[number + 2 :]
        rows = [ref[...] for ref in refs[:number]]
        rows = rows[0] if number == 1 else jnp.concatenate(rows, axis=0)
        total = jnp.zeros((rows.shape[0], 2 * width), jnp.float32)
        for k in range(0, depth, step):
            both = jnp.concatenate([gate_ref[k : k + step, :], up_ref[k : k + step, :]], axis=1)
            total += jnp.dot(rows[:, k : k + step], both, preferred_element_type=jnp.float32)
        gate_part, up_part = total[:, :width], total[:, width:]
        hidden = (gate_part * jax.nn.sigmoid(gate_part) * up_part).astype(jnp.bfloat16)
        first = 0
        for out in outs[:number]:
            out[...] = hidden[first : first + out.shape[0]]
            first += out.shape[0]
        for block, out in zip(refs, outs[number:]):
            out[...] = block[...]

    row_count = sum(block.shape[0] for block in blocks)
    shapes = [jax.ShapeDtypeStruct((block.shape[0], width), jnp.bfloat16) for block in blocks]
    shapes += [jax.ShapeDtypeStruct(block.shape, jnp.bfloat16) for block in blocks[:passed]]
    return call(
        kernel,
        tuple(shapes),
        (*blocks, gate_cols, up_cols),
        flops=4 * row_count * gate_cols.size,
        moved=4 * gate_cols.size + 4 * sum(block.size for block in blocks),
        after=after,
    )


def down(hiddens, rows_of, kind, after=()):
    number = len(hiddens)
    count = hiddens[0][0].shape[0]
    width = rows_of[0].shape[1]
    step = width // 7

    def kernel(*refs):
        *refs, out = refs
        left = [ref[first : first + count, :] for ref, (_, first) in zip(refs, hiddens)]
        left = left[0] if number == 1 else jnp.concatenate(left, axis=1)
        for k in range(0, width, step):
            right = [ref[:, k : k + step] for ref in refs[number:]]
            right = right[0] if number == 1 else jnp.concatenate(right, axis=0)
            part = jnp.dot(left, right, preferred_element_type=jnp.float32)
            out[:, k : k + step] = part.astype(kind)

    return call(
        kernel,
        jax.ShapeDtypeStruct((count, width), kind),
        (*[hidden for hidden, _ in hiddens], *rows_of),
        flops=2 * number * count * rows_of[0].size,
        moved=2 * number * rows_of[0].size + 4 * count * width,
        after=after,
    )


def finish_kernel(*refs):
    *refs, out = refs
    count = refs[0].shape[0]
    slot_count = count // EXPERTS
    for m in range(2):
        own, from_left, from_right = refs[3 * m : 3 * m + 3]
        total = own[...].astype(jnp.float32) + from_left[...].astype(jnp.float32)
        total = (total + from_right[...].astype(jnp.float32)).astype(jnp.bfloat16)
        for e in range(EXPERTS):
            start = (2 * e + m) * slot_count
            out[start : start + slot_count, :] = total[e * slot_count : (e + 1) * slot_count]


def finish(own, sums):
    rows, width = own[0].shape
    arguments = []
    for m in range(2):
        arguments += [own[m], sums[m][1], sums[m][-1]]
    return call(
        finish_kernel,
        jax.ShapeDtypeStruct((2 * rows, width), jnp.bfloat16),
        arguments,
        flops=4 * rows * width,
        moved=16 * rows * width,
    )


def combine_kernel(m, states, routes, gates, rows, out):
    count = out.shape[0]
    slot_count = count // EXPERTS
    placing = slots(routes[...], routes[...], slot_count).astype(jnp.bfloat16)
    starts = [(2 * e + m) * slot_count for e in range(EXPERTS)]
    returned = jnp.concatenate([rows[s : s + slot_count, :] for s in starts], axis=0)
    picked = lax.dot_general(
        placing, returned, (((0,), (0,)), ((), ())), preferred_element_type=jnp.float32
    )
    mixed = states[...].astype(jnp.float32) + as_column(gates[...]) * picked
    out[...] = mixed.astype(jnp.bfloat16)


def combine(m, states, routes, gates, rows, after):
    return call(
        functools.partial(combine_kernel, m),
        jax.ShapeDtypeStruct(states.shape, jnp.bfloat16),
        (states, routes, gates, rows),
        flops=2 * states.shape[0] * states.size,
        moved=8 * states.size,
        after=after,
    )


def body(
    x_forward,
    x_backward,
    norm_gain,
    w_gate,
    w_up,
    w_down,
    routes_forward,
    routes_backward,
    gates_forward,
    gates_backward,
):
    weights = (w_gate[0], w_up[0])
    down_here = w_down[0]
    ring = lax.axis_size("z")
    far = ring // 2
    states = (x_forward[0], x_backward[0])
    routes = (routes_forward.reshape(1, -1), routes_backward.reshape(1, -1))
    gates = (gates_forward.reshape(1, -1), gates_backward.reshape(1, -1))
    travel = (1, -1)

    here, last = [], ()
    for m in range(2):
        buffer = prepare(states[m], routes[m], norm_gain, last)
        here.append(lax.all_to_all(buffer, "x", split_axis=0, concat_axis=0, tiled=True))
        last = (here[m],)

    down_from = {way: shifted(down_here, "z", way) for way in (1, -1)}

    hidden = [{}, {}]
    own = experts(here, *weights, after=(down_from[1], down_from[-1]))
    last = (own[0],)
    for m in range(2):
        hidden[m][0] = own[m]
    moving = [{way: here[m] for way in (1, -1)} for m in range(2)]
    for step in range(1, far + 1):
        for m in range(2):
            ways = [way for way in (travel[m], -travel[m]) if step < far or way == travel[m]]
            for way in ways:
                moving[m][way] = shifted(moving[m][way], "z", way)
            goes_on = [way for way in ways if step + 1 < far or (step < far and way == travel[m])]
            results = experts(
                [moving[m][way] for way in ways], *weights, passed=len(goes_on), after=last
            )
            last = (results[0],)
            for way, part in zip(ways, results):
                hidden[m][-way * step] = part
            for way, block in zip(goes_on, results[len(ways) :]):
                moving[m][way] = block

    count = here[0].shape[0]
    ahead, behind = [], []
    for m, t in enumerate(travel):
        ahead.append(
            shifted(
                jnp.concatenate([hidden[m][k * t] for k in (3, -2, 1)], axis=0), "z", t
            )
        )
    for m, t in enumerate(travel):
        behind.append(
            shifted(jnp.concatenate([hidden[m][k * t] for k in (-4, -1)], axis=0), "z", -t)
        )
    sums = [{}, {}]
    for m, t in enumerate(travel):
        part = down(
            [(hidden[m][2 * t], 0), (ahead[m], 0)], [down_here, down_from[t]], jnp.bfloat16, last
        )
        last = (part,)
        sums[m][1] = shifted(part, "z", 2 * t)
    rows_of = [(down_here, down_from[t], down_from[-t]) for t in travel]
    for m, t in enumerate(travel):
        parts = [(hidden[m][-3 * t], 0), (ahead[m], count), (behind[m], 0)]
        part = down(parts, rows_of[m], jnp.bfloat16, last)
        last = (part,)
        sums[m][-1] = shifted(part, "z", -3 * t)
    own = []
    for m, t in enumerate(travel):
        parts = [(hidden[m][0], 0), (ahead[m], 2 * count), (behind[m], count)]
        own.append(down(parts, rows_of[m], jnp.float32, last))
        last = (own[m],)

    total = finish(own, sums)
    returned = lax.all_to_all(total, "x", split_axis=0, concat_axis=0, tiled=True)
    done, last = [], ()
    for m in range(2):
        result = combine(m, states[m], routes[m], gates[m], returned, last)
        done.append(shifted(result, "pipe", travel[m])[None])
        last = (result,)
    return (done[0], done[1])


def solution(mesh):
    sections, members = mesh.devices.shape
    inner = Mesh(
        mesh.devices.reshape(sections, EXPERTS, members // EXPERTS), ("pipe", "x", "z")
    )
    tokens = P("pipe", ("x", "z"), None)
    placed = (
        tokens,
        tokens,
        P("pipe", None),
        P("pipe", None, ("x", "z")),
        P("pipe", None, ("x", "z")),
        tokens,
        tokens,
        tokens,
        tokens,
        tokens,
    )
    return jax.shard_map(
        body, mesh=inner, in_specs=placed, out_specs=(tokens, tokens), check_vma=False
    )
```

time: 224 us -> 205 us (0.915)
  starting transfers between devices: 114 us -> 93.5 us
  waiting for transfers between devices: 53.3 us -> 66 us
  blocking collectives: 26 us -> 14.5 us
    ppermute x4 -> x0, starting transfers between devices: 22 us -> none  [shifted_twice(): return lax.ppermute(array, ('pipe', 'z'), pairs)]
    ppermute x26, waiting for transfers between devices: 41.3 us -> 59.3 us  [shifted(): lax.ppermute(array, axis, [(i, (i + by) % peers) for i in range(peers)])]
    ppermute x4 -> x0, waiting for transfers between devices: 12 us -> none  [shifted_twice(): return lax.ppermute(array, ('pipe', 'z'), pairs)]
    all_to_all x1 -> x0, blocking collectives: 11.5 us -> none  [body(): lax.all_to_all(buffer, 'x', split_axis=0, concat_axis=0, tiled=True)]
    all_to_all x1 -> x2, waiting for transfers between devices: 0.01 us -> 6.69 us  [body(): lax.all_to_all(buffer, 'x', split_axis=0, concat_axis=0, tiled=True)]
    all_to_all x1 -> x2, starting transfers between devices: 4.14 us -> 8.26 us  [body(): lax.all_to_all(buffer, 'x', split_axis=0, concat_axis=0, tiled=True)]
    ppermute x26, starting transfers between devices: 88.1 us -> 85.3 us  [shifted(): lax.ppermute(array, axis, [(i, (i + by) % peers) for i in range(peers)])]
    unnamed x34 -> x30, local copies, waits for them, and re-layouts: 6.09 us -> 7.71 us
  transfers between devices with their start and end apart: 31 -> 28, of which waited for: 11 -> 12; matrix products, arithmetic and copies ran while one was open for 0% -> 0% of each run, Pallas kernels for 7% -> 9%
where the time goes in v3:
time: 205 us; the launch traced here: 203 us
  starting transfers between devices  93.5 us (46%)
  waiting for transfers between devices  66 us (32%)
  Pallas kernels  20.3 us (10%)
  blocking collectives  14.5 us (7%)
  local copies, waits for them, and re-layouts  7.71 us (4%)
    ppermute x26, starting transfers between devices, shifted(): lax.ppermute(array, axis, [(i, (i + by) % peers) for i in range(peers)])  85.3 us
    ppermute x26, waiting for transfers between devices, shifted(): lax.ppermute(array, axis, [(i, (i + by) % peers) for i in range(peers)])  59.3 us
    pallas_call x20, Pallas kernels, call(): pl.pallas_call(ordered, out_shape=out_shape, in_specs=specs, out_specs=ja...  20.3 us
    all_to_all x1, blocking collectives, body(): lax.all_to_all(total, 'x', split_axis=0, concat_axis=0, tiled=True)  14.5 us
    all_to_all x2, starting transfers between devices, body(): lax.all_to_all(buffer, 'x', split_axis=0, concat_axis=0, tiled=True)  8.26 us
    unnamed x30, local copies, waits for them, and re-layouts  7.71 us
    all_to_all x2, waiting for transfers between devices, body(): lax.all_to_all(buffer, 'x', split_axis=0, concat_axis=0, tiled=True)  6.69 us
  transfers between devices with their start and end apart: 28, of which 12 were waited for; matrix products, arithmetic and copies ran while one was open for 0% of the time, Pallas kernels for 9%

profile of v3, /device:TPU:25, one launch (start us, length us, event | category | flops | bytes accessed | tf_op | source)
XLA Modules:
  0.0 203.2 jit_solution(10128939780270836228)
XLA Ops:
  0.6 10.7 %collective-permute-start.1 = (bf16[128,3584]{1,0:T(8,128)(2,1)}, bf16[128,3584]{1,0:T(8,128)(2,1)}, u32[]{:S(2)}, u32[]{:S(2)}) collective-permute-start(bf16[128,3584]{1,0:T(8,128)(2,1)} %bitcast.35), channel_id=1, source_target_pairs={{0,7},{1,0},{2,1},{3,2},{4,3},{5,4},{6,5},{7,6},{8,15},{9,8},{10,9... | collective-permute-start | bytes 2752520 | tf_op jit(solution)/shard_map/ppermute | solution.py:38
  14.9 4.1 %all-to-all-start = ((bf16[4,16,3584]{2,1,0:T(8,128)(2,1)}), bf16[4,16,3584]{2,1,0:T(8,128)(2,1)S(1)}, u32[]{:S(2)}, u32[]{:S(2)}) async-start(bf16[4,16,3584]{2,1,0:T(8,128)(2,1)} %bitcast.3), calls=%async_computation | async-start | bytes 917504 | tf_op jit(solution)/shard_map/all_to_all | solution.py:216
  21.0 5.4 %all-to-all-done = bf16[4,16,3584]{2,1,0:T(8,128)(2,1)S(1)} async-done(((bf16[4,16,3584]{2,1,0:T(8,128)(2,1)}), bf16[4,16,3584]{2,1,0:T(8,128)(2,1)S(1)}, u32[]{:S(2)}, u32[]{:S(2)}) %all-to-all-start) | async-done | bytes 458784 | tf_op jit(solution)/shard_map/all_to_all | solution.py:216
  29.3 4.1 %all-to-all-start.1 = ((bf16[4,16,3584]{2,1,0:T(8,128)(2,1)}), bf16[4,16,3584]{2,1,0:T(8,128)(2,1)}, u32[]{:S(2)}, u32[]{:S(2)}) async-start(bf16[4,16,3584]{2,1,0:T(8,128)(2,1)} %bitcast.52), calls=%async_computation.1 | async-start | bytes 917504 | tf_op jit(solution)/shard_map/all_to_all | solution.py:216
  35.6 3.1 %collective-permute-start.2 = (bf16[64,3584]{1,0:T(8,128)(2,1)S(1)}, bf16[64,3584]{1,0:T(8,128)(2,1)}, u32[]{:S(2)}, u32[]{:S(2)}) collective-permute-start(bf16[64,3584]{1,0:T(8,128)(2,1)S(1)} %bitcast.47), channel_id=1, source_target_pairs={{0,1},{1,2},{2,3},{3,4},{4,5},{5,6},{6,7},{7,0},{8,9},{9,10},{10,1... | collective-permute-start | bytes 1376264 | tf_op jit(solution)/shard_map/ppermute | solution.py:38
  42.0 4.6 %collective-permute-start.6 = (bf16[64,3584]{1,0:T(8,128)(2,1)}, bf16[64,3584]{1,0:T(8,128)(2,1)S(1)}, u32[]{:S(2)}, u32[]{:S(2)}) collective-permute-start(bf16[64,3584]{1,0:T(8,128)(2,1)} %bitcast.8.refs_1_), channel_id=1, source_target_pairs={{0,7},{1,0},{2,1},{3,2},{4,3},{5,4},{6,5},{7,6},{8,15},{9,8},{10,9... | collective-permute-start | bytes 1376264 | tf_op jit(solution)/shard_map/ppermute | solution.py:38
  48.0 4.7 %collective-permute-done.2.refs_0_ = bf16[64,3584]{1,0:T(8,128)(2,1)} collective-permute-done((bf16[64,3584]{1,0:T(8,128)(2,1)S(1)}, bf16[64,3584]{1,0:T(8,128)(2,1)}, u32[]{:S(2)}, u32[]{:S(2)}) %collective-permute-start.2) | collective-permute-done | bytes 458784 | tf_op jit(solution)/shard_map/ppermute | solution.py:38
  56.3 4.6 %collective-permute-start.5 = (bf16[64,3584]{1,0:T(8,128)(2,1)S(1)}, bf16[64,3584]{1,0:T(8,128)(2,1)S(1)}, u32[]{:S(2)}, u32[]{:S(2)}) collective-permute-start(bf16[64,3584]{1,0:T(8,128)(2,1)S(1)} %get-tuple-element.28), channel_id=1, source_target_pairs={{0,7},{1,0},{2,1},{3,2},{4,3},{5,4},{6,5},{7,6},{8,15},{9,8},{10,9... | collective-permute-start | bytes 1376264 | tf_op jit(solution)/shard_map/ppermute | solution.py:38
  64.8 3.4 %collective-permute-start.11 = (bf16[64,3584]{1,0:T(8,128)(2,1)S(1)}, bf16[64,3584]{1,0:T(8,128)(2,1)S(1)}, u32[]{:S(2)}, u32[]{:S(2)}) collective-permute-start(bf16[64,3584]{1,0:T(8,128)(2,1)S(1)} %get-tuple-element.34), channel_id=1, source_target_pairs={{0,1},{1,2},{2,3},{3,4},{4,5},{5,6},{6,7},{7,0},{8,9},{9,10},{10,1... | collective-permute-start | bytes 1376264 | tf_op jit(solution)/shard_map/ppermute | solution.py:38
  68.2 4.1 %collective-permute-done.4.refs_0_ = bf16[64,3584]{1,0:T(8,128)(2,1)S(1)} collective-permute-done((bf16[64,3584]{1,0:T(8,128)(2,1)S(1)}, bf16[64,3584]{1,0:T(8,128)(2,1)S(1)}, u32[]{:S(2)}, u32[]{:S(2)}) %collective-permute-start.4) | collective-permute-done | bytes 458784 | tf_op jit(solution)/shard_map/ppermute | solution.py:38
  74.6 4.6 %collective-permute-start.9 = (bf16[64,3584]{1,0:T(8,128)(2,1)S(1)}, bf16[64,3584]{1,0:T(8,128)(2,1)S(1)}, u32[]{:S(2)}, u32[]{:S(2)}) collective-permute-start(bf16[64,3584]{1,0:T(8,128)(2,1)S(1)} %get-tuple-element.32), channel_id=1, source_target_pairs={{0,7},{1,0},{2,1},{3,2},{4,3},{5,4},{6,5},{7,6},{8,15},{9,8},{10,9... | collective-permute-start | bytes 1376264 | tf_op jit(solution)/shard_map/ppermute | solution.py:38
  79.2 2.9 %collective-permute-done.11.refs_1_ = bf16[64,3584]{1,0:T(8,128)(2,1)S(1)} collective-permute-done((bf16[64,3584]{1,0:T(8,128)(2,1)S(1)}, bf16[64,3584]{1,0:T(8,128)(2,1)S(1)}, u32[]{:S(2)}, u32[]{:S(2)}) %collective-permute-start.11) | collective-permute-done | bytes 458784 | tf_op jit(solution)/shard_map/ppermute | solution.py:38
  84.4 3.4 %collective-permute-start.15 = (bf16[64,3584]{1,0:T(8,128)(2,1)S(1)}, bf16[64,3584]{1,0:T(8,128)(2,1)S(1)}, u32[]{:S(2)}, u32[]{:S(2)}) collective-permute-start(bf16[64,3584]{1,0:T(8,128)(2,1)S(1)} %get-tuple-element.41), channel_id=1, source_target_pairs={{0,1},{1,2},{2,3},{3,4},{4,5},{5,6},{6,7},{7,0},{8,9},{9,10},{10,1... | collective-permute-start | bytes 1376264 | tf_op jit(solution)/shard_map/ppermute | solution.py:38
  87.8 4.1 %collective-permute-done.8.refs_0_ = bf16[64,3584]{1,0:T(8,128)(2,1)S(1)} collective-permute-done((bf16[64,3584]{1,0:T(8,128)(2,1)S(1)}, bf16[64,3584]{1,0:T(8,128)(2,1)S(1)}, u32[]{:S(2)}, u32[]{:S(2)}) %collective-permute-start.8) | collective-permute-done | bytes 458784 | tf_op jit(solution)/shard_map/ppermute | solution.py:38
  97.0 4.8 %collective-permute-done.15.refs_1_ = bf16[64,3584]{1,0:T(8,128)(2,1)S(1)} collective-permute-done((bf16[64,3584]{1,0:T(8,128)(2,1)S(1)}, bf16[64,3584]{1,0:T(8,128)(2,1)S(1)}, u32[]{:S(2)}, u32[]{:S(2)}) %collective-permute-start.15) | collective-permute-done | bytes 458784 | tf_op jit(solution)/shard_map/ppermute | solution.py:38
  104.1 3.4 %collective-permute-start.12 = (bf16[192,128]{1,0:T(8,128)(2,1)S(1)}, bf16[192,128]{1,0:T(8,128)(2,1)S(1)}, u32[]{:S(2)}, u32[]{:S(2)}) collective-permute-start(bf16[192,128]{1,0:T(8,128)(2,1)S(1)} %pad_maximum_fusion), channel_id=1, source_target_pairs={{0,1},{1,2},{2,3},{3,4},{4,5},{5,6},{6,7},{7,0},{8,9},{9,10},{10,1... | collective-permute-start | bytes 147464 | tf_op jit(solution)/shard_map/ppermute | solution.py:38
  107.5 3.1 %collective-permute-start.17 = (bf16[192,128]{1,0:T(8,128)(2,1)S(1)}, bf16[192,128]{1,0:T(8,128)(2,1)S(1)}, u32[]{:S(2)}, u32[]{:S(2)}) collective-permute-start(bf16[192,128]{1,0:T(8,128)(2,1)S(1)} %pad_maximum_fusion.1), channel_id=1, source_target_pairs={{0,7},{1,0},{2,1},{3,2},{4,3},{5,4},{6,5},{7,6},{8,15},{9,8},{10,9... | collective-permute-start | bytes 147464 | tf_op jit(solution)/shard_map/ppermute | solution.py:38
  114.5 3.4 %collective-permute-start.19 = (bf16[128,128]{1,0:T(8,128)(2,1)S(1)}, bf16[128,128]{1,0:T(8,128)(2,1)S(1)}, u32[]{:S(2)}, u32[]{:S(2)}) collective-permute-start(bf16[128,128]{1,0:T(8,128)(2,1)S(1)} %pad_maximum_fusion.3), channel_id=1, source_target_pairs={{0,1},{1,2},{2,3},{3,4},{4,5},{5,6},{6,7},{7,0},{8,9},{9,10},{10,1... | collective-permute-start | bytes 98312 | tf_op jit(solution)/shard_map/ppermute | solution.py:38
  123.0 5.5 %collective-permute-start.22 = (bf16[64,3584]{1,0:T(8,128)(2,1)S(1)}, bf16[64,3584]{1,0:T(8,128)(2,1)S(1)}, u32[]{:S(2)}, u32[]{:S(2)}) collective-permute-start(bf16[64,3584]{1,0:T(8,128)(2,1)S(1)} %shard_map.125.refs_6_), channel_id=1, source_target_pairs={{0,6},{1,7},{2,0},{3,1},{4,2},{5,3},{6,4},{7,5},{8,14},{9,15},{10,... | collective-permute-start | bytes 1376264 | tf_op jit(solution)/shard_map/ppermute | solution.py:38
  134.6 5.2 %collective-permute-start.23 = (bf16[64,3584]{1,0:T(8,128)(2,1)S(1)}, bf16[64,3584]{1,0:T(8,128)(2,1)S(1)}, u32[]{:S(2)}, u32[]{:S(2)}) collective-permute-start(bf16[64,3584]{1,0:T(8,128)(2,1)S(1)} %shard_map.127.refs_6_), channel_id=1, source_target_pairs={{0,3},{1,4},{2,5},{3,6},{4,7},{5,0},{6,1},{7,2},{8,11},{9,12},{10,... | collective-permute-start | bytes 1376264 | tf_op jit(solution)/shard_map/ppermute | solution.py:38
  143.9 27.4 %collective-permute-done.21.refs_2_ = bf16[64,3584]{1,0:T(8,128)(2,1)S(1)} collective-permute-done((bf16[64,3584]{1,0:T(8,128)(2,1)S(1)}, bf16[64,3584]{1,0:T(8,128)(2,1)S(1)}, u32[]{:S(2)}, u32[]{:S(2)}) %collective-permute-start.21) | collective-permute-done | bytes 458784 | tf_op jit(solution)/shard_map/ppermute | solution.py:38
  171.5 14.5 %all_to_all.33 = bf16[4,32,3584]{2,1,0:T(8,128)(2,1)S(1)} all-to-all(bf16[4,32,3584]{2,1,0:T(8,128)(2,1)S(1)} %bitcast.49), channel_id=1, replica_groups=mesh['pipe'=16,'x'=4,'z'=8] {'x'}, dimensions={0} | all-to-all | bytes 1835008 | tf_op jit(solution)/shard_map/all_to_all | solution.py:274
  188.2 4.9 %collective-permute-start.25 = (bf16[64,3584]{1,0:T(8,128)(2,1)S(1)}, bf16[64,3584]{1,0:T(8,128)(2,1)S(1)}, u32[]{:S(2)}, u32[]{:S(2)}) collective-permute-start(bf16[64,3584]{1,0:T(8,128)(2,1)S(1)} %shard_map.132), channel_id=1, source_target_pairs={{0,480},{32,0},{64,32},{96,64},{128,96},{160,128},{192,160},{224,1... | collective-permute-start | bytes 1376264 | tf_op jit(solution)/shard_map/ppermute | solution.py:38
  195.5 6.1 %collective-permute-done.25 = bf16[64,3584]{1,0:T(8,128)(2,1)S(1)} collective-permute-done((bf16[64,3584]{1,0:T(8,128)(2,1)S(1)}, bf16[64,3584]{1,0:T(8,128)(2,1)S(1)}, u32[]{:S(2)}, u32[]{:S(2)}) %collective-permute-start.25) | collective-permute-done | bytes 458784 | tf_op jit(solution)/shard_map/ppermute | solution.py:38
  (87 shorter events, 60.3 us)
Async XLA Ops:
  0.6 41.3 %collective-permute-start.1 = (bf16[128,3584]{1,0:T(8,128)(2,1)}, bf16[128,3584]{1,0:T(8,128)(2,1)}, u32[]{:S(2)}, u32[]{:S(2)}) collective-permute-start(bf16[128,3584]{1,0:T(8,128)(2,1)} %bitcast.35), channel_id=1, source_target_pairs={{0,7},{1,0},{2,1},{3,2},{4,3},{5,4},{6,5},{7,6},{8,15},{9,8},{10,9... | collective-permute-start | bytes 2752520 | tf_op jit(solution)/shard_map/ppermute | solution.py:38
  19.1 27.5 %collective-permute-start = (bf16[128,3584]{1,0:T(8,128)(2,1)S(1)}, bf16[128,3584]{1,0:T(8,128)(2,1)}, u32[]{:S(2)}, u32[]{:S(2)}) collective-permute-start(bf16[128,3584]{1,0:T(8,128)(2,1)S(1)} %bitcast.36), channel_id=1, source_target_pairs={{0,1},{1,2},{2,3},{3,4},{4,5},{5,6},{6,7},{7,0},{8,9},{9,10},{10,1... | collective-permute-start | bytes 2752520 | tf_op jit(solution)/shard_map/ppermute | solution.py:38
  33.4 14.6 %collective-permute-start.3 = (bf16[64,3584]{1,0:T(8,128)(2,1)S(1)}, bf16[64,3584]{1,0:T(8,128)(2,1)}, u32[]{:S(2)}, u32[]{:S(2)}) collective-permute-start(bf16[64,3584]{1,0:T(8,128)(2,1)S(1)} %bitcast.46), channel_id=1, source_target_pairs={{0,7},{1,0},{2,1},{3,2},{4,3},{5,4},{6,5},{7,6},{8,15},{9,8},{10,9... | collective-permute-start | bytes 1376264 | tf_op jit(solution)/shard_map/ppermute | solution.py:38
  35.6 17.1 %collective-permute-start.2 = (bf16[64,3584]{1,0:T(8,128)(2,1)S(1)}, bf16[64,3584]{1,0:T(8,128)(2,1)}, u32[]{:S(2)}, u32[]{:S(2)}) collective-permute-start(bf16[64,3584]{1,0:T(8,128)(2,1)S(1)} %bitcast.47), channel_id=1, source_target_pairs={{0,1},{1,2},{2,3},{3,4},{4,5},{5,6},{6,7},{7,0},{8,9},{9,10},{10,1... | collective-permute-start | bytes 1376264 | tf_op jit(solution)/shard_map/ppermute | solution.py:38
  40.0 22.4 %collective-permute-start.7 = (bf16[64,3584]{1,0:T(8,128)(2,1)}, bf16[64,3584]{1,0:T(8,128)(2,1)S(1)}, u32[]{:S(2)}, u32[]{:S(2)}) collective-permute-start(bf16[64,3584]{1,0:T(8,128)(2,1)} %bitcast.8.refs_1_), channel_id=1, source_target_pairs={{0,1},{1,2},{2,3},{3,4},{4,5},{5,6},{6,7},{7,0},{8,9},{9,10},{10,1... | collective-permute-start | bytes 1376264 | tf_op jit(solution)/shard_map/ppermute | solution.py:38
  42.0 20.5 %collective-permute-start.6 = (bf16[64,3584]{1,0:T(8,128)(2,1)}, bf16[64,3584]{1,0:T(8,128)(2,1)S(1)}, u32[]{:S(2)}, u32[]{:S(2)}) collective-permute-start(bf16[64,3584]{1,0:T(8,128)(2,1)} %bitcast.8.refs_1_), channel_id=1, source_target_pairs={{0,7},{1,0},{2,1},{3,2},{4,3},{5,4},{6,5},{7,6},{8,15},{9,8},{10,9... | collective-permute-start | bytes 1376264 | tf_op jit(solution)/shard_map/ppermute | solution.py:38
  54.3 17.9 %collective-permute-start.4 = (bf16[64,3584]{1,0:T(8,128)(2,1)S(1)}, bf16[64,3584]{1,0:T(8,128)(2,1)S(1)}, u32[]{:S(2)}, u32[]{:S(2)}) collective-permute-start(bf16[64,3584]{1,0:T(8,128)(2,1)S(1)} %get-tuple-element.27), channel_id=1, source_target_pairs={{0,1},{1,2},{2,3},{3,4},{4,5},{5,6},{6,7},{7,0},{8,9},{9,10},{10,1... | collective-permute-start | bytes 1376264 | tf_op jit(solution)/shard_map/ppermute | solution.py:38
  56.3 16.0 %collective-permute-start.5 = (bf16[64,3584]{1,0:T(8,128)(2,1)S(1)}, bf16[64,3584]{1,0:T(8,128)(2,1)S(1)}, u32[]{:S(2)}, u32[]{:S(2)}) collective-permute-start(bf16[64,3584]{1,0:T(8,128)(2,1)S(1)} %get-tuple-element.28), channel_id=1, source_target_pairs={{0,7},{1,0},{2,1},{3,2},{4,3},{5,4},{6,5},{7,6},{8,15},{9,8},{10,9... | collective-permute-start | bytes 1376264 | tf_op jit(solution)/shard_map/ppermute | solution.py:38
  62.9 16.3 %collective-permute-start.10 = (bf16[64,3584]{1,0:T(8,128)(2,1)S(1)}, bf16[64,3584]{1,0:T(8,128)(2,1)S(1)}, u32[]{:S(2)}, u32[]{:S(2)}) collective-permute-start(bf16[64,3584]{1,0:T(8,128)(2,1)S(1)} %get-tuple-element.33), channel_id=1, source_target_pairs={{0,7},{1,0},{2,1},{3,2},{4,3},{5,4},{6,5},{7,6},{8,15},{9,8},{10,9... | collective-permute-start | bytes 1376264 | tf_op jit(solution)/shard_map/ppermute | solution.py:38
  64.8 17.3 %collective-permute-start.11 = (bf16[64,3584]{1,0:T(8,128)(2,1)S(1)}, bf16[64,3584]{1,0:T(8,128)(2,1)S(1)}, u32[]{:S(2)}, u32[]{:S(2)}) collective-permute-start(bf16[64,3584]{1,0:T(8,128)(2,1)S(1)} %get-tuple-element.34), channel_id=1, source_target_pairs={{0,1},{1,2},{2,3},{3,4},{4,5},{5,6},{6,7},{7,0},{8,9},{9,10},{10,1... | collective-permute-start | bytes 1376264 | tf_op jit(solution)/shard_map/ppermute | solution.py:38
  72.7 19.2 %collective-permute-start.8 = (bf16[64,3584]{1,0:T(8,128)(2,1)S(1)}, bf16[64,3584]{1,0:T(8,128)(2,1)S(1)}, u32[]{:S(2)}, u32[]{:S(2)}) collective-permute-start(bf16[64,3584]{1,0:T(8,128)(2,1)S(1)} %get-tuple-element.31), channel_id=1, source_target_pairs={{0,1},{1,2},{2,3},{3,4},{4,5},{5,6},{6,7},{7,0},{8,9},{9,10},{10,1... | collective-permute-start | bytes 1376264 | tf_op jit(solution)/shard_map/ppermute | solution.py:38
  74.6 17.3 %collective-permute-start.9 = (bf16[64,3584]{1,0:T(8,128)(2,1)S(1)}, bf16[64,3584]{1,0:T(8,128)(2,1)S(1)}, u32[]{:S(2)}, u32[]{:S(2)}) collective-permute-start(bf16[64,3584]{1,0:T(8,128)(2,1)S(1)} %get-tuple-element.32), channel_id=1, source_target_pairs={{0,7},{1,0},{2,1},{3,2},{4,3},{5,4},{6,5},{7,6},{8,15},{9,8},{10,9... | collective-permute-start | bytes 1376264 | tf_op jit(solution)/shard_map/ppermute | solution.py:38
  82.5 14.4 %collective-permute-start.14 = (bf16[64,3584]{1,0:T(8,128)(2,1)S(1)}, bf16[64,3584]{1,0:T(8,128)(2,1)S(1)}, u32[]{:S(2)}, u32[]{:S(2)}) collective-permute-start(bf16[64,3584]{1,0:T(8,128)(2,1)S(1)} %get-tuple-element.40), channel_id=1, source_target_pairs={{0,7},{1,0},{2,1},{3,2},{4,3},{5,4},{6,5},{7,6},{8,15},{9,8},{10,9... | collective-permute-start | bytes 1376264 | tf_op jit(solution)/shard_map/ppermute | solution.py:38
  84.4 17.3 %collective-permute-start.15 = (bf16[64,3584]{1,0:T(8,128)(2,1)S(1)}, bf16[64,3584]{1,0:T(8,128)(2,1)S(1)}, u32[]{:S(2)}, u32[]{:S(2)}) collective-permute-start(bf16[64,3584]{1,0:T(8,128)(2,1)S(1)} %get-tuple-element.41), channel_id=1, source_target_pairs={{0,1},{1,2},{2,3},{3,4},{4,5},{5,6},{6,7},{7,0},{8,9},{9,10},{10,1... | collective-permute-start | bytes 1376264 | tf_op jit(solution)/shard_map/ppermute | solution.py:38
  92.4 19.2 %collective-permute-start.13 = (bf16[64,3584]{1,0:T(8,128)(2,1)S(1)}, bf16[64,3584]{1,0:T(8,128)(2,1)S(1)}, u32[]{:S(2)}, u32[]{:S(2)}) collective-permute-start(bf16[64,3584]{1,0:T(8,128)(2,1)S(1)} %get-tuple-element.39), channel_id=1, source_target_pairs={{0,1},{1,2},{2,3},{3,4},{4,5},{5,6},{6,7},{7,0},{8,9},{9,10},{10,1... | collective-permute-start | bytes 1376264 | tf_op jit(solution)/shard_map/ppermute | solution.py:38
  104.1 13.7 %collective-permute-start.12 = (bf16[192,128]{1,0:T(8,128)(2,1)S(1)}, bf16[192,128]{1,0:T(8,128)(2,1)S(1)}, u32[]{:S(2)}, u32[]{:S(2)}) collective-permute-start(bf16[192,128]{1,0:T(8,128)(2,1)S(1)} %pad_maximum_fusion), channel_id=1, source_target_pairs={{0,1},{1,2},{2,3},{3,4},{4,5},{5,6},{6,7},{7,0},{8,9},{9,10},{10,1... | collective-permute-start | bytes 147464 | tf_op jit(solution)/shard_map/ppermute | solution.py:38
  107.5 13.9 %collective-permute-start.17 = (bf16[192,128]{1,0:T(8,128)(2,1)S(1)}, bf16[192,128]{1,0:T(8,128)(2,1)S(1)}, u32[]{:S(2)}, u32[]{:S(2)}) collective-permute-start(bf16[192,128]{1,0:T(8,128)(2,1)S(1)} %pad_maximum_fusion.1), channel_id=1, source_target_pairs={{0,7},{1,0},{2,1},{3,2},{4,3},{5,4},{6,5},{7,6},{8,15},{9,8},{10,9... | collective-permute-start | bytes 147464 | tf_op jit(solution)/shard_map/ppermute | solution.py:38
  112.1 16.4 %collective-permute-start.16 = (bf16[128,128]{1,0:T(8,128)(2,1)S(1)}, bf16[128,128]{1,0:T(8,128)(2,1)S(1)}, u32[]{:S(2)}, u32[]{:S(2)}) collective-permute-start(bf16[128,128]{1,0:T(8,128)(2,1)S(1)} %pad_maximum_fusion.2), channel_id=1, source_target_pairs={{0,7},{1,0},{2,1},{3,2},{4,3},{5,4},{6,5},{7,6},{8,15},{9,8},{10,9... | collective-permute-start | bytes 98312 | tf_op jit(solution)/shard_map/ppermute | solution.py:38
  114.5 18.0 %collective-permute-start.19 = (bf16[128,128]{1,0:T(8,128)(2,1)S(1)}, bf16[128,128]{1,0:T(8,128)(2,1)S(1)}, u32[]{:S(2)}, u32[]{:S(2)}) collective-permute-start(bf16[128,128]{1,0:T(8,128)(2,1)S(1)} %pad_maximum_fusion.3), channel_id=1, source_target_pairs={{0,1},{1,2},{2,3},{3,4},{4,5},{5,6},{6,7},{7,0},{8,9},{9,10},{10,1... | collective-permute-start | bytes 98312 | tf_op jit(solution)/shard_map/ppermute | solution.py:38
  119.5 51.8 %collective-permute-start.20 = (bf16[64,3584]{1,0:T(8,128)(2,1)S(1)}, bf16[64,3584]{1,0:T(8,128)(2,1)S(1)}, u32[]{:S(2)}, u32[]{:S(2)}) collective-permute-start(bf16[64,3584]{1,0:T(8,128)(2,1)S(1)} %shard_map.124.refs_4_), channel_id=1, source_target_pairs={{0,2},{1,3},{2,4},{3,5},{4,6},{5,7},{6,0},{7,1},{8,10},{9,11},{10,... | collective-permute-start | bytes 1376264 | tf_op jit(solution)/shard_map/ppermute | solution.py:38
  123.0 48.2 %collective-permute-start.22 = (bf16[64,3584]{1,0:T(8,128)(2,1)S(1)}, bf16[64,3584]{1,0:T(8,128)(2,1)S(1)}, u32[]{:S(2)}, u32[]{:S(2)}) collective-permute-start(bf16[64,3584]{1,0:T(8,128)(2,1)S(1)} %shard_map.125.refs_6_), channel_id=1, source_target_pairs={{0,6},{1,7},{2,0},{3,1},{4,2},{5,3},{6,4},{7,5},{8,14},{9,15},{10,... | collective-permute-start | bytes 1376264 | tf_op jit(solution)/shard_map/ppermute | solution.py:38
  130.6 40.7 %collective-permute-start.21 = (bf16[64,3584]{1,0:T(8,128)(2,1)S(1)}, bf16[64,3584]{1,0:T(8,128)(2,1)S(1)}, u32[]{:S(2)}, u32[]{:S(2)}) collective-permute-start(bf16[64,3584]{1,0:T(8,128)(2,1)S(1)} %shard_map.126.refs_6_), channel_id=1, source_target_pairs={{0,5},{1,6},{2,7},{3,0},{4,1},{5,2},{6,3},{7,4},{8,13},{9,14},{10,... | collective-permute-start | bytes 1376264 | tf_op jit(solution)/shard_map/ppermute | solution.py:38
  134.6 36.7 %collective-permute-start.23 = (bf16[64,3584]{1,0:T(8,128)(2,1)S(1)}, bf16[64,3584]{1,0:T(8,128)(2,1)S(1)}, u32[]{:S(2)}, u32[]{:S(2)}) collective-permute-start(bf16[64,3584]{1,0:T(8,128)(2,1)S(1)} %shard_map.127.refs_6_), channel_id=1, source_target_pairs={{0,3},{1,4},{2,5},{3,6},{4,7},{5,0},{6,1},{7,2},{8,11},{9,12},{10,... | collective-permute-start | bytes 1376264 | tf_op jit(solution)/shard_map/ppermute | solution.py:38
  188.2 13.4 %collective-permute-start.25 = (bf16[64,3584]{1,0:T(8,128)(2,1)S(1)}, bf16[64,3584]{1,0:T(8,128)(2,1)S(1)}, u32[]{:S(2)}, u32[]{:S(2)}) collective-permute-start(bf16[64,3584]{1,0:T(8,128)(2,1)S(1)} %shard_map.132), channel_id=1, source_target_pairs={{0,480},{32,0},{64,32},{96,64},{128,96},{160,128},{192,160},{224,1... | collective-permute-start | bytes 1376264 | tf_op jit(solution)/shard_map/ppermute | solution.py:38
  (18 other events, 118.1 us)

commit v4 on v3

--- a/solution.py
+++ b/solution.py
@@ -54,23 +54,64 @@
     return place == blocks * per_block + rank
 
 
-def prepare_kernel(states, routes, gain, buffer):
-    count = states.shape[0]
-    values = states[...].astype(jnp.float32)
-    mean_square = jnp.mean(values * values, axis=-1, keepdims=True)
-    normed = (values * lax.rsqrt(mean_square + 1e-06) * gain[...]).astype(jnp.bfloat16)
-    placing = slots(routes[...], routes[...], count // EXPERTS).astype(jnp.bfloat16)
-    buffer[...] = jnp.dot(placing, normed, preferred_element_type=jnp.float32).astype(jnp.bfloat16)
-
-
-def prepare(states, routes, gain, after):
-    rows, width = states.shape
-    return call(
+def prepare_kernel(*refs):
+    sources, (buffer, *held), arrived = refs[:5], refs[5:11], refs[11]
+    copies = [
+        pltpu.make_async_copy(source, place, arrived.at[i])
+        for i, (source, place) in enumerate(zip(sources, held))
+    ]
+    for copy in copies:
+        copy.start()
+    for copy in copies:
+        copy.wait()
+    gain, *pairs = held
+    count = pairs[0].shape[0]
+    slot_count = count // EXPERTS
+    for m in range(2):
+        states, routes = pairs[m], pairs[2 + m]
+        values = states[...].astype(jnp.float32)
+        mean_square = jnp.mean(values * values, axis=-1, keepdims=True)
+        normed = (values * lax.rsqrt(mean_square + 1e-06) * gain[...]).astype(jnp.bfloat16)
+        placing = slots(routes[...], routes[...], slot_count).astype(jnp.bfloat16)
+        placed = jnp.dot(placing, normed, preferred_element_type=jnp.float32)
+        placed = placed.astype(jnp.bfloat16)
+        for e in range(EXPERTS):
+            start = (e * 2 + m) * slot_count
+            buffer[start : start + slot_count, :] = placed[e * slot_count : (e + 1) * slot_count]
+
+
+def prepare(states, routes, gain):
+    rows, width = states[0].shape
+    arguments = (gain, *states, *routes)
+    return pl.pallas_call(
         prepare_kernel,
-        jax.ShapeDtypeStruct((rows, width), jnp.bfloat16),
-        (states, routes, gain),
-        flops=2 * rows * rows * width,
-        moved=4 * rows * width,
+        out_shape=jax.ShapeDtypeStruct((2 * rows, width), jnp.bfloat16),
+        in_specs=[pl.BlockSpec(memory_space=pl.ANY)] * 5,
+        out_specs=vmem_spec(),
+        scratch_shapes=[pltpu.VMEM(array.shape, array.dtype) for array in arguments]
+        + [pltpu.SemaphoreType.DMA((5,))],
+        compiler_params=pltpu.CompilerParams(vmem_limit_bytes=VMEM_BYTES),
+        cost_estimate=pl.CostEstimate(
+            flops=4 * rows * rows * width, bytes_accessed=8 * rows * width, transcendentals=0
+        ),
+    )(*arguments)
+
+
+def parted_kernel(gathered, *outs):
+    slot_count = outs[0].shape[0] // EXPERTS
+    for m, out in enumerate(outs):
+        for e in range(EXPERTS):
+            start = (2 * e + m) * slot_count
+            out[e * slot_count : (e + 1) * slot_count, :] = gathered[start : start + slot_count, :]
+
+
+def parted(gathered, after):
+    rows, width = gathered.shape
+    return call(
+        parted_kernel,
+        (jax.ShapeDtypeStruct((rows // 2, width), jnp.bfloat16),) * 2,
+        (gathered,),
+        moved=4 * gathered.size,
         after=after,
     )
 
@@ -210,13 +251,12 @@
     gates = (gates_forward.reshape(1, -1), gates_backward.reshape(1, -1))
     travel = (1, -1)
 
-    here, last = [], ()
-    for m in range(2):
-        buffer = prepare(states[m], routes[m], norm_gain, last)
-        here.append(lax.all_to_all(buffer, "x", split_axis=0, concat_axis=0, tiled=True))
-        last = (here[m],)
-
     down_from = {way: shifted(down_here, "z", way) for way in (1, -1)}
+
+    gathered = lax.all_to_all(
+        prepare(states, routes, norm_gain), "x", split_axis=0, concat_axis=0, tiled=True
+    )
+    here = parted(gathered, (down_from[1], down_from[-1]))
 
     hidden = [{}, {}]
     own = experts(here, *weights, after=(down_from[1], down_from[-1]))

time: 205 us -> 202 us (0.985)
  blocking collectives: 14.5 us -> 34.1 us
  Pallas kernels: 20.3 us -> 9.51 us
  waiting for transfers between devices: 66 us -> 61 us
  starting transfers between devices: 93.5 us -> 89.4 us
    all_to_all x0 -> x1, blocking collectives: none -> 16 us  [body(): lax.all_to_all(prepare(states, routes, norm_gain), 'x', split_axis=0, con...]
    pallas_call x20 -> x19, Pallas kernels: 20.3 us -> 8.26 us  [call(): pl.pallas_call(ordered, out_shape=out_shape, in_specs=specs, out_specs=ja...]
    all_to_all x2 -> x0, starting transfers between devices: 8.26 us -> none  [body(): lax.all_to_all(buffer, 'x', split_axis=0, concat_axis=0, tiled=True)]
    all_to_all x2 -> x0, waiting for transfers between devices: 6.69 us -> none  [body(): lax.all_to_all(buffer, 'x', split_axis=0, concat_axis=0, tiled=True)]
    ppermute x26, starting transfers between devices: 85.3 us -> 89.4 us  [shifted(): lax.ppermute(array, axis, [(i, (i + by) % peers) for i in range(peers)])]
    all_to_all x1, blocking collectives: 14.5 us -> 18.1 us  [body(): lax.all_to_all(total, 'x', split_axis=0, concat_axis=0, tiled=True)]
    unnamed x30 -> x26, local copies, waits for them, and re-layouts: 7.71 us -> 6.3 us
  transfers between devices with their start and end apart: 28 -> 26, of which waited for: 12 -> 14; matrix products, arithmetic and copies ran while one was open for 0% -> 0% of each run, Pallas kernels for 9% -> 4%
where the time goes in v4:
time: 202 us; the launch traced here: 201 us
  starting transfers between devices  89.4 us (44%)
  waiting for transfers between devices  61 us (30%)
  blocking collectives  34.1 us (17%)
  Pallas kernels  9.51 us (5%)
  local copies, waits for them, and re-layouts  6.3 us (3%)
    ppermute x26, starting transfers between devices, shifted(): lax.ppermute(array, axis, [(i, (i + by) % peers) for i in range(peers)])  89.4 us
    ppermute x26, waiting for transfers between devices, shifted(): lax.ppermute(array, axis, [(i, (i + by) % peers) for i in range(peers)])  61 us
    all_to_all x1, blocking collectives, body(): lax.all_to_all(total, 'x', split_axis=0, concat_axis=0, tiled=True)  18.1 us
    all_to_all x1, blocking collectives, body(): lax.all_to_all(prepare(states, routes, norm_gain), 'x', split_axis=0, con...  16 us
    pallas_call x19, Pallas kernels, call(): pl.pallas_call(ordered, out_shape=out_shape, in_specs=specs, out_specs=ja...  8.26 us
    unnamed x26, local copies, waits for them, and re-layouts  6.3 us
  transfers between devices with their start and end apart: 26, of which 14 were waited for; matrix products, arithmetic and copies ran while one was open for 0% of the time, Pallas kernels for 4%

profile of v4, /device:TPU:25, one launch (start us, length us, event | category | flops | bytes accessed | tf_op | source)
XLA Modules:
  0.0 201.4 jit_solution(5068121408773976651)
XLA Ops:
  0.6 10.7 %collective-permute-start.1 = (bf16[128,3584]{1,0:T(8,128)(2,1)}, bf16[128,3584]{1,0:T(8,128)(2,1)S(1)}, u32[]{:S(2)}, u32[]{:S(2)}) collective-permute-start(bf16[128,3584]{1,0:T(8,128)(2,1)} %bitcast.33), channel_id=1, source_target_pairs={{0,7},{1,0},{2,1},{3,2},{4,3},{5,4},{6,5},{7,6},{8,15},{9,8},{10,9... | collective-permute-start | bytes 2752520 | tf_op jit(solution)/shard_map/ppermute | solution.py:38
  17.9 16.0 %all_to_all.22 = bf16[4,32,3584]{2,1,0:T(8,128)(2,1)S(1)} all-to-all(bf16[4,32,3584]{2,1,0:T(8,128)(2,1)S(1)} %bitcast.43), channel_id=1, replica_groups=mesh['pipe'=16,'x'=4,'z'=8] {'x'}, dimensions={0} | all-to-all | bytes 1835008 | tf_op jit(solution)/shard_map/all_to_all | solution.py:256
  35.6 3.0 %collective-permute-start.3 = (bf16[64,3584]{1,0:T(8,128)(2,1)S(1)}, bf16[64,3584]{1,0:T(8,128)(2,1)S(1)}, u32[]{:S(2)}, u32[]{:S(2)}) collective-permute-start(bf16[64,3584]{1,0:T(8,128)(2,1)S(1)} %get-tuple-element.28.refs_0_), channel_id=1, source_target_pairs={{0,7},{1,0},{2,1},{3,2},{4,3},{5,4},{6,5},{7,6},{8,15},{9,8},{10,9... | collective-permute-start | bytes 1376264 | tf_op jit(solution)/shard_map/ppermute | solution.py:38
  43.0 4.6 %collective-permute-start.6 = (bf16[64,3584]{1,0:T(8,128)(2,1)S(1)}, bf16[64,3584]{1,0:T(8,128)(2,1)S(1)}, u32[]{:S(2)}, u32[]{:S(2)}) collective-permute-start(bf16[64,3584]{1,0:T(8,128)(2,1)S(1)} %get-tuple-element.29.refs_1_), channel_id=1, source_target_pairs={{0,7},{1,0},{2,1},{3,2},{4,3},{5,4},{6,5},{7,6},{8,15},{9,8},{10,9... | collective-permute-start | bytes 1376264 | tf_op jit(solution)/shard_map/ppermute | solution.py:38
  48.0 2.9 %collective-permute-done.2.refs_0_ = bf16[64,3584]{1,0:T(8,128)(2,1)S(1)} collective-permute-done((bf16[64,3584]{1,0:T(8,128)(2,1)S(1)}, bf16[64,3584]{1,0:T(8,128)(2,1)S(1)}, u32[]{:S(2)}, u32[]{:S(2)}) %collective-permute-start.2) | collective-permute-done | bytes 458784 | tf_op jit(solution)/shard_map/ppermute | solution.py:38
  53.2 4.6 %collective-permute-start.5 = (bf16[64,3584]{1,0:T(8,128)(2,1)S(1)}, bf16[64,3584]{1,0:T(8,128)(2,1)S(1)}, u32[]{:S(2)}, u32[]{:S(2)}) collective-permute-start(bf16[64,3584]{1,0:T(8,128)(2,1)S(1)} %get-tuple-element.32), channel_id=1, source_target_pairs={{0,7},{1,0},{2,1},{3,2},{4,3},{5,4},{6,5},{7,6},{8,15},{9,8},{10,9... | collective-permute-start | bytes 1376264 | tf_op jit(solution)/shard_map/ppermute | solution.py:38
  57.8 2.9 %collective-permute-done.7.refs_1_ = bf16[64,3584]{1,0:T(8,128)(2,1)S(1)} collective-permute-done((bf16[64,3584]{1,0:T(8,128)(2,1)S(1)}, bf16[64,3584]{1,0:T(8,128)(2,1)S(1)}, u32[]{:S(2)}, u32[]{:S(2)}) %collective-permute-start.7) | collective-permute-done | bytes 458784 | tf_op jit(solution)/shard_map/ppermute | solution.py:38
  63.1 3.4 %collective-permute-start.11 = (bf16[64,3584]{1,0:T(8,128)(2,1)S(1)}, bf16[64,3584]{1,0:T(8,128)(2,1)S(1)}, u32[]{:S(2)}, u32[]{:S(2)}) collective-permute-start(bf16[64,3584]{1,0:T(8,128)(2,1)S(1)} %get-tuple-element.38), channel_id=1, source_target_pairs={{0,1},{1,2},{2,3},{3,4},{4,5},{5,6},{6,7},{7,0},{8,9},{9,10},{10,1... | collective-permute-start | bytes 1376264 | tf_op jit(solution)/shard_map/ppermute | solution.py:38
  66.4 4.1 %collective-permute-done.4.refs_0_ = bf16[64,3584]{1,0:T(8,128)(2,1)S(1)} collective-permute-done((bf16[64,3584]{1,0:T(8,128)(2,1)S(1)}, bf16[64,3584]{1,0:T(8,128)(2,1)S(1)}, u32[]{:S(2)}, u32[]{:S(2)}) %collective-permute-start.4) | collective-permute-done | bytes 458784 | tf_op jit(solution)/shard_map/ppermute | solution.py:38
  72.9 4.6 %collective-permute-start.9 = (bf16[64,3584]{1,0:T(8,128)(2,1)S(1)}, bf16[64,3584]{1,0:T(8,128)(2,1)S(1)}, u32[]{:S(2)}, u32[]{:S(2)}) collective-permute-start(bf16[64,3584]{1,0:T(8,128)(2,1)S(1)} %get-tuple-element.36), channel_id=1, source_target_pairs={{0,7},{1,0},{2,1},{3,2},{4,3},{5,4},{6,5},{7,6},{8,15},{9,8},{10,9... | collective-permute-start | bytes 1376264 | tf_op jit(solution)/shard_map/ppermute | solution.py:38
  77.5 2.9 %collective-permute-done.11.refs_1_ = bf16[64,3584]{1,0:T(8,128)(2,1)S(1)} collective-permute-done((bf16[64,3584]{1,0:T(8,128)(2,1)S(1)}, bf16[64,3584]{1,0:T(8,128)(2,1)S(1)}, u32[]{:S(2)}, u32[]{:S(2)}) %collective-permute-start.11) | collective-permute-done | bytes 458784 | tf_op jit(solution)/shard_map/ppermute | solution.py:38
  82.7 3.4 %collective-permute-start.15 = (bf16[64,3584]{1,0:T(8,128)(2,1)S(1)}, bf16[64,3584]{1,0:T(8,128)(2,1)S(1)}, u32[]{:S(2)}, u32[]{:S(2)}) collective-permute-start(bf16[64,3584]{1,0:T(8,128)(2,1)S(1)} %get-tuple-element.45), channel_id=1, source_target_pairs={{0,1},{1,2},{2,3},{3,4},{4,5},{5,6},{6,7},{7,0},{8,9},{9,10},{10,1... | collective-permute-start | bytes 1376264 | tf_op jit(solution)/shard_map/ppermute | solution.py:38
  86.1 4.1 %collective-permute-done.8.refs_0_ = bf16[64,3584]{1,0:T(8,128)(2,1)S(1)} collective-permute-done((bf16[64,3584]{1,0:T(8,128)(2,1)S(1)}, bf16[64,3584]{1,0:T(8,128)(2,1)S(1)}, u32[]{:S(2)}, u32[]{:S(2)}) %collective-permute-start.8) | collective-permute-done | bytes 458784 | tf_op jit(solution)/shard_map/ppermute | solution.py:38
  92.5 2.7 %collective-permute-done.14.refs_0_ = bf16[64,3584]{1,0:T(8,128)(2,1)S(1)} collective-permute-done((bf16[64,3584]{1,0:T(8,128)(2,1)S(1)}, bf16[64,3584]{1,0:T(8,128)(2,1)S(1)}, u32[]{:S(2)}, u32[]{:S(2)}) %collective-permute-start.14) | collective-permute-done | bytes 458784 | tf_op jit(solution)/shard_map/ppermute | solution.py:38
  95.2 4.8 %collective-permute-done.15.refs_1_ = bf16[64,3584]{1,0:T(8,128)(2,1)S(1)} collective-permute-done((bf16[64,3584]{1,0:T(8,128)(2,1)S(1)}, bf16[64,3584]{1,0:T(8,128)(2,1)S(1)}, u32[]{:S(2)}, u32[]{:S(2)}) %collective-permute-start.15) | collective-permute-done | bytes 458784 | tf_op jit(solution)/shard_map/ppermute | solution.py:38
  102.4 3.4 %collective-permute-start.12 = (bf16[192,128]{1,0:T(8,128)(2,1)S(1)}, bf16[192,128]{1,0:T(8,128)(2,1)S(1)}, u32[]{:S(2)}, u32[]{:S(2)}) collective-permute-start(bf16[192,128]{1,0:T(8,128)(2,1)S(1)} %pad_maximum_fusion), channel_id=1, source_target_pairs={{0,1},{1,2},{2,3},{3,4},{4,5},{5,6},{6,7},{7,0},{8,9},{9,10},{10,1... | collective-permute-start | bytes 147464 | tf_op jit(solution)/shard_map/ppermute | solution.py:38
  105.8 3.1 %collective-permute-start.17 = (bf16[192,128]{1,0:T(8,128)(2,1)S(1)}, bf16[192,128]{1,0:T(8,128)(2,1)S(1)}, u32[]{:S(2)}, u32[]{:S(2)}) collective-permute-start(bf16[192,128]{1,0:T(8,128)(2,1)S(1)} %pad_maximum_fusion.1), channel_id=1, source_target_pairs={{0,7},{1,0},{2,1},{3,2},{4,3},{5,4},{6,5},{7,6},{8,15},{9,8},{10,9... | collective-permute-start | bytes 147464 | tf_op jit(solution)/shard_map/ppermute | solution.py:38
  112.9 3.4 %collective-permute-start.19 = (bf16[128,128]{1,0:T(8,128)(2,1)S(1)}, bf16[128,128]{1,0:T(8,128)(2,1)S(1)}, u32[]{:S(2)}, u32[]{:S(2)}) collective-permute-start(bf16[128,128]{1,0:T(8,128)(2,1)S(1)} %pad_maximum_fusion.3), channel_id=1, source_target_pairs={{0,1},{1,2},{2,3},{3,4},{4,5},{5,6},{6,7},{7,0},{8,9},{9,10},{10,1... | collective-permute-start | bytes 98312 | tf_op jit(solution)/shard_map/ppermute | solution.py:38
  119.1 5.5 %collective-permute-start.22 = (bf16[64,3584]{1,0:T(8,128)(2,1)S(1)}, bf16[64,3584]{1,0:T(8,128)(2,1)S(1)}, u32[]{:S(2)}, u32[]{:S(2)}) collective-permute-start(bf16[64,3584]{1,0:T(8,128)(2,1)S(1)} %shard_map.125.refs_6_), channel_id=1, source_target_pairs={{0,6},{1,7},{2,0},{3,1},{4,2},{5,3},{6,4},{7,5},{8,14},{9,15},{10,... | collective-permute-start | bytes 1376264 | tf_op jit(solution)/shard_map/ppermute | solution.py:38
  127.7 6.4 %collective-permute-start.21 = (bf16[64,3584]{1,0:T(8,128)(2,1)S(1)}, bf16[64,3584]{1,0:T(8,128)(2,1)S(1)}, u32[]{:S(2)}, u32[]{:S(2)}) collective-permute-start(bf16[64,3584]{1,0:T(8,128)(2,1)S(1)} %shard_map.126.refs_6_), channel_id=1, source_target_pairs={{0,5},{1,6},{2,7},{3,0},{4,1},{5,2},{6,3},{7,4},{8,13},{9,14},{10,... | collective-permute-start | bytes 1376264 | tf_op jit(solution)/shard_map/ppermute | solution.py:38
  137.2 24.7 %collective-permute-done.23.refs_5_ = bf16[64,3584]{1,0:T(8,128)(2,1)S(1)} collective-permute-done((bf16[64,3584]{1,0:T(8,128)(2,1)S(1)}, bf16[64,3584]{1,0:T(8,128)(2,1)S(1)}, u32[]{:S(2)}, u32[]{:S(2)}) %collective-permute-start.23) | collective-permute-done | bytes 458784 | tf_op jit(solution)/shard_map/ppermute | solution.py:38
  163.6 18.1 %all_to_all.23 = bf16[4,32,3584]{2,1,0:T(8,128)(2,1)S(1)} all-to-all(bf16[4,32,3584]{2,1,0:T(8,128)(2,1)S(1)} %bitcast.45), channel_id=1, replica_groups=mesh['pipe'=16,'x'=4,'z'=8] {'x'}, dimensions={0} | all-to-all | bytes 1835008 | tf_op jit(solution)/shard_map/all_to_all | solution.py:314
  183.9 7.5 %collective-permute-start.25 = (bf16[64,3584]{1,0:T(8,128)(2,1)S(1)}, bf16[64,3584]{1,0:T(8,128)(2,1)S(1)}, u32[]{:S(2)}, u32[]{:S(2)}) collective-permute-start(bf16[64,3584]{1,0:T(8,128)(2,1)S(1)} %shard_map.132), channel_id=1, source_target_pairs={{0,480},{32,0},{64,32},{96,64},{128,96},{160,128},{192,160},{224,1... | collective-permute-start | bytes 1376264 | tf_op jit(solution)/shard_map/ppermute | solution.py:38
  193.8 6.1 %collective-permute-done.25 = bf16[64,3584]{1,0:T(8,128)(2,1)S(1)} collective-permute-done((bf16[64,3584]{1,0:T(8,128)(2,1)S(1)}, bf16[64,3584]{1,0:T(8,128)(2,1)S(1)}, u32[]{:S(2)}, u32[]{:S(2)}) %collective-permute-start.25) | collective-permute-done | bytes 458784 | tf_op jit(solution)/shard_map/ppermute | solution.py:38
  (80 shorter events, 47.7 us)
Async XLA Ops:
  0.6 33.3 %collective-permute-start.1 = (bf16[128,3584]{1,0:T(8,128)(2,1)}, bf16[128,3584]{1,0:T(8,128)(2,1)S(1)}, u32[]{:S(2)}, u32[]{:S(2)}) collective-permute-start(bf16[128,3584]{1,0:T(8,128)(2,1)} %bitcast.33), channel_id=1, source_target_pairs={{0,7},{1,0},{2,1},{3,2},{4,3},{5,4},{6,5},{7,6},{8,15},{9,8},{10,9... | collective-permute-start | bytes 2752520 | tf_op jit(solution)/shard_map/ppermute | solution.py:38
  11.3 24.2 %collective-permute-start = (bf16[128,3584]{1,0:T(8,128)(2,1)}, bf16[128,3584]{1,0:T(8,128)(2,1)S(1)}, u32[]{:S(2)}, u32[]{:S(2)}) collective-permute-start(bf16[128,3584]{1,0:T(8,128)(2,1)} %bitcast.34), channel_id=1, source_target_pairs={{0,1},{1,2},{2,3},{3,4},{4,5},{5,6},{6,7},{7,0},{8,9},{9,10},{10,1... | collective-permute-start | bytes 2752520 | tf_op jit(solution)/shard_map/ppermute | solution.py:38
  35.6 12.4 %collective-permute-start.3 = (bf16[64,3584]{1,0:T(8,128)(2,1)S(1)}, bf16[64,3584]{1,0:T(8,128)(2,1)S(1)}, u32[]{:S(2)}, u32[]{:S(2)}) collective-permute-start(bf16[64,3584]{1,0:T(8,128)(2,1)S(1)} %get-tuple-element.28.refs_0_), channel_id=1, source_target_pairs={{0,7},{1,0},{2,1},{3,2},{4,3},{5,4},{6,5},{7,6},{8,15},{9,8},{10,9... | collective-permute-start | bytes 1376264 | tf_op jit(solution)/shard_map/ppermute | solution.py:38
  38.6 12.3 %collective-permute-start.2 = (bf16[64,3584]{1,0:T(8,128)(2,1)S(1)}, bf16[64,3584]{1,0:T(8,128)(2,1)S(1)}, u32[]{:S(2)}, u32[]{:S(2)}) collective-permute-start(bf16[64,3584]{1,0:T(8,128)(2,1)S(1)} %get-tuple-element.28.refs_0_), channel_id=1, source_target_pairs={{0,1},{1,2},{2,3},{3,4},{4,5},{5,6},{6,7},{7,0},{8,9},{9,10},{10,1... | collective-permute-start | bytes 1376264 | tf_op jit(solution)/shard_map/ppermute | solution.py:38
  41.0 19.7 %collective-permute-start.7 = (bf16[64,3584]{1,0:T(8,128)(2,1)S(1)}, bf16[64,3584]{1,0:T(8,128)(2,1)S(1)}, u32[]{:S(2)}, u32[]{:S(2)}) collective-permute-start(bf16[64,3584]{1,0:T(8,128)(2,1)S(1)} %get-tuple-element.29.refs_1_), channel_id=1, source_target_pairs={{0,1},{1,2},{2,3},{3,4},{4,5},{5,6},{6,7},{7,0},{8,9},{9,10},{10,1... | collective-permute-start | bytes 1376264 | tf_op jit(solution)/shard_map/ppermute | solution.py:38
  43.0 17.8 %collective-permute-start.6 = (bf16[64,3584]{1,0:T(8,128)(2,1)S(1)}, bf16[64,3584]{1,0:T(8,128)(2,1)S(1)}, u32[]{:S(2)}, u32[]{:S(2)}) collective-permute-start(bf16[64,3584]{1,0:T(8,128)(2,1)S(1)} %get-tuple-element.29.refs_1_), channel_id=1, source_target_pairs={{0,7},{1,0},{2,1},{3,2},{4,3},{5,4},{6,5},{7,6},{8,15},{9,8},{10,9... | collective-permute-start | bytes 1376264 | tf_op jit(solution)/shard_map/ppermute | solution.py:38
  51.3 19.2 %collective-permute-start.4 = (bf16[64,3584]{1,0:T(8,128)(2,1)S(1)}, bf16[64,3584]{1,0:T(8,128)(2,1)S(1)}, u32[]{:S(2)}, u32[]{:S(2)}) collective-permute-start(bf16[64,3584]{1,0:T(8,128)(2,1)S(1)} %get-tuple-element.31), channel_id=1, source_target_pairs={{0,1},{1,2},{2,3},{3,4},{4,5},{5,6},{6,7},{7,0},{8,9},{9,10},{10,1... | collective-permute-start | bytes 1376264 | tf_op jit(solution)/shard_map/ppermute | solution.py:38
  53.2 17.3 %collective-permute-start.5 = (bf16[64,3584]{1,0:T(8,128)(2,1)S(1)}, bf16[64,3584]{1,0:T(8,128)(2,1)S(1)}, u32[]{:S(2)}, u32[]{:S(2)}) collective-permute-start(bf16[64,3584]{1,0:T(8,128)(2,1)S(1)} %get-tuple-element.32), channel_id=1, source_target_pairs={{0,7},{1,0},{2,1},{3,2},{4,3},{5,4},{6,5},{7,6},{8,15},{9,8},{10,9... | collective-permute-start | bytes 1376264 | tf_op jit(solution)/shard_map/ppermute | solution.py:38
  61.1 16.3 %collective-permute-start.10 = (bf16[64,3584]{1,0:T(8,128)(2,1)S(1)}, bf16[64,3584]{1,0:T(8,128)(2,1)S(1)}, u32[]{:S(2)}, u32[]{:S(2)}) collective-permute-start(bf16[64,3584]{1,0:T(8,128)(2,1)S(1)} %get-tuple-element.37), channel_id=1, source_target_pairs={{0,7},{1,0},{2,1},{3,2},{4,3},{5,4},{6,5},{7,6},{8,15},{9,8},{10,9... | collective-permute-start | bytes 1376264 | tf_op jit(solution)/shard_map/ppermute | solution.py:38
  63.1 17.3 %collective-permute-start.11 = (bf16[64,3584]{1,0:T(8,128)(2,1)S(1)}, bf16[64,3584]{1,0:T(8,128)(2,1)S(1)}, u32[]{:S(2)}, u32[]{:S(2)}) collective-permute-start(bf16[64,3584]{1,0:T(8,128)(2,1)S(1)} %get-tuple-element.38), channel_id=1, source_target_pairs={{0,1},{1,2},{2,3},{3,4},{4,5},{5,6},{6,7},{7,0},{8,9},{9,10},{10,1... | collective-permute-start | bytes 1376264 | tf_op jit(solution)/shard_map/ppermute | solution.py:38
  71.0 19.2 %collective-permute-start.8 = (bf16[64,3584]{1,0:T(8,128)(2,1)S(1)}, bf16[64,3584]{1,0:T(8,128)(2,1)S(1)}, u32[]{:S(2)}, u32[]{:S(2)}) collective-permute-start(bf16[64,3584]{1,0:T(8,128)(2,1)S(1)} %get-tuple-element.35), channel_id=1, source_target_pairs={{0,1},{1,2},{2,3},{3,4},{4,5},{5,6},{6,7},{7,0},{8,9},{9,10},{10,1... | collective-permute-start | bytes 1376264 | tf_op jit(solution)/shard_map/ppermute | solution.py:38
  72.9 17.3 %collective-permute-start.9 = (bf16[64,3584]{1,0:T(8,128)(2,1)S(1)}, bf16[64,3584]{1,0:T(8,128)(2,1)S(1)}, u32[]{:S(2)}, u32[]{:S(2)}) collective-permute-start(bf16[64,3584]{1,0:T(8,128)(2,1)S(1)} %get-tuple-element.36), channel_id=1, source_target_pairs={{0,7},{1,0},{2,1},{3,2},{4,3},{5,4},{6,5},{7,6},{8,15},{9,8},{10,9... | collective-permute-start | bytes 1376264 | tf_op jit(solution)/shard_map/ppermute | solution.py:38
  80.8 14.4 %collective-permute-start.14 = (bf16[64,3584]{1,0:T(8,128)(2,1)S(1)}, bf16[64,3584]{1,0:T(8,128)(2,1)S(1)}, u32[]{:S(2)}, u32[]{:S(2)}) collective-permute-start(bf16[64,3584]{1,0:T(8,128)(2,1)S(1)} %get-tuple-element.44), channel_id=1, source_target_pairs={{0,7},{1,0},{2,1},{3,2},{4,3},{5,4},{6,5},{7,6},{8,15},{9,8},{10,9... | collective-permute-start | bytes 1376264 | tf_op jit(solution)/shard_map/ppermute | solution.py:38
  82.7 17.3 %collective-permute-start.15 = (bf16[64,3584]{1,0:T(8,128)(2,1)S(1)}, bf16[64,3584]{1,0:T(8,128)(2,1)S(1)}, u32[]{:S(2)}, u32[]{:S(2)}) collective-permute-start(bf16[64,3584]{1,0:T(8,128)(2,1)S(1)} %get-tuple-element.45), channel_id=1, source_target_pairs={{0,1},{1,2},{2,3},{3,4},{4,5},{5,6},{6,7},{7,0},{8,9},{9,10},{10,1... | collective-permute-start | bytes 1376264 | tf_op jit(solution)/shard_map/ppermute | solution.py:38
  90.6 19.2 %collective-permute-start.13 = (bf16[64,3584]{1,0:T(8,128)(2,1)S(1)}, bf16[64,3584]{1,0:T(8,128)(2,1)S(1)}, u32[]{:S(2)}, u32[]{:S(2)}) collective-permute-start(bf16[64,3584]{1,0:T(8,128)(2,1)S(1)} %get-tuple-element.43), channel_id=1, source_target_pairs={{0,1},{1,2},{2,3},{3,4},{4,5},{5,6},{6,7},{7,0},{8,9},{9,10},{10,1... | collective-permute-start | bytes 1376264 | tf_op jit(solution)/shard_map/ppermute | solution.py:38
  102.4 13.9 %collective-permute-start.12 = (bf16[192,128]{1,0:T(8,128)(2,1)S(1)}, bf16[192,128]{1,0:T(8,128)(2,1)S(1)}, u32[]{:S(2)}, u32[]{:S(2)}) collective-permute-start(bf16[192,128]{1,0:T(8,128)(2,1)S(1)} %pad_maximum_fusion), channel_id=1, source_target_pairs={{0,1},{1,2},{2,3},{3,4},{4,5},{5,6},{6,7},{7,0},{8,9},{9,10},{10,1... | collective-permute-start | bytes 147464 | tf_op jit(solution)/shard_map/ppermute | solution.py:38
  105.8 12.9 %collective-permute-start.17 = (bf16[192,128]{1,0:T(8,128)(2,1)S(1)}, bf16[192,128]{1,0:T(8,128)(2,1)S(1)}, u32[]{:S(2)}, u32[]{:S(2)}) collective-permute-start(bf16[192,128]{1,0:T(8,128)(2,1)S(1)} %pad_maximum_fusion.1), channel_id=1, source_target_pairs={{0,7},{1,0},{2,1},{3,2},{4,3},{5,4},{6,5},{7,6},{8,15},{9,8},{10,9... | collective-permute-start | bytes 147464 | tf_op jit(solution)/shard_map/ppermute | solution.py:38
  110.3 14.2 %collective-permute-start.16 = (bf16[128,128]{1,0:T(8,128)(2,1)S(1)}, bf16[128,128]{1,0:T(8,128)(2,1)S(1)}, u32[]{:S(2)}, u32[]{:S(2)}) collective-permute-start(bf16[128,128]{1,0:T(8,128)(2,1)S(1)} %pad_maximum_fusion.2), channel_id=1, source_target_pairs={{0,7},{1,0},{2,1},{3,2},{4,3},{5,4},{6,5},{7,6},{8,15},{9,8},{10,9... | collective-permute-start | bytes 98312 | tf_op jit(solution)/shard_map/ppermute | solution.py:38
  112.9 12.3 %collective-permute-start.19 = (bf16[128,128]{1,0:T(8,128)(2,1)S(1)}, bf16[128,128]{1,0:T(8,128)(2,1)S(1)}, u32[]{:S(2)}, u32[]{:S(2)}) collective-permute-start(bf16[128,128]{1,0:T(8,128)(2,1)S(1)} %pad_maximum_fusion.3), channel_id=1, source_target_pairs={{0,1},{1,2},{2,3},{3,4},{4,5},{5,6},{6,7},{7,0},{8,9},{9,10},{10,1... | collective-permute-start | bytes 98312 | tf_op jit(solution)/shard_map/ppermute | solution.py:38
  116.7 20.5 %collective-permute-start.20 = (bf16[64,3584]{1,0:T(8,128)(2,1)S(1)}, bf16[64,3584]{1,0:T(8,128)(2,1)S(1)}, u32[]{:S(2)}, u32[]{:S(2)}) collective-permute-start(bf16[64,3584]{1,0:T(8,128)(2,1)S(1)} %shard_map.124.refs_4_), channel_id=1, source_target_pairs={{0,2},{1,3},{2,4},{3,5},{4,6},{5,7},{6,0},{7,1},{8,10},{9,11},{10,... | collective-permute-start | bytes 1376264 | tf_op jit(solution)/shard_map/ppermute | solution.py:38
  119.1 17.0 %collective-permute-start.22 = (bf16[64,3584]{1,0:T(8,128)(2,1)S(1)}, bf16[64,3584]{1,0:T(8,128)(2,1)S(1)}, u32[]{:S(2)}, u32[]{:S(2)}) collective-permute-start(bf16[64,3584]{1,0:T(8,128)(2,1)S(1)} %shard_map.125.refs_6_), channel_id=1, source_target_pairs={{0,6},{1,7},{2,0},{3,1},{4,2},{5,3},{6,4},{7,5},{8,14},{9,15},{10,... | collective-permute-start | bytes 1376264 | tf_op jit(solution)/shard_map/ppermute | solution.py:38
  125.8 36.1 %collective-permute-start.23 = (bf16[64,3584]{1,0:T(8,128)(2,1)S(1)}, bf16[64,3584]{1,0:T(8,128)(2,1)S(1)}, u32[]{:S(2)}, u32[]{:S(2)}) collective-permute-start(bf16[64,3584]{1,0:T(8,128)(2,1)S(1)} %shard_map.127.refs_6_), channel_id=1, source_target_pairs={{0,3},{1,4},{2,5},{3,6},{4,7},{5,0},{6,1},{7,2},{8,11},{9,12},{10,... | collective-permute-start | bytes 1376264 | tf_op jit(solution)/shard_map/ppermute | solution.py:38
  127.7 35.5 %collective-permute-start.21 = (bf16[64,3584]{1,0:T(8,128)(2,1)S(1)}, bf16[64,3584]{1,0:T(8,128)(2,1)S(1)}, u32[]{:S(2)}, u32[]{:S(2)}) collective-permute-start(bf16[64,3584]{1,0:T(8,128)(2,1)S(1)} %shard_map.126.refs_6_), channel_id=1, source_target_pairs={{0,5},{1,6},{2,7},{3,0},{4,1},{5,2},{6,3},{7,4},{8,13},{9,14},{10,... | collective-permute-start | bytes 1376264 | tf_op jit(solution)/shard_map/ppermute | solution.py:38
  183.9 16.0 %collective-permute-start.25 = (bf16[64,3584]{1,0:T(8,128)(2,1)S(1)}, bf16[64,3584]{1,0:T(8,128)(2,1)S(1)}, u32[]{:S(2)}, u32[]{:S(2)}) collective-permute-start(bf16[64,3584]{1,0:T(8,128)(2,1)S(1)} %shard_map.132), channel_id=1, source_target_pairs={{0,480},{32,0},{64,32},{96,64},{128,96},{160,128},{192,160},{224,1... | collective-permute-start | bytes 1376264 | tf_op jit(solution)/shard_map/ppermute | solution.py:38
  (14 other events, 75.0 us)

commit v5 on v4

--- a/solution.py
+++ b/solution.py
@@ -1,5 +1,3 @@
-import functools
-
 import jax
 import jax.numpy as jnp
 from jax import lax
@@ -206,27 +204,29 @@
     )
 
 
-def combine_kernel(m, states, routes, gates, rows, out):
-    count = out.shape[0]
-    slot_count = count // EXPERTS
-    placing = slots(routes[...], routes[...], slot_count).astype(jnp.bfloat16)
-    starts = [(2 * e + m) * slot_count for e in range(EXPERTS)]
-    returned = jnp.concatenate([rows[s : s + slot_count, :] for s in starts], axis=0)
-    picked = lax.dot_general(
-        placing, returned, (((0,), (0,)), ((), ())), preferred_element_type=jnp.float32
-    )
-    mixed = states[...].astype(jnp.float32) + as_column(gates[...]) * picked
-    out[...] = mixed.astype(jnp.bfloat16)
-
-
-def combine(m, states, routes, gates, rows, after):
-    return call(
-        functools.partial(combine_kernel, m),
-        jax.ShapeDtypeStruct(states.shape, jnp.bfloat16),
-        (states, routes, gates, rows),
-        flops=2 * states.shape[0] * states.size,
-        moved=8 * states.size,
-        after=after,
+def combine_kernel(*refs):
+    rows, *outs = refs[6:]
+    for m, out in enumerate(outs):
+        states, routes, gates = refs[m], refs[2 + m], refs[4 + m]
+        count = out.shape[0]
+        slot_count = count // EXPERTS
+        placing = slots(routes[...], routes[...], slot_count).astype(jnp.bfloat16)
+        starts = [(2 * e + m) * slot_count for e in range(EXPERTS)]
+        returned = jnp.concatenate([rows[s : s + slot_count, :] for s in starts], axis=0)
+        picked = lax.dot_general(
+            placing, returned, (((0,), (0,)), ((), ())), preferred_element_type=jnp.float32
+        )
+        mixed = states[...].astype(jnp.float32) + as_column(gates[...]) * picked
+        out[...] = mixed.astype(jnp.bfloat16)
+
+
+def combine(states, routes, gates, rows):
+    return call(
+        combine_kernel,
+        tuple(jax.ShapeDtypeStruct(array.shape, jnp.bfloat16) for array in states),
+        (*states, *routes, *gates, rows),
+        flops=4 * states[0].shape[0] * states[0].size,
+        moved=16 * states[0].size,
     )
 
 
@@ -312,11 +312,8 @@
 
     total = finish(own, sums)
     returned = lax.all_to_all(total, "x", split_axis=0, concat_axis=0, tiled=True)
-    done, last = [], ()
-    for m in range(2):
-        result = combine(m, states[m], routes[m], gates[m], returned, last)
-        done.append(shifted(result, "pipe", travel[m])[None])
-        last = (result,)
+    results = combine(states, routes, gates, returned)
+    done = [shifted(result, "pipe", t)[None] for result, t in zip(results, travel)]
     return (done[0], done[1])
 
 

time: 202 us -> 204 us (level)
  waiting for transfers between devices: 61 us -> 64 us
    ppermute x26, waiting for transfers between devices: 61 us -> 64 us  [shifted(): lax.ppermute(array, axis, [(i, (i + by) % peers) for i in range(peers)])]
    pallas_call x19 -> x18, Pallas kernels: 8.26 us -> 7.97 us  [call(): pl.pallas_call(ordered, out_shape=out_shape, in_specs=specs, out_specs=ja...]
  transfers between devices with their start and end apart: 26 -> 26, of which waited for: 14 -> 15; matrix products, arithmetic and copies ran while one was open for 0% -> 0% of each run, Pallas kernels for 4% -> 4%
where the time goes in v5:
time: 204 us; the launch traced here: 203 us
  starting transfers between devices  89.3 us (44%)
  waiting for transfers between devices  64 us (31%)
  blocking collectives  34.1 us (17%)
  Pallas kernels  9.22 us (5%)
  local copies, waits for them, and re-layouts  5.63 us (3%)
    ppermute x26, starting transfers between devices, shifted(): lax.ppermute(array, axis, [(i, (i + by) % peers) for i in range(peers)])  89.3 us
    ppermute x26, waiting for transfers between devices, shifted(): lax.ppermute(array, axis, [(i, (i + by) % peers) for i in range(peers)])  64 us
    all_to_all x1, blocking collectives, body(): lax.all_to_all(total, 'x', split_axis=0, concat_axis=0, tiled=True)  18.1 us
    all_to_all x1, blocking collectives, body(): lax.all_to_all(prepare(states, routes, norm_gain), 'x', split_axis=0, con...  16 us
    pallas_call x18, Pallas kernels, call(): pl.pallas_call(ordered, out_shape=out_shape, in_specs=specs, out_specs=ja...  7.97 us
    unnamed x26, local copies, waits for them, and re-layouts  5.63 us
  transfers between devices with their start and end apart: 26, of which 15 were waited for; matrix products, arithmetic and copies ran while one was open for 0% of the time, Pallas kernels for 4%

profile of v5, /device:TPU:25, one launch (start us, length us, event | category | flops | bytes accessed | tf_op | source)
XLA Modules:
  0.0 203.4 jit_solution(10985710619332976796)
XLA Ops:
  0.6 10.7 %collective-permute-start.1 = (bf16[128,3584]{1,0:T(8,128)(2,1)}, bf16[128,3584]{1,0:T(8,128)(2,1)S(1)}, u32[]{:S(2)}, u32[]{:S(2)}) collective-permute-start(bf16[128,3584]{1,0:T(8,128)(2,1)} %bitcast.33), channel_id=1, source_target_pairs={{0,7},{1,0},{2,1},{3,2},{4,3},{5,4},{6,5},{7,6},{8,15},{9,8},{10,9... | collective-permute-start | bytes 2752520 | tf_op jit(solution)/shard_map/ppermute | solution.py:36
  17.9 16.0 %all_to_all.22 = bf16[4,32,3584]{2,1,0:T(8,128)(2,1)S(1)} all-to-all(bf16[4,32,3584]{2,1,0:T(8,128)(2,1)S(1)} %bitcast.42), channel_id=1, replica_groups=mesh['pipe'=16,'x'=4,'z'=8] {'x'}, dimensions={0} | all-to-all | bytes 1835008 | tf_op jit(solution)/shard_map/all_to_all | solution.py:256
  35.6 3.0 %collective-permute-start.3 = (bf16[64,3584]{1,0:T(8,128)(2,1)S(1)}, bf16[64,3584]{1,0:T(8,128)(2,1)S(1)}, u32[]{:S(2)}, u32[]{:S(2)}) collective-permute-start(bf16[64,3584]{1,0:T(8,128)(2,1)S(1)} %get-tuple-element.30.refs_0_), channel_id=1, source_target_pairs={{0,7},{1,0},{2,1},{3,2},{4,3},{5,4},{6,5},{7,6},{8,15},{9,8},{10,9... | collective-permute-start | bytes 1376264 | tf_op jit(solution)/shard_map/ppermute | solution.py:36
  43.0 4.6 %collective-permute-start.6 = (bf16[64,3584]{1,0:T(8,128)(2,1)S(1)}, bf16[64,3584]{1,0:T(8,128)(2,1)S(1)}, u32[]{:S(2)}, u32[]{:S(2)}) collective-permute-start(bf16[64,3584]{1,0:T(8,128)(2,1)S(1)} %get-tuple-element.31.refs_1_), channel_id=1, source_target_pairs={{0,7},{1,0},{2,1},{3,2},{4,3},{5,4},{6,5},{7,6},{8,15},{9,8},{10,9... | collective-permute-start | bytes 1376264 | tf_op jit(solution)/shard_map/ppermute | solution.py:36
  48.0 2.9 %collective-permute-done.2.refs_0_ = bf16[64,3584]{1,0:T(8,128)(2,1)S(1)} collective-permute-done((bf16[64,3584]{1,0:T(8,128)(2,1)S(1)}, bf16[64,3584]{1,0:T(8,128)(2,1)S(1)}, u32[]{:S(2)}, u32[]{:S(2)}) %collective-permute-start.2) | collective-permute-done | bytes 458784 | tf_op jit(solution)/shard_map/ppermute | solution.py:36
  53.2 4.6 %collective-permute-start.5 = (bf16[64,3584]{1,0:T(8,128)(2,1)S(1)}, bf16[64,3584]{1,0:T(8,128)(2,1)S(1)}, u32[]{:S(2)}, u32[]{:S(2)}) collective-permute-start(bf16[64,3584]{1,0:T(8,128)(2,1)S(1)} %get-tuple-element.34), channel_id=1, source_target_pairs={{0,7},{1,0},{2,1},{3,2},{4,3},{5,4},{6,5},{7,6},{8,15},{9,8},{10,9... | collective-permute-start | bytes 1376264 | tf_op jit(solution)/shard_map/ppermute | solution.py:36
  57.8 2.9 %collective-permute-done.7.refs_1_ = bf16[64,3584]{1,0:T(8,128)(2,1)S(1)} collective-permute-done((bf16[64,3584]{1,0:T(8,128)(2,1)S(1)}, bf16[64,3584]{1,0:T(8,128)(2,1)S(1)}, u32[]{:S(2)}, u32[]{:S(2)}) %collective-permute-start.7) | collective-permute-done | bytes 458784 | tf_op jit(solution)/shard_map/ppermute | solution.py:36
  63.1 3.4 %collective-permute-start.11 = (bf16[64,3584]{1,0:T(8,128)(2,1)S(1)}, bf16[64,3584]{1,0:T(8,128)(2,1)S(1)}, u32[]{:S(2)}, u32[]{:S(2)}) collective-permute-start(bf16[64,3584]{1,0:T(8,128)(2,1)S(1)} %get-tuple-element.40), channel_id=1, source_target_pairs={{0,1},{1,2},{2,3},{3,4},{4,5},{5,6},{6,7},{7,0},{8,9},{9,10},{10,1... | collective-permute-start | bytes 1376264 | tf_op jit(solution)/shard_map/ppermute | solution.py:36
  66.4 4.1 %collective-permute-done.4.refs_0_ = bf16[64,3584]{1,0:T(8,128)(2,1)S(1)} collective-permute-done((bf16[64,3584]{1,0:T(8,128)(2,1)S(1)}, bf16[64,3584]{1,0:T(8,128)(2,1)S(1)}, u32[]{:S(2)}, u32[]{:S(2)}) %collective-permute-start.4) | collective-permute-done | bytes 458784 | tf_op jit(solution)/shard_map/ppermute | solution.py:36
  72.9 4.6 %collective-permute-start.9 = (bf16[64,3584]{1,0:T(8,128)(2,1)S(1)}, bf16[64,3584]{1,0:T(8,128)(2,1)S(1)}, u32[]{:S(2)}, u32[]{:S(2)}) collective-permute-start(bf16[64,3584]{1,0:T(8,128)(2,1)S(1)} %get-tuple-element.38), channel_id=1, source_target_pairs={{0,7},{1,0},{2,1},{3,2},{4,3},{5,4},{6,5},{7,6},{8,15},{9,8},{10,9... | collective-permute-start | bytes 1376264 | tf_op jit(solution)/shard_map/ppermute | solution.py:36
  77.5 2.9 %collective-permute-done.11.refs_1_ = bf16[64,3584]{1,0:T(8,128)(2,1)S(1)} collective-permute-done((bf16[64,3584]{1,0:T(8,128)(2,1)S(1)}, bf16[64,3584]{1,0:T(8,128)(2,1)S(1)}, u32[]{:S(2)}, u32[]{:S(2)}) %collective-permute-start.11) | collective-permute-done | bytes 458784 | tf_op jit(solution)/shard_map/ppermute | solution.py:36
  82.7 3.4 %collective-permute-start.15 = (bf16[64,3584]{1,0:T(8,128)(2,1)S(1)}, bf16[64,3584]{1,0:T(8,128)(2,1)S(1)}, u32[]{:S(2)}, u32[]{:S(2)}) collective-permute-start(bf16[64,3584]{1,0:T(8,128)(2,1)S(1)} %get-tuple-element.47), channel_id=1, source_target_pairs={{0,1},{1,2},{2,3},{3,4},{4,5},{5,6},{6,7},{7,0},{8,9},{9,10},{10,1... | collective-permute-start | bytes 1376264 | tf_op jit(solution)/shard_map/ppermute | solution.py:36
  86.1 4.1 %collective-permute-done.8.refs_0_ = bf16[64,3584]{1,0:T(8,128)(2,1)S(1)} collective-permute-done((bf16[64,3584]{1,0:T(8,128)(2,1)S(1)}, bf16[64,3584]{1,0:T(8,128)(2,1)S(1)}, u32[]{:S(2)}, u32[]{:S(2)}) %collective-permute-start.8) | collective-permute-done | bytes 458784 | tf_op jit(solution)/shard_map/ppermute | solution.py:36
  95.2 4.8 %collective-permute-done.15.refs_1_ = bf16[64,3584]{1,0:T(8,128)(2,1)S(1)} collective-permute-done((bf16[64,3584]{1,0:T(8,128)(2,1)S(1)}, bf16[64,3584]{1,0:T(8,128)(2,1)S(1)}, u32[]{:S(2)}, u32[]{:S(2)}) %collective-permute-start.15) | collective-permute-done | bytes 458784 | tf_op jit(solution)/shard_map/ppermute | solution.py:36
  102.4 3.4 %collective-permute-start.12 = (bf16[192,128]{1,0:T(8,128)(2,1)S(1)}, bf16[192,128]{1,0:T(8,128)(2,1)S(1)}, u32[]{:S(2)}, u32[]{:S(2)}) collective-permute-start(bf16[192,128]{1,0:T(8,128)(2,1)S(1)} %pad_maximum_fusion), channel_id=1, source_target_pairs={{0,1},{1,2},{2,3},{3,4},{4,5},{5,6},{6,7},{7,0},{8,9},{9,10},{10,1... | collective-permute-start | bytes 147464 | tf_op jit(solution)/shard_map/ppermute | solution.py:36
  105.8 3.1 %collective-permute-start.17 = (bf16[192,128]{1,0:T(8,128)(2,1)S(1)}, bf16[192,128]{1,0:T(8,128)(2,1)S(1)}, u32[]{:S(2)}, u32[]{:S(2)}) collective-permute-start(bf16[192,128]{1,0:T(8,128)(2,1)S(1)} %pad_maximum_fusion.1), channel_id=1, source_target_pairs={{0,7},{1,0},{2,1},{3,2},{4,3},{5,4},{6,5},{7,6},{8,15},{9,8},{10,9... | collective-permute-start | bytes 147464 | tf_op jit(solution)/shard_map/ppermute | solution.py:36
  112.9 3.4 %collective-permute-start.19 = (bf16[128,128]{1,0:T(8,128)(2,1)S(1)}, bf16[128,128]{1,0:T(8,128)(2,1)S(1)}, u32[]{:S(2)}, u32[]{:S(2)}) collective-permute-start(bf16[128,128]{1,0:T(8,128)(2,1)S(1)} %pad_maximum_fusion.3), channel_id=1, source_target_pairs={{0,1},{1,2},{2,3},{3,4},{4,5},{5,6},{6,7},{7,0},{8,9},{9,10},{10,1... | collective-permute-start | bytes 98312 | tf_op jit(solution)/shard_map/ppermute | solution.py:36
  119.1 5.5 %collective-permute-start.22 = (bf16[64,3584]{1,0:T(8,128)(2,1)S(1)}, bf16[64,3584]{1,0:T(8,128)(2,1)S(1)}, u32[]{:S(2)}, u32[]{:S(2)}) collective-permute-start(bf16[64,3584]{1,0:T(8,128)(2,1)S(1)} %shard_map.125.refs_6_), channel_id=1, source_target_pairs={{0,6},{1,7},{2,0},{3,1},{4,2},{5,3},{6,4},{7,5},{8,14},{9,15},{10,... | collective-permute-start | bytes 1376264 | tf_op jit(solution)/shard_map/ppermute | solution.py:36
  127.7 6.4 %collective-permute-start.21 = (bf16[64,3584]{1,0:T(8,128)(2,1)S(1)}, bf16[64,3584]{1,0:T(8,128)(2,1)S(1)}, u32[]{:S(2)}, u32[]{:S(2)}) collective-permute-start(bf16[64,3584]{1,0:T(8,128)(2,1)S(1)} %shard_map.126.refs_6_), channel_id=1, source_target_pairs={{0,5},{1,6},{2,7},{3,0},{4,1},{5,2},{6,3},{7,4},{8,13},{9,14},{10,... | collective-permute-start | bytes 1376264 | tf_op jit(solution)/shard_map/ppermute | solution.py:36
  137.2 24.7 %collective-permute-done.23.refs_5_ = bf16[64,3584]{1,0:T(8,128)(2,1)S(1)} collective-permute-done((bf16[64,3584]{1,0:T(8,128)(2,1)S(1)}, bf16[64,3584]{1,0:T(8,128)(2,1)S(1)}, u32[]{:S(2)}, u32[]{:S(2)}) %collective-permute-start.23) | collective-permute-done | bytes 458784 | tf_op jit(solution)/shard_map/ppermute | solution.py:36
  163.6 18.1 %all_to_all.23 = bf16[4,32,3584]{2,1,0:T(8,128)(2,1)S(1)} all-to-all(bf16[4,32,3584]{2,1,0:T(8,128)(2,1)S(1)} %bitcast.44), channel_id=1, replica_groups=mesh['pipe'=16,'x'=4,'z'=8] {'x'}, dimensions={0} | all-to-all | bytes 1835008 | tf_op jit(solution)/shard_map/all_to_all | solution.py:314
  182.9 9.9 %collective-permute-start.24 = (bf16[64,3584]{1,0:T(8,128)(2,1)S(1)}, bf16[64,3584]{1,0:T(8,128)(2,1)S(1)}, u32[]{:S(2)}, u32[]{:S(2)}) collective-permute-start(bf16[64,3584]{1,0:T(8,128)(2,1)S(1)} %get-tuple-element.56), channel_id=1, source_target_pairs={{0,32},{32,64},{64,96},{96,128},{128,160},{160,192},{192,224},{224... | collective-permute-start | bytes 1376264 | tf_op jit(solution)/shard_map/ppermute | solution.py:36
  192.8 5.4 %collective-permute-done.24 = bf16[64,3584]{1,0:T(8,128)(2,1)S(1)} collective-permute-done((bf16[64,3584]{1,0:T(8,128)(2,1)S(1)}, bf16[64,3584]{1,0:T(8,128)(2,1)S(1)}, u32[]{:S(2)}, u32[]{:S(2)}) %collective-permute-start.24) | collective-permute-done | bytes 458784 | tf_op jit(solution)/shard_map/ppermute | solution.py:36
  198.2 3.7 %collective-permute-done.25 = bf16[64,3584]{1,0:T(8,128)(2,1)S(1)} collective-permute-done((bf16[64,3584]{1,0:T(8,128)(2,1)S(1)}, bf16[64,3584]{1,0:T(8,128)(2,1)S(1)}, u32[]{:S(2)}, u32[]{:S(2)}) %collective-permute-start.25) | collective-permute-done | bytes 458784 | tf_op jit(solution)/shard_map/ppermute | solution.py:36
  (79 shorter events, 47.0 us)
Async XLA Ops:
  0.6 33.3 %collective-permute-start.1 = (bf16[128,3584]{1,0:T(8,128)(2,1)}, bf16[128,3584]{1,0:T(8,128)(2,1)S(1)}, u32[]{:S(2)}, u32[]{:S(2)}) collective-permute-start(bf16[128,3584]{1,0:T(8,128)(2,1)} %bitcast.33), channel_id=1, source_target_pairs={{0,7},{1,0},{2,1},{3,2},{4,3},{5,4},{6,5},{7,6},{8,15},{9,8},{10,9... | collective-permute-start | bytes 2752520 | tf_op jit(solution)/shard_map/ppermute | solution.py:36
  11.3 24.2 %collective-permute-start = (bf16[128,3584]{1,0:T(8,128)(2,1)}, bf16[128,3584]{1,0:T(8,128)(2,1)S(1)}, u32[]{:S(2)}, u32[]{:S(2)}) collective-permute-start(bf16[128,3584]{1,0:T(8,128)(2,1)} %bitcast.34), channel_id=1, source_target_pairs={{0,1},{1,2},{2,3},{3,4},{4,5},{5,6},{6,7},{7,0},{8,9},{9,10},{10,1... | collective-permute-start | bytes 2752520 | tf_op jit(solution)/shard_map/ppermute | solution.py:36
  35.6 12.4 %collective-permute-start.3 = (bf16[64,3584]{1,0:T(8,128)(2,1)S(1)}, bf16[64,3584]{1,0:T(8,128)(2,1)S(1)}, u32[]{:S(2)}, u32[]{:S(2)}) collective-permute-start(bf16[64,3584]{1,0:T(8,128)(2,1)S(1)} %get-tuple-element.30.refs_0_), channel_id=1, source_target_pairs={{0,7},{1,0},{2,1},{3,2},{4,3},{5,4},{6,5},{7,6},{8,15},{9,8},{10,9... | collective-permute-start | bytes 1376264 | tf_op jit(solution)/shard_map/ppermute | solution.py:36
  38.6 12.3 %collective-permute-start.2 = (bf16[64,3584]{1,0:T(8,128)(2,1)S(1)}, bf16[64,3584]{1,0:T(8,128)(2,1)S(1)}, u32[]{:S(2)}, u32[]{:S(2)}) collective-permute-start(bf16[64,3584]{1,0:T(8,128)(2,1)S(1)} %get-tuple-element.30.refs_0_), channel_id=1, source_target_pairs={{0,1},{1,2},{2,3},{3,4},{4,5},{5,6},{6,7},{7,0},{8,9},{9,10},{10,1... | collective-permute-start | bytes 1376264 | tf_op jit(solution)/shard_map/ppermute | solution.py:36
  41.0 19.7 %collective-permute-start.7 = (bf16[64,3584]{1,0:T(8,128)(2,1)S(1)}, bf16[64,3584]{1,0:T(8,128)(2,1)S(1)}, u32[]{:S(2)}, u32[]{:S(2)}) collective-permute-start(bf16[64,3584]{1,0:T(8,128)(2,1)S(1)} %get-tuple-element.31.refs_1_), channel_id=1, source_target_pairs={{0,1},{1,2},{2,3},{3,4},{4,5},{5,6},{6,7},{7,0},{8,9},{9,10},{10,1... | collective-permute-start | bytes 1376264 | tf_op jit(solution)/shard_map/ppermute | solution.py:36
  43.0 17.8 %collective-permute-start.6 = (bf16[64,3584]{1,0:T(8,128)(2,1)S(1)}, bf16[64,3584]{1,0:T(8,128)(2,1)S(1)}, u32[]{:S(2)}, u32[]{:S(2)}) collective-permute-start(bf16[64,3584]{1,0:T(8,128)(2,1)S(1)} %get-tuple-element.31.refs_1_), channel_id=1, source_target_pairs={{0,7},{1,0},{2,1},{3,2},{4,3},{5,4},{6,5},{7,6},{8,15},{9,8},{10,9... | collective-permute-start | bytes 1376264 | tf_op jit(solution)/shard_map/ppermute | solution.py:36
  51.3 19.2 %collective-permute-start.4 = (bf16[64,3584]{1,0:T(8,128)(2,1)S(1)}, bf16[64,3584]{1,0:T(8,128)(2,1)S(1)}, u32[]{:S(2)}, u32[]{:S(2)}) collective-permute-start(bf16[64,3584]{1,0:T(8,128)(2,1)S(1)} %get-tuple-element.33), channel_id=1, source_target_pairs={{0,1},{1,2},{2,3},{3,4},{4,5},{5,6},{6,7},{7,0},{8,9},{9,10},{10,1... | collective-permute-start | bytes 1376264 | tf_op jit(solution)/shard_map/ppermute | solution.py:36
  53.2 17.3 %collective-permute-start.5 = (bf16[64,3584]{1,0:T(8,128)(2,1)S(1)}, bf16[64,3584]{1,0:T(8,128)(2,1)S(1)}, u32[]{:S(2)}, u32[]{:S(2)}) collective-permute-start(bf16[64,3584]{1,0:T(8,128)(2,1)S(1)} %get-tuple-element.34), channel_id=1, source_target_pairs={{0,7},{1,0},{2,1},{3,2},{4,3},{5,4},{6,5},{7,6},{8,15},{9,8},{10,9... | collective-permute-start | bytes 1376264 | tf_op jit(solution)/shard_map/ppermute | solution.py:36
  61.1 16.3 %collective-permute-start.10 = (bf16[64,3584]{1,0:T(8,128)(2,1)S(1)}, bf16[64,3584]{1,0:T(8,128)(2,1)S(1)}, u32[]{:S(2)}, u32[]{:S(2)}) collective-permute-start(bf16[64,3584]{1,0:T(8,128)(2,1)S(1)} %get-tuple-element.39), channel_id=1, source_target_pairs={{0,7},{1,0},{2,1},{3,2},{4,3},{5,4},{6,5},{7,6},{8,15},{9,8},{10,9... | collective-permute-start | bytes 1376264 | tf_op jit(solution)/shard_map/ppermute | solution.py:36
  63.1 17.3 %collective-permute-start.11 = (bf16[64,3584]{1,0:T(8,128)(2,1)S(1)}, bf16[64,3584]{1,0:T(8,128)(2,1)S(1)}, u32[]{:S(2)}, u32[]{:S(2)}) collective-permute-start(bf16[64,3584]{1,0:T(8,128)(2,1)S(1)} %get-tuple-element.40), channel_id=1, source_target_pairs={{0,1},{1,2},{2,3},{3,4},{4,5},{5,6},{6,7},{7,0},{8,9},{9,10},{10,1... | collective-permute-start | bytes 1376264 | tf_op jit(solution)/shard_map/ppermute | solution.py:36
  71.0 19.2 %collective-permute-start.8 = (bf16[64,3584]{1,0:T(8,128)(2,1)S(1)}, bf16[64,3584]{1,0:T(8,128)(2,1)S(1)}, u32[]{:S(2)}, u32[]{:S(2)}) collective-permute-start(bf16[64,3584]{1,0:T(8,128)(2,1)S(1)} %get-tuple-element.37), channel_id=1, source_target_pairs={{0,1},{1,2},{2,3},{3,4},{4,5},{5,6},{6,7},{7,0},{8,9},{9,10},{10,1... | collective-permute-start | bytes 1376264 | tf_op jit(solution)/shard_map/ppermute | solution.py:36
  72.9 17.3 %collective-permute-start.9 = (bf16[64,3584]{1,0:T(8,128)(2,1)S(1)}, bf16[64,3584]{1,0:T(8,128)(2,1)S(1)}, u32[]{:S(2)}, u32[]{:S(2)}) collective-permute-start(bf16[64,3584]{1,0:T(8,128)(2,1)S(1)} %get-tuple-element.38), channel_id=1, source_target_pairs={{0,7},{1,0},{2,1},{3,2},{4,3},{5,4},{6,5},{7,6},{8,15},{9,8},{10,9... | collective-permute-start | bytes 1376264 | tf_op jit(solution)/shard_map/ppermute | solution.py:36
  80.8 14.4 %collective-permute-start.14 = (bf16[64,3584]{1,0:T(8,128)(2,1)S(1)}, bf16[64,3584]{1,0:T(8,128)(2,1)S(1)}, u32[]{:S(2)}, u32[]{:S(2)}) collective-permute-start(bf16[64,3584]{1,0:T(8,128)(2,1)S(1)} %get-tuple-element.46), channel_id=1, source_target_pairs={{0,7},{1,0},{2,1},{3,2},{4,3},{5,4},{6,5},{7,6},{8,15},{9,8},{10,9... | collective-permute-start | bytes 1376264 | tf_op jit(solution)/shard_map/ppermute | solution.py:36
  82.7 17.3 %collective-permute-start.15 = (bf16[64,3584]{1,0:T(8,128)(2,1)S(1)}, bf16[64,3584]{1,0:T(8,128)(2,1)S(1)}, u32[]{:S(2)}, u32[]{:S(2)}) collective-permute-start(bf16[64,3584]{1,0:T(8,128)(2,1)S(1)} %get-tuple-element.47), channel_id=1, source_target_pairs={{0,1},{1,2},{2,3},{3,4},{4,5},{5,6},{6,7},{7,0},{8,9},{9,10},{10,1... | collective-permute-start | bytes 1376264 | tf_op jit(solution)/shard_map/ppermute | solution.py:36
  90.6 19.2 %collective-permute-start.13 = (bf16[64,3584]{1,0:T(8,128)(2,1)S(1)}, bf16[64,3584]{1,0:T(8,128)(2,1)S(1)}, u32[]{:S(2)}, u32[]{:S(2)}) collective-permute-start(bf16[64,3584]{1,0:T(8,128)(2,1)S(1)} %get-tuple-element.45), channel_id=1, source_target_pairs={{0,1},{1,2},{2,3},{3,4},{4,5},{5,6},{6,7},{7,0},{8,9},{9,10},{10,1... | collective-permute-start | bytes 1376264 | tf_op jit(solution)/shard_map/ppermute | solution.py:36
  102.4 13.9 %collective-permute-start.12 = (bf16[192,128]{1,0:T(8,128)(2,1)S(1)}, bf16[192,128]{1,0:T(8,128)(2,1)S(1)}, u32[]{:S(2)}, u32[]{:S(2)}) collective-permute-start(bf16[192,128]{1,0:T(8,128)(2,1)S(1)} %pad_maximum_fusion), channel_id=1, source_target_pairs={{0,1},{1,2},{2,3},{3,4},{4,5},{5,6},{6,7},{7,0},{8,9},{9,10},{10,1... | collective-permute-start | bytes 147464 | tf_op jit(solution)/shard_map/ppermute | solution.py:36
  105.8 12.9 %collective-permute-start.17 = (bf16[192,128]{1,0:T(8,128)(2,1)S(1)}, bf16[192,128]{1,0:T(8,128)(2,1)S(1)}, u32[]{:S(2)}, u32[]{:S(2)}) collective-permute-start(bf16[192,128]{1,0:T(8,128)(2,1)S(1)} %pad_maximum_fusion.1), channel_id=1, source_target_pairs={{0,7},{1,0},{2,1},{3,2},{4,3},{5,4},{6,5},{7,6},{8,15},{9,8},{10,9... | collective-permute-start | bytes 147464 | tf_op jit(solution)/shard_map/ppermute | solution.py:36
  110.3 14.2 %collective-permute-start.16 = (bf16[128,128]{1,0:T(8,128)(2,1)S(1)}, bf16[128,128]{1,0:T(8,128)(2,1)S(1)}, u32[]{:S(2)}, u32[]{:S(2)}) collective-permute-start(bf16[128,128]{1,0:T(8,128)(2,1)S(1)} %pad_maximum_fusion.2), channel_id=1, source_target_pairs={{0,7},{1,0},{2,1},{3,2},{4,3},{5,4},{6,5},{7,6},{8,15},{9,8},{10,9... | collective-permute-start | bytes 98312 | tf_op jit(solution)/shard_map/ppermute | solution.py:36
  112.9 12.3 %collective-permute-start.19 = (bf16[128,128]{1,0:T(8,128)(2,1)S(1)}, bf16[128,128]{1,0:T(8,128)(2,1)S(1)}, u32[]{:S(2)}, u32[]{:S(2)}) collective-permute-start(bf16[128,128]{1,0:T(8,128)(2,1)S(1)} %pad_maximum_fusion.3), channel_id=1, source_target_pairs={{0,1},{1,2},{2,3},{3,4},{4,5},{5,6},{6,7},{7,0},{8,9},{9,10},{10,1... | collective-permute-start | bytes 98312 | tf_op jit(solution)/shard_map/ppermute | solution.py:36
  116.7 20.5 %collective-permute-start.20 = (bf16[64,3584]{1,0:T(8,128)(2,1)S(1)}, bf16[64,3584]{1,0:T(8,128)(2,1)S(1)}, u32[]{:S(2)}, u32[]{:S(2)}) collective-permute-start(bf16[64,3584]{1,0:T(8,128)(2,1)S(1)} %shard_map.124.refs_4_), channel_id=1, source_target_pairs={{0,2},{1,3},{2,4},{3,5},{4,6},{5,7},{6,0},{7,1},{8,10},{9,11},{10,... | collective-permute-start | bytes 1376264 | tf_op jit(solution)/shard_map/ppermute | solution.py:36
  119.1 17.0 %collective-permute-start.22 = (bf16[64,3584]{1,0:T(8,128)(2,1)S(1)}, bf16[64,3584]{1,0:T(8,128)(2,1)S(1)}, u32[]{:S(2)}, u32[]{:S(2)}) collective-permute-start(bf16[64,3584]{1,0:T(8,128)(2,1)S(1)} %shard_map.125.refs_6_), channel_id=1, source_target_pairs={{0,6},{1,7},{2,0},{3,1},{4,2},{5,3},{6,4},{7,5},{8,14},{9,15},{10,... | collective-permute-start | bytes 1376264 | tf_op jit(solution)/shard_map/ppermute | solution.py:36
  125.8 36.1 %collective-permute-start.23 = (bf16[64,3584]{1,0:T(8,128)(2,1)S(1)}, bf16[64,3584]{1,0:T(8,128)(2,1)S(1)}, u32[]{:S(2)}, u32[]{:S(2)}) collective-permute-start(bf16[64,3584]{1,0:T(8,128)(2,1)S(1)} %shard_map.127.refs_6_), channel_id=1, source_target_pairs={{0,3},{1,4},{2,5},{3,6},{4,7},{5,0},{6,1},{7,2},{8,11},{9,12},{10,... | collective-permute-start | bytes 1376264 | tf_op jit(solution)/shard_map/ppermute | solution.py:36
  127.7 35.5 %collective-permute-start.21 = (bf16[64,3584]{1,0:T(8,128)(2,1)S(1)}, bf16[64,3584]{1,0:T(8,128)(2,1)S(1)}, u32[]{:S(2)}, u32[]{:S(2)}) collective-permute-start(bf16[64,3584]{1,0:T(8,128)(2,1)S(1)} %shard_map.126.refs_6_), channel_id=1, source_target_pairs={{0,5},{1,6},{2,7},{3,0},{4,1},{5,2},{6,3},{7,4},{8,13},{9,14},{10,... | collective-permute-start | bytes 1376264 | tf_op jit(solution)/shard_map/ppermute | solution.py:36
  182.9 15.3 %collective-permute-start.24 = (bf16[64,3584]{1,0:T(8,128)(2,1)S(1)}, bf16[64,3584]{1,0:T(8,128)(2,1)S(1)}, u32[]{:S(2)}, u32[]{:S(2)}) collective-permute-start(bf16[64,3584]{1,0:T(8,128)(2,1)S(1)} %get-tuple-element.56), channel_id=1, source_target_pairs={{0,32},{32,64},{64,96},{96,128},{128,160},{160,192},{192,224},{224... | collective-permute-start | bytes 1376264 | tf_op jit(solution)/shard_map/ppermute | solution.py:36
  (14 other events, 92.7 us)
